TPU v7x, 512 devices: a whole 4x8x8 slice. The times are simulated.
512 devices in a mesh: pipe: 8 (over x, core), rows: 64 (over y, z).
Axes of the slice: x: 4, y: 8, z: 8, core: 2. Of those that a mesh axis runs over, the one named last changes fastest.
Arguments:
- fwd_in: bfloat16 [8, 128, 512, 256], P('pipe', None, 'rows'), may hold values from -6 to 6
- bwd_in: bfloat16 [8, 128, 512, 256], P('pipe', None, 'rows'), may hold values from -6 to 6
- grad_in: bfloat16 [8, 128, 512, 256], P('pipe', None, 'rows'), may hold values from -6 to 6
- land_use: int32 [8, 2, 512, 256], P('pipe', None, 'rows'), may hold values from 0 to 7
- friction: float32 [8, 128, 8], P('pipe'), may hold values from 0.3 to 3
- weight_in: bfloat16 [8, 128, 1152], P('pipe'), may hold values from -0.1875 to 0.1875
- weight_out: bfloat16 [8, 128, 1152], P('pipe'), may hold values from -0.1875 to 0.1875
Outputs:
- handed_act: bfloat16 [8, 128, 512, 256], P('pipe', None, 'rows')
- handed_grad: bfloat16 [8, 128, 512, 256], P('pipe', None, 'rows')
- grad_w_in: float32 [8, 128, 1152], P('pipe')
- grad_w_out: float32 [8, 128, 1152], P('pipe')
Inputs may be any that keep to these rules, and one draw needn't show every extreme that they name: `land_use`: land-use classes.
All inputs are finite; a program needn't handle non-finite values.
Results may differ from a plain program's by a relative error of at most 0.0038.
Values may be sent and summed in bfloat16 or wider, within the bound.
No kernel may reach another device: no remote copies, remote signals or barrier semaphores. Data moves between devices by JAX's collectives and lax.ppermute only.
A program may use at most 64 MiB of HBM per device.

v0:
```python
import jax
import jax.numpy as jnp
from jax import lax
from jax.sharding import PartitionSpec as P


def with_halo(cells, sides, width):
    for axis, dim in sides:
        count = lax.axis_size(axis)
        ends = count - 1
        head = lax.slice_in_dim(cells, 0, width, axis=dim)
        tail = lax.slice_in_dim(cells, cells.shape[dim] - width, cells.shape[dim], axis=dim)
        cells = jnp.concatenate(
            [
                lax.ppermute(tail, axis, [(i, (i + 1) % count) for i in range(ends)]),
                cells,
                lax.ppermute(head, axis, [((i + 1) % count, i) for i in range(ends)]),
            ],
            axis=dim,
        )
    return cells


def from_behind(value, axis, steps):
    count = lax.axis_size(axis)
    leading, last = (max(0, -steps), min(count, count - steps))
    return lax.ppermute(value, axis, [(source, source + steps) for source in range(leading, last)])


def conv_rows(padded, weight, out_rows):
    chans = padded.shape[0]
    cells = padded.shape[2]
    wide = jnp.pad(padded, ((0, 0), (0, 0), (1, 1)))
    total = jnp.zeros((weight.shape[0], out_rows, cells), jnp.float32)
    for offset_row in range(3):
        band = wide[:, offset_row : offset_row + out_rows, :]
        stacked = jnp.concatenate(
            [band[:, :, offset_col : offset_col + cells] for offset_col in range(3)], axis=0
        )
        part_weight = weight[:, offset_row * 3 * chans : (offset_row + 1) * 3 * chans]
        total = total + jnp.einsum(
            "ok,krw->orw", part_weight, stacked, preferred_element_type=jnp.float32
        )
    return total


def flipped(weight):
    outs_count = weight.shape[0]
    ins_count = weight.shape[1] // 9
    shaped = weight.reshape(outs_count, 9, ins_count)[:, ::-1, :]
    return jnp.transpose(shaped, (2, 1, 0)).reshape(ins_count, 9 * outs_count)


def weight_grad(grad, padded):
    cells = grad.shape[2]
    out_rows = grad.shape[1]
    wide = jnp.pad(padded, ((0, 0), (0, 0), (1, 1)))
    pieces = []
    for offset_row in range(3):
        band = wide[:, offset_row : offset_row + out_rows, :]
        stacked = jnp.concatenate(
            [band[:, :, offset_col : offset_col + cells] for offset_col in range(3)], axis=0
        )
        pieces.append(jnp.einsum("orw,krw->ok", grad, stacked, preferred_element_type=jnp.float32))
    return jnp.concatenate(pieces, axis=1)


def friction_field(table, classes):
    levels = jnp.arange(table.shape[1], dtype=jnp.int32)
    onehot = (classes[None, :, :] == levels[:, None, None]).astype(jnp.float32)
    return jnp.einsum("ck,krw->crw", table, onehot, precision=lax.Precision.HIGHEST)


def body(fwd_in, bwd_in, grad_in, land_use, friction, weight_in, weight_out):
    forward_x = fwd_in[0]
    stored_x = bwd_in[0]
    grad_out = grad_in[0]
    classes = land_use[0]
    table = friction[0]
    first_w = weight_in[0]
    second_w = weight_out[0]
    local_rows = forward_x.shape[1]
    cells = forward_x.shape[2]
    row_count = lax.axis_size("rows")
    unscale = 1.0 / jnp.sqrt(jnp.float32(local_rows * row_count * cells))
    depth = 1
    forward_pad = with_halo(forward_x, (("rows", 1),), depth)
    stored_pad = with_halo(stored_x, (("rows", 1),), depth)
    grad_pad = with_halo(grad_out, (("rows", 1),), depth)
    fric_fwd = friction_field(table, classes[0])
    hidden = conv_rows(forward_pad, first_w, local_rows)
    active = (jax.nn.silu(hidden) * fric_fwd).astype(jnp.bfloat16)
    active_pad = with_halo(active, (("rows", 1),), 1)
    result = (forward_x.astype(jnp.float32) + conv_rows(active_pad, second_w, local_rows)).astype(
        jnp.bfloat16
    )
    fric_bwd = friction_field(table, classes[1])
    hidden_b = conv_rows(stored_pad, first_w, local_rows)
    sigma = jax.nn.sigmoid(hidden_b)
    active_b = (jax.nn.silu(hidden_b) * fric_bwd).astype(jnp.bfloat16)
    active_b_pad = with_halo(active_b, (("rows", 1),), 1)
    grad_act = conv_rows(grad_pad, flipped(second_w), local_rows)
    grad_hidden = (grad_act * fric_bwd * (sigma * (1.0 + hidden_b * (1.0 - sigma)))).astype(
        jnp.bfloat16
    )
    grad_hidden_pad = with_halo(grad_hidden, (("rows", 1),), 1)
    grad_x = (
        grad_out.astype(jnp.float32) + conv_rows(grad_hidden_pad, flipped(first_w), local_rows)
    ).astype(jnp.bfloat16)
    grad_second = weight_grad(grad_out, active_b_pad) * unscale
    grad_first = weight_grad(grad_hidden, stored_pad) * unscale
    summed_first, summed_second = lax.psum((grad_first, grad_second), "rows")
    handed_act = from_behind(result, "pipe", 1)
    handed_grad = from_behind(grad_x, "pipe", -1)
    return (handed_act[None], handed_grad[None], summed_first[None], summed_second[None])


def solution(mesh):
    in_specs = (
        P("pipe", None, "rows", None),
        P("pipe", None, "rows", None),
        P("pipe", None, "rows", None),
        P("pipe", None, "rows", None),
        P("pipe", None, None),
        P("pipe", None, None),
        P("pipe", None, None),
    )
    out_specs = (
        P("pipe", None, "rows", None),
        P("pipe", None, "rows", None),
        P("pipe", None, None),
        P("pipe", None, None),
    )
    return jax.shard_map(body, mesh=mesh, in_specs=in_specs, out_specs=out_specs, check_vma=False)
```

profile of v0, /device:TPU:6, one launch (start us, length us, event | category | flops | bytes accessed | tf_op | source)
XLA Modules:
  0.0 266.4 jit_solution(8575777732785719926)
XLA Ops:
  7.2 1.5 copy.40
  8.8 0.7 fusion.215
  9.4 4.9 %collective-permute-start.7 = (bf16[128,1,256]{0,2,1:T(8,128)(2,1)}, bf16[128,1,256]{0,2,1:T(8,128)(2,1)}, u32[]{:S(2)}, u32[]{:S(2)}) collective-permute-start(bf16[128,1,256]{0,2,1:T(8,128)(2,1)} %get-tuple-element.54), channel_id=1, source_target_pairs={{0,1},{1,2},{2,3},{3,4},{4,5},{5,6},{6,7},{7,8},{8,9},{9,10},{10,1... | collective-permute-start | bytes 196616 | tf_op jit(solution)/shard_map/ppermute | solution.py:15
  14.3 1.3 collective-permute-start.8
  16.1 0.7 fusion.216
  16.7 5.2 %collective-permute-start.5 = (bf16[128,1,256]{0,2,1:T(8,128)(2,1)}, bf16[128,1,256]{0,2,1:T(8,128)(2,1)}, u32[]{:S(2)}, u32[]{:S(2)}) collective-permute-start(bf16[128,1,256]{0,2,1:T(8,128)(2,1)} %get-tuple-element.56), channel_id=1, source_target_pairs={{0,1},{1,2},{2,3},{3,4},{4,5},{5,6},{6,7},{7,8},{8,9},{9,10},{10,1... | collective-permute-start | bytes 196616 | tf_op jit(solution)/shard_map/ppermute | solution.py:15
  21.9 1.4 collective-permute-start.6
  23.7 0.7 fusion.218
  24.4 5.2 %collective-permute-start = (bf16[128,1,256]{0,2,1:T(8,128)(2,1)}, bf16[128,1,256]{0,2,1:T(8,128)(2,1)}, u32[]{:S(2)}, u32[]{:S(2)}) collective-permute-start(bf16[128,1,256]{0,2,1:T(8,128)(2,1)} %get-tuple-element.60), channel_id=1, source_target_pairs={{0,1},{1,2},{2,3},{3,4},{4,5},{5,6},{6,7},{7,8},{8,9},{9,10},{10,1... | collective-permute-start | bytes 196616 | tf_op jit(solution)/shard_map/ppermute | solution.py:15
  29.6 1.2 copy.70
  31.0 0.9 copy.36
  32.2 1.0 convolution_bitcast_fusion.1
  33.4 1.3 collective-permute-start.1
  34.7 1.1 select_maximum_fusion.4
  35.8 0.6 fusion.209
  36.5 1.1 select_maximum_fusion.6
  37.5 0.6 fusion.210
  38.8 1.4 fusion.180
  40.2 1.4 fusion.99
  41.7 1.0 multiply_convert_fusion
  43.3 1.4 fusion.20
  44.7 1.6 fusion.149
  46.8 5.0 %collective-permute-start.12 = (bf16[128,1,256]{0,2,1:T(8,128)(2,1)S(1)}, bf16[128,1,256]{0,2,1:T(8,128)(2,1)S(1)}, u32[]{:S(2)}, u32[]{:S(2)}) collective-permute-start(bf16[128,1,256]{0,2,1:T(8,128)(2,1)S(1)} %get-tuple-element.50), channel_id=1, source_target_pairs={{0,1},{1,2},{2,3},{3,4},{4,5},{5,6},{6,7},{7,8},{8,9},{9,10},{10,1... | collective-permute-start | bytes 196616 | tf_op jit(solution)/shard_map/ppermute | solution.py:15
  51.9 1.3 collective-permute-start.13
  53.2 1.3 collective-permute-start.10
  54.5 6.6 %collective-permute-start.9 = (bf16[128,1,256]{0,2,1:T(8,128)(2,1)S(1)}, bf16[128,1,256]{0,2,1:T(8,128)(2,1)S(1)}, u32[]{:S(2)}, u32[]{:S(2)}) collective-permute-start(bf16[128,1,256]{0,2,1:T(8,128)(2,1)S(1)} %get-tuple-element.52), channel_id=1, source_target_pairs={{0,1},{1,2},{2,3},{3,4},{4,5},{5,6},{6,7},{7,8},{8,9},{9,10},{10,1... | collective-permute-start | bytes 196616 | tf_op jit(solution)/shard_map/ppermute | solution.py:15
  61.1 1.0 fusion.173
  62.1 0.6 fusion.212
  64.0 1.6 multiply_convert_fusion.1
  65.6 5.1 %collective-permute-start.2 = (bf16[128,1,256]{0,2,1:T(8,128)(2,1)S(1)}, bf16[128,1,256]{0,2,1:T(8,128)(2,1)S(1)}, u32[]{:S(2)}, u32[]{:S(2)}) collective-permute-start(bf16[128,1,256]{0,2,1:T(8,128)(2,1)S(1)} %get-tuple-element.58), channel_id=1, source_target_pairs={{0,1},{1,2},{2,3},{3,4},{4,5},{5,6},{6,7},{7,8},{8,9},{9,10},{10,1... | collective-permute-start | bytes 196616 | tf_op jit(solution)/shard_map/ppermute | solution.py:15
  70.7 1.3 convolution_bitcast_fusion.4
  72.0 1.3 convolution_bitcast_fusion.2
  73.3 0.9 fusion.175
  74.2 1.3 collective-permute-start.3
  77.7 1.5 fusion.155
  79.1 0.6 fusion.207
  79.8 1.9 collective-permute-start.11
  82.0 1.5 fusion.211
  84.9 0.9 fusion.176
  86.3 1.7 fusion.60
  88.5 0.6 fusion.152
  89.2 3.2 %collective-permute-start.4 = (bf16[128,8,256]{0,2,1:T(8,128)(2,1)S(1)}, bf16[128,8,256]{0,2,1:T(8,128)(2,1)S(1)}, u32[]{:S(2)}, u32[]{:S(2)}) collective-permute-start(bf16[128,8,256]{0,2,1:T(8,128)(2,1)S(1)} %fusion.152), channel_id=1, source_target_pairs={{0,64},{64,128},{128,192},{192,256},{256,320},{320,384},{384,448},... | collective-permute-start | bytes 1572872 | tf_op jit(solution)/shard_map/ppermute | solution.py:27
  92.4 2.2 copy.62
  94.6 5.1 %collective-permute-done.4 = bf16[128,8,256]{0,2,1:T(8,128)(2,1)S(1)} collective-permute-done((bf16[128,8,256]{0,2,1:T(8,128)(2,1)S(1)}, bf16[128,8,256]{0,2,1:T(8,128)(2,1)S(1)}, u32[]{:S(2)}, u32[]{:S(2)}) %collective-permute-start.4) | collective-permute-done | bytes 524320 | tf_op jit(solution)/shard_map/ppermute | solution.py:27
  99.7 1.2 copy.61
  100.9 155.9 %all-reduce.9.cloned.1.call-done = (f32[1,128,1152]{2,1,0:T(8,128)}, f32[1,128,1152]{2,1,0:T(8,128)}) async-done(((f32[1,128,1152]{2,1,0:T(8,128)}, f32[1,128,1152]{2,1,0:T(8,128)}), (f32[1,128,1152]{2,1,0:T(8,128)}, f32[1,128,1152]{2,1,0:T(8,128)})) %all-reduce.9.cloned.1.call-update) | async-done | bytes 1179664 | tf_op jit(solution)/shard_map/psum | solution.py:112
  256.7 2.0 copy.95
  258.7 0.8 copy.96
  (71 shorter events, 9.3 us)
Async XLA Ops:
  7.2 25.0 %copy-start = (f32[1,128,8]{1,2,0:T(8,128)S(1)}, f32[1,128,8]{1,2,0:T(8,128)}, u32[]{:S(2)}) copy-start(f32[1,128,8]{1,2,0:T(8,128)} %param.11) | copy-start | bytes 12292
  7.2 8.4 %copy-start.1 = (bf16[1,128,8,256]{3,2,1,0:T(8,128)(2,1)S(1)}, bf16[1,128,8,256]{3,2,1,0:T(8,128)(2,1)}, u32[]{:S(2)}) copy-start(bf16[1,128,8,256]{3,2,1,0:T(8,128)(2,1)} %param.9) | copy-start | bytes 1572868
  7.2 249.5 %all-reduce.9.cloned.1.call-start = ((), (), s32[]{:S(2)}) async-start(), calls=%async_computation | async-start | bytes 2359296 | tf_op jit(solution)/shard_map/psum | solution.py:112
  8.8 14.5 %copy-start.6 = (bf16[1,128,8,256]{3,2,1,0:T(8,128)(2,1)S(1)}, bf16[1,128,8,256]{3,2,1,0:T(8,128)(2,1)}, u32[]{:S(2)}) copy-start(bf16[1,128,8,256]{3,2,1,0:T(8,128)(2,1)} %param.7) | copy-start | bytes 1572868
  9.4 24.0 %collective-permute-start.7 = (bf16[128,1,256]{0,2,1:T(8,128)(2,1)}, bf16[128,1,256]{0,2,1:T(8,128)(2,1)}, u32[]{:S(2)}, u32[]{:S(2)}) collective-permute-start(bf16[128,1,256]{0,2,1:T(8,128)(2,1)} %get-tuple-element.54), channel_id=1, source_target_pairs={{0,1},{1,2},{2,3},{3,4},{4,5},{5,6},{6,7},{7,8},{8,9},{9,10},{10,1... | collective-permute-start | bytes 196616 | tf_op jit(solution)/shard_map/ppermute | solution.py:15
  14.3 20.4 %collective-permute-start.8 = (bf16[128,1,256]{0,2,1:T(8,128)(2,1)}, bf16[128,1,256]{0,2,1:T(8,128)(2,1)}, u32[]{:S(2)}, u32[]{:S(2)}) collective-permute-start(bf16[128,1,256]{0,2,1:T(8,128)(2,1)} %get-tuple-element.55), channel_id=1, source_target_pairs={{1,0},{2,1},{3,2},{4,3},{5,4},{6,5},{7,6},{8,7},{9,8},{10,9},{11,1... | collective-permute-start | bytes 196616 | tf_op jit(solution)/shard_map/ppermute | solution.py:17
  16.1 13.5 %copy-start.14 = (s32[1,2,8,256]{3,2,1,0:T(8,128)S(1)}, s32[1,2,8,256]{3,2,1,0:T(8,128)}, u32[]{:S(2)}) copy-start(s32[1,2,8,256]{3,2,1,0:T(8,128)} %param.10) | copy-start | bytes 49156
  16.7 19.7 %collective-permute-start.5 = (bf16[128,1,256]{0,2,1:T(8,128)(2,1)}, bf16[128,1,256]{0,2,1:T(8,128)(2,1)}, u32[]{:S(2)}, u32[]{:S(2)}) collective-permute-start(bf16[128,1,256]{0,2,1:T(8,128)(2,1)} %get-tuple-element.56), channel_id=1, source_target_pairs={{0,1},{1,2},{2,3},{3,4},{4,5},{5,6},{6,7},{7,8},{8,9},{9,10},{10,1... | collective-permute-start | bytes 196616 | tf_op jit(solution)/shard_map/ppermute | solution.py:15
  21.9 8.9 %copy-start.9 = (bf16[1,128,1152]{2,1,0:T(8,128)(2,1)S(1)}, bf16[1,128,1152]{2,1,0:T(8,128)(2,1)}, u32[]{:S(2)}) copy-start(bf16[1,128,1152]{2,1,0:T(8,128)(2,1)} %param.13) | copy-start | bytes 884740
  21.9 14.6 %collective-permute-start.6 = (bf16[128,1,256]{0,2,1:T(8,128)(2,1)}, bf16[128,1,256]{0,2,1:T(8,128)(2,1)}, u32[]{:S(2)}, u32[]{:S(2)}) collective-permute-start(bf16[128,1,256]{0,2,1:T(8,128)(2,1)} %get-tuple-element.57), channel_id=1, source_target_pairs={{1,0},{2,1},{3,2},{4,3},{5,4},{6,5},{7,6},{8,7},{9,8},{10,9},{11,1... | collective-permute-start | bytes 196616 | tf_op jit(solution)/shard_map/ppermute | solution.py:17
  24.4 30.1 %collective-permute-start = (bf16[128,1,256]{0,2,1:T(8,128)(2,1)}, bf16[128,1,256]{0,2,1:T(8,128)(2,1)}, u32[]{:S(2)}, u32[]{:S(2)}) collective-permute-start(bf16[128,1,256]{0,2,1:T(8,128)(2,1)} %get-tuple-element.60), channel_id=1, source_target_pairs={{0,1},{1,2},{2,3},{3,4},{4,5},{5,6},{6,7},{7,8},{8,9},{9,10},{10,1... | collective-permute-start | bytes 196616 | tf_op jit(solution)/shard_map/ppermute | solution.py:15
  30.8 1.2 copy-start.8
  33.4 27.7 %collective-permute-start.1 = (bf16[128,1,256]{0,2,1:T(8,128)(2,1)}, bf16[128,1,256]{0,2,1:T(8,128)(2,1)S(1)}, u32[]{:S(2)}, u32[]{:S(2)}) collective-permute-start(bf16[128,1,256]{0,2,1:T(8,128)(2,1)} %get-tuple-element.61), channel_id=1, source_target_pairs={{1,0},{2,1},{3,2},{4,3},{5,4},{6,5},{7,6},{8,7},{9,8},{10,9},{11,1... | collective-permute-start | bytes 196616 | tf_op jit(solution)/shard_map/ppermute | solution.py:17
  41.6 1.0 copy-start.11
  46.8 30.0 %collective-permute-start.12 = (bf16[128,1,256]{0,2,1:T(8,128)(2,1)S(1)}, bf16[128,1,256]{0,2,1:T(8,128)(2,1)S(1)}, u32[]{:S(2)}, u32[]{:S(2)}) collective-permute-start(bf16[128,1,256]{0,2,1:T(8,128)(2,1)S(1)} %get-tuple-element.50), channel_id=1, source_target_pairs={{0,1},{1,2},{2,3},{3,4},{4,5},{5,6},{6,7},{7,8},{8,9},{9,10},{10,1... | collective-permute-start | bytes 196616 | tf_op jit(solution)/shard_map/ppermute | solution.py:15
  51.9 25.0 %collective-permute-start.13 = (bf16[128,1,256]{0,2,1:T(8,128)(2,1)S(1)}, bf16[128,1,256]{0,2,1:T(8,128)(2,1)S(1)}, u32[]{:S(2)}, u32[]{:S(2)}) collective-permute-start(bf16[128,1,256]{0,2,1:T(8,128)(2,1)S(1)} %get-tuple-element.51), channel_id=1, source_target_pairs={{1,0},{2,1},{3,2},{4,3},{5,4},{6,5},{7,6},{8,7},{9,8},{10,9},{11,1... | collective-permute-start | bytes 196616 | tf_op jit(solution)/shard_map/ppermute | solution.py:17
  53.2 21.0 %collective-permute-start.10 = (bf16[128,1,256]{0,2,1:T(8,128)(2,1)S(1)}, bf16[128,1,256]{0,2,1:T(8,128)(2,1)S(1)}, u32[]{:S(2)}, u32[]{:S(2)}) collective-permute-start(bf16[128,1,256]{0,2,1:T(8,128)(2,1)S(1)} %get-tuple-element.53), channel_id=1, source_target_pairs={{1,0},{2,1},{3,2},{4,3},{5,4},{6,5},{7,6},{8,7},{9,8},{10,9},{11,1... | collective-permute-start | bytes 196616 | tf_op jit(solution)/shard_map/ppermute | solution.py:17
  54.5 21.0 %collective-permute-start.9 = (bf16[128,1,256]{0,2,1:T(8,128)(2,1)S(1)}, bf16[128,1,256]{0,2,1:T(8,128)(2,1)S(1)}, u32[]{:S(2)}, u32[]{:S(2)}) collective-permute-start(bf16[128,1,256]{0,2,1:T(8,128)(2,1)S(1)} %get-tuple-element.52), channel_id=1, source_target_pairs={{0,1},{1,2},{2,3},{3,4},{4,5},{5,6},{6,7},{7,8},{8,9},{9,10},{10,1... | collective-permute-start | bytes 196616 | tf_op jit(solution)/shard_map/ppermute | solution.py:15
  65.5 16.2 %copy-start.2 = (bf16[128,8,256]{0,2,1:T(8,128)(2,1)}, bf16[128,8,256]{0,2,1:T(8,128)(2,1)S(1)}, u32[]{:S(2)}) copy-start(bf16[128,8,256]{0,2,1:T(8,128)(2,1)S(1)} %multiply_convert_fusion.1) | copy-start | bytes 1572868
  65.6 16.1 %collective-permute-start.2 = (bf16[128,1,256]{0,2,1:T(8,128)(2,1)S(1)}, bf16[128,1,256]{0,2,1:T(8,128)(2,1)S(1)}, u32[]{:S(2)}, u32[]{:S(2)}) collective-permute-start(bf16[128,1,256]{0,2,1:T(8,128)(2,1)S(1)} %get-tuple-element.58), channel_id=1, source_target_pairs={{0,1},{1,2},{2,3},{3,4},{4,5},{5,6},{6,7},{7,8},{8,9},{9,10},{10,1... | collective-permute-start | bytes 196616 | tf_op jit(solution)/shard_map/ppermute | solution.py:15
  74.2 7.5 %collective-permute-start.3 = (bf16[128,1,256]{0,2,1:T(8,128)(2,1)S(1)}, bf16[128,1,256]{0,2,1:T(8,128)(2,1)S(1)}, u32[]{:S(2)}, u32[]{:S(2)}) collective-permute-start(bf16[128,1,256]{0,2,1:T(8,128)(2,1)S(1)} %get-tuple-element.59), channel_id=1, source_target_pairs={{1,0},{2,1},{3,2},{4,3},{5,4},{6,5},{7,6},{8,7},{9,8},{10,9},{11,1... | collective-permute-start | bytes 196616 | tf_op jit(solution)/shard_map/ppermute | solution.py:17
  79.8 12.6 %collective-permute-start.11 = (bf16[128,8,256]{0,2,1:T(8,128)(2,1)}, bf16[128,8,256]{0,2,1:T(8,128)(2,1)}, u32[]{:S(2)}, u32[]{:S(2)}) collective-permute-start(bf16[128,8,256]{0,2,1:T(8,128)(2,1)} %fusion.155), channel_id=1, source_target_pairs={{64,0},{128,64},{192,128},{256,192},{320,256},{384,320},{448,384},... | collective-permute-start | bytes 1572872 | tf_op jit(solution)/shard_map/ppermute | solution.py:27
  81.7 1.7 copy-start.12
  82.0 1.5 copy-start.7
  84.9 1.2 copy-start.3
  84.9 1.3 copy-start.10
  86.2 1.7 copy-start.5
  86.3 1.7 copy-start.13
  89.2 10.5 %collective-permute-start.4 = (bf16[128,8,256]{0,2,1:T(8,128)(2,1)S(1)}, bf16[128,8,256]{0,2,1:T(8,128)(2,1)S(1)}, u32[]{:S(2)}, u32[]{:S(2)}) collective-permute-start(bf16[128,8,256]{0,2,1:T(8,128)(2,1)S(1)} %fusion.152), channel_id=1, source_target_pairs={{0,64},{64,128},{128,192},{192,256},{256,320},{320,384},{384,448},... | collective-permute-start | bytes 1572872 | tf_op jit(solution)/shard_map/ppermute | solution.py:27
  256.7 2.0 copy-start.4
Sparse Core Ops, SparseCore 0:
  86.0 170.7 all-reduce.8
where the time goes:
time: 268 us; the launch traced here: 266 us
  waiting for transfers between devices  161 us (60%)
  starting transfers between devices  44.9 us (17%)
  matrix products  21.9 us (8%)
  local copies, waits for them, and re-layouts  18.5 us (7%)
  between operations  14.6 us (5%)
  other arithmetic  5.45 us (2%)
    psum x1, waiting for transfers between devices, body(): summed_first, summed_second = lax.psum((grad_first, grad_second), 'rows')  156 us
    ppermute x6, starting transfers between devices, with_halo(): lax.ppermute(tail, axis, [(i, (i + 1) % count) for i in range(ends)])  31.9 us
    dot_general x15, matrix products, conv_rows(): jnp.einsum('ok,krw->orw', part_weight, stacked, preferred_element_type=jn...  15.3 us
    unnamed x39, local copies, waits for them, and re-layouts  9.56 us
    ppermute x6, starting transfers between devices, with_halo(): lax.ppermute(head, axis, [((i + 1) % count, i) for i in range(ends)])  7.85 us
  transfers between devices with their start and end apart: 15, of which 2 were waited for; matrix products, arithmetic and copies ran while one was open for 15% of the time, Pallas kernels for 0%

commit v1 on v0

v1 whole, which is shorter than its diff:
```python
import jax
import jax.numpy as jnp
from jax import lax
from jax.experimental import pallas as pl
from jax.experimental.pallas import tpu as pltpu
from jax.sharding import PartitionSpec as P

CH = 128
COLS = 256
LOCAL = 8
CLASSES = 8
TAPS = 9
WIDE = 3 * CH
HALO_ROWS = 6 * CH + 16
BF16 = jnp.bfloat16
F32 = jnp.float32
PARAMS = pltpu.CompilerParams(vmem_limit_bytes=56 * 1024 * 1024)


def pack_kernel(fwd_ref, bwd_ref, grad_ref, use_ref, head_ref, tail_ref):
    sub = lax.broadcasted_iota(jnp.int32, (16, COLS), 0)
    for i, ref in enumerate((fwd_ref, bwd_ref, grad_ref)):
        rows = jnp.swapaxes(ref[...], 0, 1)
        for k in range(2):
            head_ref[(2 * i + k) * CH : (2 * i + k + 1) * CH] = rows[k]
            tail_ref[(2 * i + k) * CH : (2 * i + k + 1) * CH] = rows[LOCAL - 2 + k]
    for ref, row in ((head_ref, 0), (tail_ref, LOCAL - 1)):
        first = use_ref[0, row : row + 1, :].astype(F32) + 1.0
        second = use_ref[1, row : row + 1, :].astype(F32) + 1.0
        both = jnp.where(sub == 0, first, jnp.where(sub == 1, second, 0.0))
        ref[6 * CH :] = both.astype(BF16)


def put_shifted(wide_ref, at, row):
    lane = lax.broadcasted_iota(jnp.int32, (CH, COLS), 1)
    zero = jnp.zeros((CH, COLS), BF16)
    wide_ref[at, 0:CH] = jnp.where(lane == 0, zero, pltpu.roll(row, 1, 1))
    wide_ref[at, CH : 2 * CH] = row
    wide_ref[at, 2 * CH :] = jnp.where(lane == COLS - 1, zero, pltpu.roll(row, COLS - 1, 1))


def three_rows(ref, at):
    return ref[pl.ds(at, 3)].reshape(-1, COLS)


def dot(a, b):
    return jnp.dot(a, b, preferred_element_type=F32)


def dot_cells(a, b):
    return lax.dot_general(a, b, (((1,), (1,)), ((), ())), preferred_element_type=F32)


def block_kernel(
    fwd_ref, bwd_ref, grad_ref, use_ref, above_ref, below_ref, table_ref, first_ref, second_ref,
    out_ref, gx_ref, gw_ref,
    rows_ref, wide_ref, wide_act_ref, wide_gh_ref, actb_ref, gh_ref, class_ref, flip1_ref, flip2_ref, res_ref,
):
    for t in range(TAPS):
        mirrored = (TAPS - 1 - t) * CH
        flip1_ref[:, mirrored : mirrored + CH] = first_ref[:, t * CH : (t + 1) * CH].T
        flip2_ref[:, mirrored : mirrored + CH] = second_ref[:, t * CH : (t + 1) * CH].T
    for i in range(2):
        class_ref[i, 0:1] = above_ref[6 * CH : 6 * CH + 16].astype(F32)[i : i + 1]
        class_ref[i, 9:10] = below_ref[6 * CH : 6 * CH + 16].astype(F32)[i : i + 1]
        class_ref[i, 1:9] = use_ref[i].astype(F32) + 1.0
    table = table_ref[...]
    high = table.astype(BF16).astype(F32)
    middle = (table - high).astype(BF16).astype(F32)
    low = table - high - middle
    terms = jnp.concatenate([high, middle, low], axis=1).astype(BF16)
    level = (lax.broadcasted_iota(jnp.int32, (3 * CLASSES, COLS), 0) % CLASSES + 1).astype(F32)

    def friction(i, r):
        onehot = jnp.where(class_ref[i, pl.ds(r, 1)] == level, 1.0, 0.0).astype(BF16)
        return dot(terms, onehot)

    for i, ref in enumerate((fwd_ref, bwd_ref, grad_ref)):
        rows_ref[i, 2:10] = jnp.swapaxes(ref[...], 0, 1)
        for k in range(2):
            rows_ref[i, k] = above_ref[(2 * i + k) * CH : (2 * i + k + 1) * CH]
            rows_ref[i, 10 + k] = below_ref[(2 * i + k) * CH : (2 * i + k + 1) * CH]

    def widen(r, carry):
        for i in range(3):
            put_shifted(wide_ref.at[i], r, rows_ref[i, r])
        return carry

    lax.fori_loop(0, 12, widen, 0, unroll=2)

    def hidden_rows(step, carry):
        for k in range(2):
            r = 2 * step + k
            h = dot(first_ref[...], three_rows(wide_ref.at[0], r))
            half = 0.5 * h
            act = (half + half * jnp.tanh(half)) * friction(0, r)
            put_shifted(wide_act_ref, r, act.astype(BF16))
            hb = dot(first_ref[...], three_rows(wide_ref.at[1], r))
            sig = 0.5 + 0.5 * jnp.tanh(0.5 * hb)
            fric = friction(1, r)
            actb_ref[r + 1] = (hb * sig * fric).astype(BF16)
            ga = dot(flip2_ref[...], three_rows(wide_ref.at[2], r))
            gh = (ga * fric * (sig * (1.0 + hb * (1.0 - sig)))).astype(BF16)
            gh_ref[r + 1] = gh
            put_shifted(wide_gh_ref, r, gh)
        return carry

    lax.fori_loop(0, 5, hidden_rows, 0)
    for ref in (actb_ref, gh_ref):
        for r in (0, 1, 10, 11):
            ref[r] = jnp.zeros((CH, COLS), BF16)

    def result_rows(step, carry):
        for k in range(4):
            r = 4 * step + k
            add = dot(second_ref[...], three_rows(wide_act_ref, r))
            res_ref[0, r] = (rows_ref[0, r + 2].astype(F32) + add).astype(BF16)
            add = dot(flip1_ref[...], three_rows(wide_gh_ref, r))
            res_ref[1, r] = (rows_ref[2, r + 2].astype(F32) + add).astype(BF16)
        return carry

    lax.fori_loop(0, 2, result_rows, 0)
    out_ref[...] = jnp.swapaxes(res_ref[0], 0, 1)
    gx_ref[...] = jnp.swapaxes(res_ref[1], 0, 1)

    total = None
    for r in range(10):
        part = dot_cells(three_rows(gh_ref, r), wide_ref[1, r + 1])
        total = part if total is None else total + part
    for a in range(3):
        for b in range(3):
            gw_ref[(a * 3 + b) * CH : (a * 3 + b + 1) * CH] = total[a * CH : (a + 1) * CH, b * CH : (b + 1) * CH].astype(BF16)
    total = None
    for r in range(10):
        part = dot_cells(wide_ref[2, r + 1], three_rows(actb_ref, r))
        total = part if total is None else total + part
    for a in range(3):
        for b in range(3):
            at = (TAPS + a * 3 + b) * CH
            gw_ref[at : at + CH] = total[a * CH : (a + 1) * CH, b * CH : (b + 1) * CH].astype(BF16)
    spare = gw_ref.shape[0] - 2 * TAPS * CH
    if spare:
        gw_ref[2 * TAPS * CH :] = jnp.zeros((spare, CH), BF16)


def sum_kernel(scale, parts_ref, out_ref):
    total = jnp.sum(parts_ref[...].astype(F32), axis=0) * scale
    out_ref[...] = jnp.broadcast_to(total.astype(BF16)[None], out_ref.shape)


def spread_kernel(flat_ref, first_ref, second_ref):
    for a in range(3):
        for b in range(3):
            at = (a * 3 + b) * CH
            to = ((2 - a) * 3 + b) * CH
            first_ref[:, to : to + CH] = flat_ref[at : at + CH].astype(F32)
            at = (TAPS + a * 3 + b) * CH
            to = (b * 3 + 2 - a) * CH
            second_ref[:, to : to + CH] = flat_ref[at : at + CH].astype(F32)


def body(fwd_in, bwd_in, grad_in, land_use, friction, weight_in, weight_out):
    shape = jax.ShapeDtypeStruct
    row_count = lax.axis_size("rows")
    sections = lax.axis_size("pipe")
    fwd, bwd, grad = fwd_in[0], bwd_in[0], grad_in[0]
    use, table, first, second = land_use[0], friction[0], weight_in[0], weight_out[0]
    share = -(-2 * TAPS * CH // (8 * row_count)) * 8
    scale = 1.0 / (LOCAL * row_count * COLS) ** 0.5

    head, tail = pl.pallas_call(
        pack_kernel, out_shape=(shape((HALO_ROWS, COLS), BF16),) * 2, compiler_params=PARAMS, name="pack_edges"
    )(fwd, bwd, grad, use)
    above = lax.ppermute(tail, "rows", [(i, i + 1) for i in range(row_count - 1)])
    below = lax.ppermute(head, "rows", [(i + 1, i) for i in range(row_count - 1)])
    result, grad_x, partial = pl.pallas_call(
        block_kernel,
        out_shape=(
            shape((CH, LOCAL, COLS), BF16),
            shape((CH, LOCAL, COLS), BF16),
            shape((row_count * share, CH), BF16),
        ),
        scratch_shapes=[
            pltpu.VMEM((3, 12, CH, COLS), BF16),
            pltpu.VMEM((3, 12, WIDE, COLS), BF16),
            pltpu.VMEM((10, WIDE, COLS), BF16),
            pltpu.VMEM((10, WIDE, COLS), BF16),
            pltpu.VMEM((12, CH, COLS), BF16),
            pltpu.VMEM((12, CH, COLS), BF16),
            pltpu.VMEM((2, 16, COLS), F32),
            pltpu.VMEM((CH, TAPS * CH), BF16),
            pltpu.VMEM((CH, TAPS * CH), BF16),
            pltpu.VMEM((2, LOCAL, CH, COLS), BF16),
        ],
        compiler_params=PARAMS,
        name="block",
    )(fwd, bwd, grad, use, above, below, table, first, second)
    handed_act = lax.ppermute(result, "pipe", [(i, i + 1) for i in range(sections - 1)])
    handed_grad = lax.ppermute(grad_x, "pipe", [(i + 1, i) for i in range(sections - 1)])
    shares = lax.all_to_all(partial.reshape(row_count, share, CH), "rows", 0, 0)
    summed = pl.pallas_call(
        lambda *refs: sum_kernel(scale, *refs),
        out_shape=shape((row_count, share, CH), BF16), compiler_params=PARAMS, name="sum_shares",
    )(shares)
    gathered = lax.all_to_all(summed, "rows", 0, 0).reshape(row_count * share, CH)
    grad_first, grad_second = pl.pallas_call(
        spread_kernel, out_shape=(shape((CH, TAPS * CH), F32),) * 2, compiler_params=PARAMS, name="spread"
    )(gathered)
    return (handed_act[None], handed_grad[None], grad_first[None], grad_second[None])


def solution(mesh):
    cells = P("pipe", None, "rows", None)
    own = P("pipe", None, None)
    return jax.shard_map(
        body,
        mesh=mesh,
        in_specs=(cells, cells, cells, cells, own, own, own),
        out_specs=(cells, cells, own, own),
        check_vma=False,
    )
```

time: 268 us -> 106 us (0.40)
  waiting for transfers between devices: 161 us -> 26.4 us
  blocking collectives: 0 us -> 36.8 us
  starting transfers between devices: 44.9 us -> 17.2 us
  matrix products: 21.9 us -> 0 us
  Pallas kernels: 0 us -> 20.2 us
  local copies, waits for them, and re-layouts: 18.5 us -> 3.91 us
  between operations: 14.6 us -> 0.71 us
  other arithmetic: 5.45 us -> 0 us
    psum x1 -> x0, waiting for transfers between devices: 156 us -> none  [body(): summed_first, summed_second = lax.psum((grad_first, grad_second), 'rows')]
    all_to_all x0 -> x1, blocking collectives: none -> 36.8 us  [body(): shares = lax.all_to_all(partial.reshape(row_count, share, CH), 'rows', 0, 0)]
    ppermute x14 -> x4, starting transfers between devices: 44.9 us -> 11.1 us  [the longest x1 4.29 us: body(): lax.ppermute(tail, 'rows', [(i, i + 1) for i in range(row_count - 1)])]
    dot_general x23 -> x0, matrix products: 21.9 us -> none  [the longest x15 15.3 us: conv_rows(): jnp.einsum('ok,krw->orw', part_weight, stacked, preferred_element_type=jn...]
    pallas_call x0 -> x4, Pallas kernels: none -> 20.2 us  [the longest x1 13.4 us: body(): pl.pallas_call(block_kernel, out_shape=(shape((CH, LOCAL, COLS), BF16), s...]
    ppermute x14 -> x4, waiting for transfers between devices: 5.12 us -> 18.1 us  [the longest x1 6.79 us: body(): lax.ppermute(tail, 'rows', [(i, i + 1) for i in range(row_count - 1)])]
    all_to_all x0 -> x1, waiting for transfers between devices: none -> 8.25 us  [body(): lax.all_to_all(summed, 'rows', 0, 0).reshape(row_count * share, CH)]
    slice x12 -> x0, local copies, waits for them, and re-layouts: 6.61 us -> none  [the longest x5 3.96 us: conv_rows(): band[:, :, offset_col:offset_col + cells]]
  transfers between devices with their start and end apart: 15 -> 5, of which waited for: 2 -> 5; matrix products, arithmetic and copies ran while one was open for 15% -> 1% of each run, Pallas kernels for 0% -> 0%
where the time goes in v1:
time: 106 us; the launch traced here: 105 us
  blocking collectives  36.8 us (35%)
  waiting for transfers between devices  26.4 us (25%)
  Pallas kernels  20.2 us (19%)
  starting transfers between devices  17.2 us (16%)
  local copies, waits for them, and re-layouts  3.91 us (4%)
    all_to_all x1, blocking collectives, body(): shares = lax.all_to_all(partial.reshape(row_count, share, CH), 'rows', 0, 0)  36.8 us
    pallas_call x1, Pallas kernels, body(): pl.pallas_call(block_kernel, out_shape=(shape((CH, LOCAL, COLS), BF16), s...  13.4 us
    all_to_all x1, waiting for transfers between devices, body(): lax.all_to_all(summed, 'rows', 0, 0).reshape(row_count * share, CH)  8.25 us
    ppermute x1, waiting for transfers between devices, body(): lax.ppermute(tail, 'rows', [(i, i + 1) for i in range(row_count - 1)])  6.79 us
    all_to_all x1, starting transfers between devices, body(): lax.all_to_all(summed, 'rows', 0, 0).reshape(row_count * share, CH)  6.02 us
    ppermute x1, waiting for transfers between devices, body(): lax.ppermute(result, 'pipe', [(i, i + 1) for i in range(sections - 1)])  4.91 us
    ppermute x1, waiting for transfers between devices, body(): lax.ppermute(head, 'rows', [(i + 1, i) for i in range(row_count - 1)])  4.65 us
    ppermute x1, starting transfers between devices, body(): lax.ppermute(tail, 'rows', [(i, i + 1) for i in range(row_count - 1)])  4.29 us
  transfers between devices with their start and end apart: 5, of which 5 were waited for; matrix products, arithmetic and copies ran while one was open for 1% of the time, Pallas kernels for 0%

profile of v1, /device:TPU:6, one launch (start us, length us, event | category | flops | bytes accessed | tf_op | source)
XLA Modules:
  0.0 105.2 jit_solution(17656463634578962431)
XLA Ops:
  0.6 0.0 copy-start.3
  0.6 2.5 %pack_edges.1 = (bf16[784,256]{1,0:T(8,128)(2,1)}, bf16[784,256]{1,0:T(8,128)(2,1)}) custom-call(bf16[128,8,256]{2,1,0:T(8,128)(2,1)} %bitcast.14, bf16[128,8,256]{2,1,0:T(8,128)(2,1)} %bitcast.16, bf16[128,8,256]{2,1,0:T(8,128)(2,1)} %bitcast.18, s32[2,8,256]{2,1,0:T(8,128)} %bitcast.26), custom_call_target="tpu_custom_call" | custom-call | tf_op jit(solution)/shard_map/pack_edges/pallas_call | solution.py:171
  3.2 4.3 %collective-permute-start = (bf16[784,256]{1,0:T(8,128)(2,1)}, bf16[784,256]{1,0:T(8,128)(2,1)S(1)}, u32[]{:S(2)}, u32[]{:S(2)}) collective-permute-start(bf16[784,256]{1,0:T(8,128)(2,1)} %get-tuple-element.11), channel_id=1, source_target_pairs={{0,1},{1,2},{2,3},{3,4},{4,5},{5,6},{6,7},{7,8},{8,9},{9,10},{10,1... | collective-permute-start | bytes 1204232 | tf_op jit(solution)/shard_map/ppermute | solution.py:174
  7.5 1.3 %collective-permute-start.1 = (bf16[784,256]{1,0:T(8,128)(2,1)}, bf16[784,256]{1,0:T(8,128)(2,1)S(1)}, u32[]{:S(2)}, u32[]{:S(2)}) collective-permute-start(bf16[784,256]{1,0:T(8,128)(2,1)} %get-tuple-element.12), channel_id=1, source_target_pairs={{1,0},{2,1},{3,2},{4,3},{5,4},{6,5},{7,6},{8,7},{9,8},{10,9},{11,1... | collective-permute-start | bytes 1204232 | tf_op jit(solution)/shard_map/ppermute | solution.py:175
  8.8 0.0 copy-done.3
  8.8 0.7 copy.11
  9.5 6.8 %collective-permute-done.above_ref = bf16[784,256]{1,0:T(8,128)(2,1)S(1)} collective-permute-done((bf16[784,256]{1,0:T(8,128)(2,1)}, bf16[784,256]{1,0:T(8,128)(2,1)S(1)}, u32[]{:S(2)}, u32[]{:S(2)}) %collective-permute-start) | collective-permute-done | bytes 401440 | tf_op jit(solution)/shard_map/ppermute | solution.py:174
  16.3 0.0 copy-start.1
  16.3 4.6 %collective-permute-done.1.below_ref = bf16[784,256]{1,0:T(8,128)(2,1)S(1)} collective-permute-done((bf16[784,256]{1,0:T(8,128)(2,1)}, bf16[784,256]{1,0:T(8,128)(2,1)S(1)}, u32[]{:S(2)}, u32[]{:S(2)}) %collective-permute-start.1) | collective-permute-done | bytes 401440 | tf_op jit(solution)/shard_map/ppermute | solution.py:175
  21.0 0.0 copy-start.2
  21.0 0.0 copy-done.1
  21.0 0.7 copy-done.2
  21.7 13.4 %block.1 = (bf16[128,8,256]{2,1,0:T(8,128)(2,1)}, bf16[128,8,256]{2,1,0:T(8,128)(2,1)}, bf16[2560,128]{1,0:T(8,128)(2,1)}) custom-call(bf16[128,8,256]{2,1,0:T(8,128)(2,1)} %bitcast.15, bf16[128,8,256]{2,1,0:T(8,128)(2,1)} %bitcast.17, bf16[128,8,256]{2,1,0:T(8,128)(2,1)} %bitcast.19, s32[2,8,256]{2,1,0:T(8,128)} %bitcast.27, bf16[784,256]{1,0:T(8,128)(2,1)} %copy-done.1, ...), custom_call_target="tpu_custom_call" | custom-call | tf_op jit(solution)/shard_map/block/pallas_call | solution.py:176
  35.1 36.8 %all_to_all.10.refs_0_ = bf16[64,40,128]{2,1,0:T(8,128)(2,1)} all-to-all(bf16[64,40,128]{2,1,0:T(8,128)(2,1)} %bitcast.20), channel_id=1, replica_groups=mesh['pipe'=8,'rows'=64] {'rows'}, dimensions={0} | all-to-all | bytes 1310720 | tf_op jit(solution)/shard_map/all_to_all | solution.py:200
  71.9 2.1 %sum_shares.1 = bf16[64,40,128]{2,1,0:T(8,128)(2,1)} custom-call(bf16[64,40,128]{2,1,0:T(8,128)(2,1)} %all_to_all.10.refs_0_), custom_call_target="tpu_custom_call" | custom-call | tf_op jit(solution)/shard_map/sum_shares/pallas_call | solution.py:201
  74.0 0.0 copy-start.5
  74.0 0.0 copy-start.4
  74.0 6.0 %all-to-all-start.1 = ((bf16[64,40,128]{2,1,0:T(8,128)(2,1)}), bf16[64,40,128]{2,1,0:T(8,128)(2,1)S(1)}, u32[]{:S(2)}, u32[]{:S(2)}) async-start(bf16[64,40,128]{2,1,0:T(8,128)(2,1)} %sum_shares.1), calls=%async_computation.1 | async-start | bytes 1310720 | tf_op jit(solution)/shard_map/all_to_all | solution.py:205
  80.0 0.0 copy-done.5
  80.0 1.9 %collective-permute-start.2 = (bf16[128,8,256]{2,1,0:T(8,128)(2,1)S(1)}, bf16[128,8,256]{2,1,0:T(8,128)(2,1)S(1)}, u32[]{:S(2)}, u32[]{:S(2)}) collective-permute-start(bf16[128,8,256]{2,1,0:T(8,128)(2,1)S(1)} %copy-done.5), channel_id=1, source_target_pairs={{0,64},{64,128},{128,192},{192,256},{256,320},{320,384},{384,448},... | collective-permute-start | bytes 1572872 | tf_op jit(solution)/shard_map/ppermute | solution.py:198
  82.0 0.0 copy-done.4
  82.0 3.6 %collective-permute-start.3 = (bf16[128,8,256]{2,1,0:T(8,128)(2,1)S(1)}, bf16[128,8,256]{2,1,0:T(8,128)(2,1)S(1)}, u32[]{:S(2)}, u32[]{:S(2)}) collective-permute-start(bf16[128,8,256]{2,1,0:T(8,128)(2,1)S(1)} %copy-done.4), channel_id=1, source_target_pairs={{64,0},{128,64},{192,128},{256,192},{320,256},{384,320},{448,384},... | collective-permute-start | bytes 1572872 | tf_op jit(solution)/shard_map/ppermute | solution.py:199
  85.6 4.9 %collective-permute-done.2 = bf16[128,8,256]{2,1,0:T(8,128)(2,1)S(1)} collective-permute-done((bf16[128,8,256]{2,1,0:T(8,128)(2,1)S(1)}, bf16[128,8,256]{2,1,0:T(8,128)(2,1)S(1)}, u32[]{:S(2)}, u32[]{:S(2)}) %collective-permute-start.2) | collective-permute-done | bytes 524320 | tf_op jit(solution)/shard_map/ppermute | solution.py:198
  90.5 1.8 %collective-permute-done.3 = bf16[128,8,256]{2,1,0:T(8,128)(2,1)S(1)} collective-permute-done((bf16[128,8,256]{2,1,0:T(8,128)(2,1)S(1)}, bf16[128,8,256]{2,1,0:T(8,128)(2,1)S(1)}, u32[]{:S(2)}, u32[]{:S(2)}) %collective-permute-start.3) | collective-permute-done | bytes 524320 | tf_op jit(solution)/shard_map/ppermute | solution.py:199
  92.3 8.3 %all-to-all-done.1 = bf16[64,40,128]{2,1,0:T(8,128)(2,1)S(1)} async-done(((bf16[64,40,128]{2,1,0:T(8,128)(2,1)}), bf16[64,40,128]{2,1,0:T(8,128)(2,1)S(1)}, u32[]{:S(2)}, u32[]{:S(2)}) %all-to-all-start.1) | async-done | bytes 655392 | tf_op jit(solution)/shard_map/all_to_all | solution.py:205
  100.6 0.0 copy-start
  100.6 0.8 copy-done
  101.4 2.2 %spread.1 = (f32[128,1152]{1,0:T(8,128)}, f32[128,1152]{1,0:T(8,128)}) custom-call(bf16[2560,128]{1,0:T(8,128)(2,1)} %bitcast.13), custom_call_target="tpu_custom_call" | custom-call | tf_op jit(solution)/shard_map/spread/pallas_call | solution.py:206
  103.6 0.8 copy.14
  104.4 0.8 copy.15
Async XLA Ops:
  0.6 8.2 %copy-start.3 = (f32[1,128,8]{1,2,0:T(8,128)S(1)}, f32[1,128,8]{1,2,0:T(8,128)}, u32[]{:S(2)}) copy-start(f32[1,128,8]{1,2,0:T(8,128)} %param.11) | copy-start | bytes 12292
  3.2 13.1 %collective-permute-start = (bf16[784,256]{1,0:T(8,128)(2,1)}, bf16[784,256]{1,0:T(8,128)(2,1)S(1)}, u32[]{:S(2)}, u32[]{:S(2)}) collective-permute-start(bf16[784,256]{1,0:T(8,128)(2,1)} %get-tuple-element.11), channel_id=1, source_target_pairs={{0,1},{1,2},{2,3},{3,4},{4,5},{5,6},{6,7},{7,8},{8,9},{9,10},{10,1... | collective-permute-start | bytes 1204232 | tf_op jit(solution)/shard_map/ppermute | solution.py:174
  7.5 13.5 %collective-permute-start.1 = (bf16[784,256]{1,0:T(8,128)(2,1)}, bf16[784,256]{1,0:T(8,128)(2,1)S(1)}, u32[]{:S(2)}, u32[]{:S(2)}) collective-permute-start(bf16[784,256]{1,0:T(8,128)(2,1)} %get-tuple-element.12), channel_id=1, source_target_pairs={{1,0},{2,1},{3,2},{4,3},{5,4},{6,5},{7,6},{8,7},{9,8},{10,9},{11,1... | collective-permute-start | bytes 1204232 | tf_op jit(solution)/shard_map/ppermute | solution.py:175
  16.3 4.7 %copy-start.1 = (bf16[784,256]{1,0:T(8,128)(2,1)}, bf16[784,256]{1,0:T(8,128)(2,1)S(1)}, u32[]{:S(2)}) copy-start(bf16[784,256]{1,0:T(8,128)(2,1)S(1)} %collective-permute-done.above_ref) | copy-start | bytes 1204228
  21.0 0.7 copy-start.2
  74.0 6.0 %copy-start.5 = (bf16[128,8,256]{2,1,0:T(8,128)(2,1)S(1)}, bf16[128,8,256]{2,1,0:T(8,128)(2,1)}, u32[]{:S(2)}) copy-start(bf16[128,8,256]{2,1,0:T(8,128)(2,1)} %get-tuple-element.13) | copy-start | bytes 1572868
  74.0 8.0 %copy-start.4 = (bf16[128,8,256]{2,1,0:T(8,128)(2,1)S(1)}, bf16[128,8,256]{2,1,0:T(8,128)(2,1)}, u32[]{:S(2)}) copy-start(bf16[128,8,256]{2,1,0:T(8,128)(2,1)} %get-tuple-element.14) | copy-start | bytes 1572868
  74.0 26.6 %all-to-all-start.1 = ((bf16[64,40,128]{2,1,0:T(8,128)(2,1)}), bf16[64,40,128]{2,1,0:T(8,128)(2,1)S(1)}, u32[]{:S(2)}, u32[]{:S(2)}) async-start(bf16[64,40,128]{2,1,0:T(8,128)(2,1)} %sum_shares.1), calls=%async_computation.1 | async-start | bytes 1310720 | tf_op jit(solution)/shard_map/all_to_all | solution.py:205
  80.0 10.5 %collective-permute-start.2 = (bf16[128,8,256]{2,1,0:T(8,128)(2,1)S(1)}, bf16[128,8,256]{2,1,0:T(8,128)(2,1)S(1)}, u32[]{:S(2)}, u32[]{:S(2)}) collective-permute-start(bf16[128,8,256]{2,1,0:T(8,128)(2,1)S(1)} %copy-done.5), channel_id=1, source_target_pairs={{0,64},{64,128},{128,192},{192,256},{256,320},{320,384},{384,448},... | collective-permute-start | bytes 1572872 | tf_op jit(solution)/shard_map/ppermute | solution.py:198
  82.0 10.3 %collective-permute-start.3 = (bf16[128,8,256]{2,1,0:T(8,128)(2,1)S(1)}, bf16[128,8,256]{2,1,0:T(8,128)(2,1)S(1)}, u32[]{:S(2)}, u32[]{:S(2)}) collective-permute-start(bf16[128,8,256]{2,1,0:T(8,128)(2,1)S(1)} %copy-done.4), channel_id=1, source_target_pairs={{64,0},{128,64},{192,128},{256,192},{320,256},{384,320},{448,384},... | collective-permute-start | bytes 1572872 | tf_op jit(solution)/shard_map/ppermute | solution.py:199
  100.6 0.8 copy-start

commit v2 on v1

v2 whole, which is shorter than its diff:
```python
import jax
import jax.numpy as jnp
from jax import lax
from jax.experimental import pallas as pl
from jax.experimental.pallas import tpu as pltpu
from jax.sharding import PartitionSpec as P

CH = 128
COLS = 256
LOCAL = 8
CLASSES = 8
TAPS = 9
WIDE = 3 * CH
BF16 = jnp.bfloat16
F32 = jnp.float32


def fetch(sems, *pairs):
    copies = [pltpu.make_async_copy(src, dst, sems.at[i]) for i, (src, dst) in enumerate(pairs)]
    for copy in copies:
        copy.start()
    return copies


def edges_kernel(bwd_hbm, grad_hbm, fwd_hbm, use_hbm, head_ref, tail_ref, bwd_ref, grad_ref, fwd_ref, use_ref, sems):
    copies = fetch(sems, (bwd_hbm, bwd_ref), (grad_hbm, grad_ref), (fwd_hbm, fwd_ref), (use_hbm, use_ref))
    for i, ref in enumerate((bwd_ref, grad_ref, fwd_ref)):
        copies[i].wait()
        rows = jnp.swapaxes(ref[...], 0, 1)
        for k in range(2):
            head_ref[(2 * i + k) * CH : (2 * i + k + 1) * CH] = rows[k]
            tail_ref[(2 * i + k) * CH : (2 * i + k + 1) * CH] = rows[LOCAL - 2 + k]
    copies[3].wait()
    sub = lax.broadcasted_iota(jnp.int32, (16, COLS), 0)
    for out, edge in ((head_ref, 0), (tail_ref, LOCAL - 1)):
        ahead = use_ref[0, edge : edge + 1, :].astype(F32) + 1.0
        back = use_ref[1, edge : edge + 1, :].astype(F32) + 1.0
        out[6 * CH :] = jnp.where(sub == 0, ahead, jnp.where(sub == 1, back, 0.0)).astype(BF16)


def put_shifted(wide_ref, at, row):
    lane = lax.broadcasted_iota(jnp.int32, (CH, COLS), 1)
    zero = jnp.zeros((CH, COLS), BF16)
    wide_ref[at, 0:CH] = jnp.where(lane == 0, zero, pltpu.roll(row, 1, 1))
    wide_ref[at, CH : 2 * CH] = row
    wide_ref[at, 2 * CH :] = jnp.where(lane == COLS - 1, zero, pltpu.roll(row, COLS - 1, 1))


def three_rows(ref, at):
    return ref[pl.ds(at, 3)].reshape(-1, COLS)


def dot(a, b):
    return jnp.dot(a, b, preferred_element_type=F32)


def dot_cells(a, b):
    return lax.dot_general(a, b, (((1,), (1,)), ((), ())), preferred_element_type=F32)


def put_flipped(flip_ref, weight_ref):
    for t in range(TAPS):
        mirrored = (TAPS - 1 - t) * CH
        flip_ref[:, mirrored : mirrored + CH] = weight_ref[:, t * CH : (t + 1) * CH].T


def friction_terms(table):
    high = table.astype(BF16).astype(F32)
    middle = (table - high).astype(BF16).astype(F32)
    low = table - high - middle
    return jnp.concatenate([high, middle, low], axis=0).T.astype(BF16)


def friction_row(terms, classes):
    level = (lax.broadcasted_iota(jnp.int32, (3 * CLASSES, COLS), 0) % CLASSES + 1).astype(F32)
    return dot(terms, jnp.where(classes == level, 1.0, 0.0).astype(BF16))


def backward_row(first, flip2, fric, stored_rows, grad_rows):
    hb = dot(first, stored_rows)
    sig = 0.5 + 0.5 * jnp.tanh(0.5 * hb)
    active = (hb * sig * fric).astype(BF16)
    ga = dot(flip2, grad_rows)
    return active, (ga * fric * (sig * (1.0 + hb * (1.0 - sig)))).astype(BF16)


def inner_kernel(
    bwd_hbm, grad_hbm, use_hbm, table_hbm, first_hbm, second_hbm,
    gh_out_ref, near_ref, sum_ref, fric_ref, flip_ref,
    bwd_ref, grad_ref, use_ref, table_ref, first_ref, second_ref,
    wide_b_ref, wide_g_ref, actb_ref, gh_ref, class_ref, sems,
):
    copies = fetch(
        sems, (second_hbm, second_ref), (bwd_hbm, bwd_ref), (grad_hbm, grad_ref),
        (use_hbm, use_ref), (table_hbm, table_ref), (first_hbm, first_ref),
    )
    for ref in (actb_ref, gh_ref):
        for r in (0, 1, 8, 9):
            ref[r] = jnp.zeros((CH, COLS), BF16)
    copies[0].wait()
    put_flipped(flip_ref, second_ref)
    for i, (ref, wide_ref) in enumerate(((bwd_ref, wide_b_ref), (grad_ref, wide_g_ref))):
        copies[1 + i].wait()
        rows = jnp.swapaxes(ref[...], 0, 1)
        for r in range(LOCAL):
            put_shifted(wide_ref, r, rows[r])
        for k, r in enumerate((0, 1, LOCAL - 2, LOCAL - 1)):
            near_ref[i, k] = rows[r]
    copies[3].wait()
    copies[4].wait()
    class_ref[...] = use_ref[1].astype(F32) + 1.0
    terms = friction_terms(table_ref[...])
    for k, r in enumerate((0, LOCAL - 1)):
        fric_ref[k] = friction_row(terms, class_ref[r : r + 1])
    copies[5].wait()

    def step(n, carry):
        for k in range(3):
            r = 3 * n + k + 1
            active, gh = backward_row(
                first_ref[...], flip_ref[...], friction_row(terms, class_ref[pl.ds(r, 1)]),
                three_rows(wide_b_ref, r - 1), three_rows(wide_g_ref, r - 1),
            )
            actb_ref[r + 1] = active
            gh_ref[r + 1] = gh
            gh_out_ref[r - 1] = gh
        return carry

    lax.fori_loop(0, 2, step, 0)
    total = None
    for r in range(LOCAL):
        part = dot_cells(three_rows(gh_ref, r), wide_b_ref[r])
        total = part if total is None else total + part
    sum_ref[0] = total
    total = None
    for r in range(LOCAL):
        part = dot_cells(wide_g_ref[r], three_rows(actb_ref, r))
        total = part if total is None else total + part
    sum_ref[1] = total


def outer_kernel(
    first_hbm, near_ref, above_ref, below_ref, fric_ref, flip_ref, sum_ref,
    gh_out_ref, gw_ref,
    first_ref, wide_ref, sems,
):
    (copy,) = fetch(sems, (first_hbm, first_ref))
    for i in range(2):
        put_shifted(wide_ref.at[i], 0, above_ref[(2 * i + 1) * CH : (2 * i + 2) * CH])
        for k in range(4):
            put_shifted(wide_ref.at[i], 1 + k, near_ref[i, k])
        put_shifted(wide_ref.at[i], 5, below_ref[2 * i * CH : (2 * i + 1) * CH])
    copy.wait()
    first_part = second_part = None
    for k in range(2):
        stored_rows, grad_rows = three_rows(wide_ref.at[0], 3 * k), three_rows(wide_ref.at[1], 3 * k)
        active, gh = backward_row(first_ref[...], flip_ref[...], fric_ref[k], stored_rows, grad_rows)
        gh_out_ref[k] = gh
        one, two = dot_cells(gh, stored_rows), dot_cells(grad_rows, active)
        first_part = one if first_part is None else first_part + one
        second_part = two if second_part is None else second_part + two
    for a in range(3):
        for b in range(3):
            at = (a * 3 + b) * CH
            whole = sum_ref[0, a * CH : (a + 1) * CH, b * CH : (b + 1) * CH]
            whole = whole + first_part[:, (2 - a) * WIDE + b * CH : (2 - a) * WIDE + (b + 1) * CH]
            gw_ref[at : at + CH] = whole.astype(BF16)
            at = (TAPS + a * 3 + b) * CH
            whole = sum_ref[1, a * CH : (a + 1) * CH, b * CH : (b + 1) * CH]
            whole = whole + second_part[(2 - b) * WIDE + a * CH : (2 - b) * WIDE + (a + 1) * CH]
            gw_ref[at : at + CH] = whole.astype(BF16)
    spare = gw_ref.shape[0] - 2 * TAPS * CH
    if spare:
        gw_ref[2 * TAPS * CH :] = jnp.zeros((spare, CH), BF16)


def forward_kernel(
    fwd_hbm, use_hbm, table_hbm, first_hbm, second_hbm, above_ref, below_ref,
    out_ref,
    fwd_ref, use_ref, table_ref, first_ref, second_ref,
    rows_ref, wide_ref, wide_act_ref, class_ref, sems,
):
    copies = fetch(
        sems, (fwd_hbm, fwd_ref), (use_hbm, use_ref), (table_hbm, table_ref),
        (first_hbm, first_ref), (second_hbm, second_ref),
    )
    class_ref[0:1] = above_ref[6 * CH :].astype(F32)[0:1]
    class_ref[9:10] = below_ref[6 * CH :].astype(F32)[0:1]
    for k in range(2):
        put_shifted(wide_ref, k, above_ref[(4 + k) * CH : (5 + k) * CH])
        put_shifted(wide_ref, 10 + k, below_ref[(4 + k) * CH : (5 + k) * CH])
    copies[0].wait()
    rows = jnp.swapaxes(fwd_ref[...], 0, 1)
    rows_ref[...] = rows
    for r in range(LOCAL):
        put_shifted(wide_ref, 2 + r, rows[r])
    for copy in copies[1:]:
        copy.wait()
    class_ref[1:9] = use_ref[0].astype(F32) + 1.0
    terms = friction_terms(table_ref[...])

    def hidden_rows(step, carry):
        for k in range(5):
            r = 5 * step + k
            half = 0.5 * dot(first_ref[...], three_rows(wide_ref, r))
            act = (half + half * jnp.tanh(half)) * friction_row(terms, class_ref[pl.ds(r, 1)])
            put_shifted(wide_act_ref, r, act.astype(BF16))
        return carry

    lax.fori_loop(0, 2, hidden_rows, 0)

    def result_rows(step, carry):
        for k in range(4):
            r = 4 * step + k
            add = dot(second_ref[...], three_rows(wide_act_ref, r))
            out_ref[r] = (rows_ref[r].astype(F32) + add).astype(BF16)
        return carry

    lax.fori_loop(0, 2, result_rows, 0)


def grad_x_kernel(
    grad_hbm, first_hbm, table_hbm, inner_ref, outer_ref, near_ref, above_ref, below_ref, flip2_ref,
    gx_ref,
    grad_ref, first_ref, table_ref, rows_ref, wide_ref, beside_ref, flip_ref, sems,
):
    copies = fetch(sems, (first_hbm, first_ref), (table_hbm, table_ref), (grad_hbm, grad_ref))
    for i in range(2):
        for k in range(2):
            put_shifted(beside_ref.at[i], k, above_ref[(2 * i + k) * CH : (2 * i + k + 1) * CH])
            put_shifted(beside_ref.at[i], 4 + k, below_ref[(2 * i + k) * CH : (2 * i + k + 1) * CH])
        put_shifted(beside_ref.at[i], 2, near_ref[i, 0])
        put_shifted(beside_ref.at[i], 3, near_ref[i, 3])
    put_shifted(wide_ref, 1, outer_ref[0])
    for r in range(LOCAL - 2):
        put_shifted(wide_ref, 2 + r, inner_ref[r])
    put_shifted(wide_ref, 8, outer_ref[1])
    for copy in copies[:2]:
        copy.wait()
    put_flipped(flip_ref, first_ref)
    terms = friction_terms(table_ref[...])
    for k, ref in enumerate((above_ref, below_ref)):
        _, gh = backward_row(
            first_ref[...], flip2_ref[...], friction_row(terms, ref[6 * CH :].astype(F32)[1:2]),
            three_rows(beside_ref.at[0], 3 * k), three_rows(beside_ref.at[1], 3 * k),
        )
        put_shifted(wide_ref, 9 * k, gh)
    copies[2].wait()
    rows_ref[...] = jnp.swapaxes(grad_ref[...], 0, 1)

    def result_rows(step, carry):
        for k in range(4):
            r = 4 * step + k
            add = dot(flip_ref[...], three_rows(wide_ref, r))
            gx_ref[r] = (rows_ref[r].astype(F32) + add).astype(BF16)
        return carry

    lax.fori_loop(0, 2, result_rows, 0)


def turn_kernel(act_ref, grad_ref, act_out_ref, grad_out_ref):
    act_out_ref[...] = jnp.swapaxes(act_ref[...], 0, 1)
    grad_out_ref[...] = jnp.swapaxes(grad_ref[...], 0, 1)


def sum_kernel(scale, parts_ref, out_ref):
    total = jnp.sum(parts_ref[...].astype(F32), axis=0) * scale
    out_ref[...] = jnp.broadcast_to(total.astype(BF16)[None], out_ref.shape)


def spread_kernel(flat_ref, first_ref, second_ref):
    for a in range(3):
        for b in range(3):
            at = (a * 3 + b) * CH
            to = ((2 - a) * 3 + b) * CH
            first_ref[:, to : to + CH] = flat_ref[at : at + CH].astype(F32)
            at = (TAPS + a * 3 + b) * CH
            to = (b * 3 + 2 - a) * CH
            second_ref[:, to : to + CH] = flat_ref[at : at + CH].astype(F32)


def kernel_call(kernel, outs, scratch, name, flops, hbm, vmem, limit=24):
    outs = [jax.ShapeDtypeStruct(dims, kind) for dims, kind in outs]
    scratch = [(x.shape, x.dtype) for x in hbm] + scratch
    sems = [pltpu.SemaphoreType.DMA((len(hbm),))] if hbm else []
    size = sum(x.size * x.dtype.itemsize for x in [*hbm, *vmem, *outs])
    return pl.pallas_call(
        kernel,
        in_specs=[pl.BlockSpec(memory_space=pltpu.HBM)] * len(hbm) + [pl.BlockSpec(memory_space=pltpu.VMEM)] * len(vmem),
        out_shape=outs,
        scratch_shapes=[pltpu.VMEM(dims, kind) for dims, kind in scratch] + sems,
        cost_estimate=pl.CostEstimate(flops=flops, bytes_accessed=size, transcendentals=0),
        compiler_params=pltpu.CompilerParams(vmem_limit_bytes=limit * 1024 * 1024),
        name=name,
    )(*hbm, *vmem)


def body(fwd_in, bwd_in, grad_in, land_use, friction, weight_in, weight_out):
    row_count = lax.axis_size("rows")
    sections = lax.axis_size("pipe")
    fwd, bwd, grad = fwd_in[0], bwd_in[0], grad_in[0]
    use, table, first, second = land_use[0], friction[0].T, weight_in[0], weight_out[0]
    scale = 1.0 / (LOCAL * row_count * COLS) ** 0.5
    share = -(-2 * TAPS * CH // (8 * row_count)) * 8
    cells, weight = (CH, LOCAL, COLS), (CH, TAPS * CH)
    row, wide = (CH, COLS), (WIDE, COLS)
    row_flops = 2 * CH * TAPS * CH * COLS
    down = [(i, i + 1) for i in range(row_count - 1)]
    up = [(i + 1, i) for i in range(row_count - 1)]

    head, tail = kernel_call(
        edges_kernel, [((6 * CH + 16, COLS), BF16)] * 2, [], "edges", 0, [bwd, grad, fwd, use], [], 56
    )
    above, below = lax.ppermute(tail, "rows", down), lax.ppermute(head, "rows", up)
    gh_inner, near, sums, fric, flip = kernel_call(
        inner_kernel,
        [((LOCAL - 2, *row), BF16), ((2, 4, *row), BF16), ((2, WIDE, WIDE), F32), ((2, *row), F32), (weight, BF16)],
        [((LOCAL, *wide), BF16)] * 2 + [((10, *row), BF16)] * 2 + [((LOCAL, COLS), F32)],
        "inner", 28 * row_flops,
        [bwd, grad, use, table, first, second], [],
    )
    gh_outer, partial = kernel_call(
        outer_kernel,
        [((2, *row), BF16), ((row_count * share, CH), BF16)],
        [((2, 6, *wide), BF16)],
        "outer", 8 * row_flops,
        [first], [near, above, below, fric, flip, sums],
    )
    shares = lax.all_to_all(partial.reshape(row_count, share, CH), "rows", 0, 0)

    above, below, gh_outer = lax.optimization_barrier((above, below, gh_outer))
    (result,) = kernel_call(
        forward_kernel,
        [((LOCAL, *row), BF16)],
        [((LOCAL, *row), BF16), ((12, *wide), BF16), ((10, *wide), BF16), ((16, COLS), F32)],
        "forward", 18 * row_flops,
        [fwd, use, table, first, second], [above, below],
    )
    handed_act = lax.ppermute(result, "pipe", [(i, i + 1) for i in range(sections - 1)])
    (grad_x,) = kernel_call(
        grad_x_kernel,
        [((LOCAL, *row), BF16)],
        [((LOCAL, *row), BF16), ((10, *wide), BF16), ((2, 6, *wide), BF16), (weight, BF16)],
        "grad_x", 12 * row_flops,
        [grad, first, table], [gh_inner, gh_outer, near, above, below, flip],
    )
    handed_grad = lax.ppermute(grad_x, "pipe", [(i + 1, i) for i in range(sections - 1)])
    handed_act, handed_grad = kernel_call(
        turn_kernel, [(cells, BF16)] * 2, [], "turn", 0, [], [handed_act, handed_grad]
    )
    shares, result, grad_x = lax.optimization_barrier((shares, result, grad_x))

    (summed,) = kernel_call(
        lambda *refs: sum_kernel(scale, *refs), [((row_count, share, CH), BF16)], [], "sum_shares", 0, [], [shares]
    )
    gathered = lax.all_to_all(summed, "rows", 0, 0).reshape(row_count * share, CH)
    grad_first, grad_second = kernel_call(spread_kernel, [(weight, F32)] * 2, [], "spread", 0, [], [gathered])
    return (handed_act[None], handed_grad[None], grad_first[None], grad_second[None])


def solution(mesh):
    cells = P("pipe", None, "rows", None)
    own = P("pipe", None, None)
    return jax.shard_map(
        body,
        mesh=mesh,
        in_specs=(cells, cells, cells, cells, own, own, own),
        out_specs=(cells, cells, own, own),
        check_vma=False,
    )
```

time: 106 us -> 90.3 us (0.85)
  blocking collectives: 36.8 us -> 0 us
  starting transfers between devices: 17.2 us -> 33 us
  waiting for transfers between devices: 26.4 us -> 32 us
    all_to_all x1 -> x0, blocking collectives: 36.8 us -> none  [body(): shares = lax.all_to_all(partial.reshape(row_count, share, CH), 'rows', 0, 0)]
    all_to_all x0 -> x1, starting transfers between devices: none -> 16 us  [body(): shares = lax.all_to_all(partial.reshape(row_count, share, CH), 'rows', 0, 0)]
    all_to_all x0 -> x1, waiting for transfers between devices: none -> 11.9 us  [body(): shares = lax.all_to_all(partial.reshape(row_count, share, CH), 'rows', 0, 0)]
    ppermute x2, waiting for transfers between devices: 11.4 us -> 6.28 us  [the longest x1 4.65 us: body(): lax.ppermute(head, 'rows', up)]
    all_to_all x1, waiting for transfers between devices: 8.25 us -> 7.16 us  [body(): lax.all_to_all(summed, 'rows', 0, 0).reshape(row_count * share, CH)]
    pallas_call x4 -> x8, Pallas kernels: 20.2 us -> 19.4 us  [kernel_call(): pl.pallas_call(kernel, in_specs=[pl.BlockSpec(memory_space=pltpu.HBM)] *...]
    unnamed x15 -> x26, local copies, waits for them, and re-layouts: 3.91 us -> 4.18 us
  transfers between devices with their start and end apart: 5 -> 6, of which waited for: 5 -> 6; matrix products, arithmetic and copies ran while one was open for 1% -> 0% of each run, Pallas kernels for 0% -> 15%
where the time goes in v2:
time: 90.3 us; the launch traced here: 89.5 us
  starting transfers between devices  33 us (37%)
  waiting for transfers between devices  32 us (35%)
  Pallas kernels  19.4 us (21%)
  local copies, waits for them, and re-layouts  4.18 us (5%)
    pallas_call x8, Pallas kernels, kernel_call(): pl.pallas_call(kernel, in_specs=[pl.BlockSpec(memory_space=pltpu.HBM)] *...  19.4 us
    all_to_all x1, starting transfers between devices, body(): shares = lax.all_to_all(partial.reshape(row_count, share, CH), 'rows', 0, 0)  16 us
    all_to_all x1, waiting for transfers between devices, body(): shares = lax.all_to_all(partial.reshape(row_count, share, CH), 'rows', 0, 0)  11.9 us
    all_to_all x1, waiting for transfers between devices, body(): lax.all_to_all(summed, 'rows', 0, 0).reshape(row_count * share, CH)  7.16 us
    all_to_all x1, starting transfers between devices, body(): lax.all_to_all(summed, 'rows', 0, 0).reshape(row_count * share, CH)  5.88 us
    ppermute x1, waiting for transfers between devices, body(): lax.ppermute(result, 'pipe', [(i, i + 1) for i in range(sections - 1)])  5.12 us
    ppermute x1, waiting for transfers between devices, body(): lax.ppermute(head, 'rows', up)  4.65 us
    ppermute x1, starting transfers between devices, body(): lax.ppermute(tail, 'rows', down)  4.3 us
  transfers between devices with their start and end apart: 6, of which 6 were waited for; matrix products, arithmetic and copies ran while one was open for 0% of the time, Pallas kernels for 15%

profile of v2, /device:TPU:6, one launch (start us, length us, event | category | flops | bytes accessed | tf_op | source)
XLA Modules:
  0.0 89.5 jit_solution(11425266686847181062)
XLA Ops:
  0.6 0.0 copy-start.9
  0.6 0.0 copy-start
  0.7 0.0 copy-start.3
  0.7 0.0 copy-start.1
  0.7 0.0 copy-start.10
  0.7 2.5 %edges.1 = (bf16[784,256]{1,0:T(8,128)(2,1)}, bf16[784,256]{1,0:T(8,128)(2,1)}) custom-call(bf16[128,8,256]{2,1,0:T(8,128)(2,1)} %bitcast.24, bf16[128,8,256]{2,1,0:T(8,128)(2,1)} %bitcast.16, bf16[128,8,256]{2,1,0:T(8,128)(2,1)} %bitcast.26, s32[2,8,256]{2,1,0:T(8,128)} %bitcast.28), custom_call_target="tpu_custom_call" | custom-call | bytes 2392064 | tf_op jit(solution)/shard_map/edges/pallas_call | solution.py:287
  3.2 4.3 %collective-permute-start = (bf16[784,256]{1,0:T(8,128)(2,1)}, bf16[784,256]{1,0:T(8,128)(2,1)S(1)}, u32[]{:S(2)}, u32[]{:S(2)}) collective-permute-start(bf16[784,256]{1,0:T(8,128)(2,1)} %get-tuple-element.21), channel_id=1, source_target_pairs={{0,1},{1,2},{2,3},{3,4},{4,5},{5,6},{6,7},{7,8},{8,9},{9,10},{10,1... | collective-permute-start | bytes 1204232 | tf_op jit(solution)/shard_map/ppermute | solution.py:314
  7.5 1.3 %collective-permute-start.1 = (bf16[784,256]{1,0:T(8,128)(2,1)}, bf16[784,256]{1,0:T(8,128)(2,1)S(1)}, u32[]{:S(2)}, u32[]{:S(2)}) collective-permute-start(bf16[784,256]{1,0:T(8,128)(2,1)} %get-tuple-element.22), channel_id=1, source_target_pairs={{1,0},{2,1},{3,2},{4,3},{5,4},{6,5},{7,6},{8,7},{9,8},{10,9},{11,1... | collective-permute-start | bytes 1204232 | tf_op jit(solution)/shard_map/ppermute | solution.py:314
  8.8 0.0 copy-done.9
  8.8 0.0 copy-done
  8.8 0.0 copy-done.3
  8.8 0.0 copy-done.1
  8.8 0.0 copy-done.10
  8.8 0.0 copy-start.11
  8.8 1.0 %copy-done.11 = bf16[1,128,1152]{2,1,0:T(8,128)(2,1)S(1)} copy-done((bf16[1,128,1152]{2,1,0:T(8,128)(2,1)S(1)}, bf16[1,128,1152]{2,1,0:T(8,128)(2,1)}, u32[]{:S(2)}) %copy-start.11) | copy-done | bytes 294936
  9.8 4.9 %inner.1 = (bf16[6,128,256]{2,1,0:T(8,128)(2,1)S(1)}, bf16[2,4,128,256]{3,2,1,0:T(8,128)(2,1)S(1)}, f32[2,384,384]{2,1,0:T(8,128)S(1)}, f32[2,128,256]{2,1,0:T(8,128)S(1)}, bf16[128,1152]{1,0:T(8,128)(2,1)S(1)}) custom-call(bf16[128,8,256]{2,1,0:T(8,128)(2,1)S(1)} %bitcast.25, bf16[128,8,256]{2,1,0:T(8,128)(2,1)S(1)} %bitcast.17, s32[2,8,256]{2,1,0:T(8,128)S(1)} %bitcast.29, ...), custom_call_target="tpu_custom_call" | custom-call | flops 2113929216 | bytes 4313088 | tf_op jit(solution)/shard_map/inner/pallas_call | solution.py:287
  14.7 1.6 %collective-permute-done.above_ref = bf16[784,256]{1,0:T(8,128)(2,1)S(1)} collective-permute-done((bf16[784,256]{1,0:T(8,128)(2,1)}, bf16[784,256]{1,0:T(8,128)(2,1)S(1)}, u32[]{:S(2)}, u32[]{:S(2)}) %collective-permute-start) | collective-permute-done | bytes 401440 | tf_op jit(solution)/shard_map/ppermute | solution.py:314
  16.3 4.6 %collective-permute-done.1.below_ref = bf16[784,256]{1,0:T(8,128)(2,1)S(1)} collective-permute-done((bf16[784,256]{1,0:T(8,128)(2,1)}, bf16[784,256]{1,0:T(8,128)(2,1)S(1)}, u32[]{:S(2)}, u32[]{:S(2)}) %collective-permute-start.1) | collective-permute-done | bytes 401440 | tf_op jit(solution)/shard_map/ppermute | solution.py:314
  21.0 1.8 %outer.1 = (bf16[2,128,256]{2,1,0:T(8,128)(2,1)S(1)}, bf16[2560,128]{1,0:T(8,128)(2,1)S(1)}) custom-call(bf16[128,1152]{1,0:T(8,128)(2,1)S(1)} %bitcast.20, bf16[2,4,128,256]{3,2,1,0:T(8,128)(2,1)S(1)} %get-tuple-element.23.near_ref, bf16[784,256]{1,0:T(8,128)(2,1)S(1)} %collective-permute-done.above_ref, ...), custom_call_target="tpu_custom_call" | custom-call | flops 603979776 | bytes 4145152 | tf_op jit(solution)/shard_map/outer/pallas_call | solution.py:287
  22.7 0.0 copy-start.2
  22.7 0.8 copy-done.2
  23.6 0.0 copy-start.7
  23.6 0.7 copy-done.7
  24.2 16.0 %all-to-all-start = ((bf16[64,40,128]{2,1,0:T(8,128)(2,1)}), bf16[64,40,128]{2,1,0:T(8,128)(2,1)S(1)}, u32[]{:S(2)}, u32[]{:S(2)}) async-start(bf16[64,40,128]{2,1,0:T(8,128)(2,1)} %bitcast.23), calls=%async_computation | async-start | bytes 1310720 | tf_op jit(solution)/shard_map/all_to_all | solution.py:329
  40.2 0.0 copy-start.8
  40.2 0.9 %copy-done.8 = bf16[2,128,256]{2,1,0:T(8,128)(2,1)S(1)} copy-done((bf16[2,128,256]{2,1,0:T(8,128)(2,1)S(1)}, bf16[2,128,256]{2,1,0:T(8,128)(2,1)}, u32[]{:S(2)}) %copy-start.8) | copy-done | bytes 131096
  41.1 0.0 copy-start.4
  41.1 0.0 copy-start.12
  41.1 2.7 %grad_x.1 = bf16[8,128,256]{2,1,0:T(8,128)(2,1)S(1)} custom-call(bf16[128,8,256]{2,1,0:T(8,128)(2,1)S(1)} %bitcast.18, bf16[128,1152]{1,0:T(8,128)(2,1)S(1)} %bitcast.21, f32[8,128]{1,0:T(8,128)S(1)} %bitcast.32, bf16[6,128,256]{2,1,0:T(8,128)(2,1)S(1)} %get-tuple-element.30.inner_ref, bf16[2,128,256]{2,1,0:T(8,128)(2,1)S(1)} %copy-done.8, ...), custom_call_target="tpu_custom_call" | custom-call | flops 905969664 | bytes 3493888 | tf_op jit(solution)/shard_map/grad_x/pallas_call | solution.py:287
  43.9 0.0 copy-start.5
  43.9 0.8 copy-done.5
  44.7 0.0 copy-done.4
  44.7 0.0 copy-done.12
  44.7 4.4 %forward.1 = bf16[8,128,256]{2,1,0:T(8,128)(2,1)} custom-call(bf16[128,8,256]{2,1,0:T(8,128)(2,1)S(1)} %bitcast.27, s32[2,8,256]{2,1,0:T(8,128)S(1)} %bitcast.30, f32[8,128]{1,0:T(8,128)S(1)} %bitcast.33, bf16[128,1152]{1,0:T(8,128)(2,1)S(1)} %bitcast.22, bf16[128,1152]{1,0:T(8,128)(2,1)S(1)} %bitcast.35, ...), custom_call_target="tpu_custom_call" | custom-call | flops 1358954496 | bytes 2461696 | tf_op jit(solution)/shard_map/forward/pallas_call | solution.py:287
  49.1 0.0 copy-start.6
  49.1 11.9 %all-to-all-done.refs_0_ = bf16[64,40,128]{2,1,0:T(8,128)(2,1)S(1)} async-done(((bf16[64,40,128]{2,1,0:T(8,128)(2,1)}), bf16[64,40,128]{2,1,0:T(8,128)(2,1)S(1)}, u32[]{:S(2)}, u32[]{:S(2)}) %all-to-all-start) | async-done | bytes 655392 | tf_op jit(solution)/shard_map/all_to_all | solution.py:329
  61.0 1.0 %sum_shares.1 = bf16[64,40,128]{2,1,0:T(8,128)(2,1)} custom-call(bf16[64,40,128]{2,1,0:T(8,128)(2,1)S(1)} %all-to-all-done.refs_0_), custom_call_target="tpu_custom_call" | custom-call | bytes 1310720 | tf_op jit(solution)/shard_map/sum_shares/pallas_call | solution.py:287
  62.0 5.9 %all-to-all-start.1 = ((bf16[64,40,128]{2,1,0:T(8,128)(2,1)}), bf16[64,40,128]{2,1,0:T(8,128)(2,1)S(1)}, u32[]{:S(2)}, u32[]{:S(2)}) async-start(bf16[64,40,128]{2,1,0:T(8,128)(2,1)} %sum_shares.1), calls=%async_computation.1 | async-start | bytes 1310720 | tf_op jit(solution)/shard_map/all_to_all | solution.py:356
  67.9 1.9 %collective-permute-start.2 = (bf16[8,128,256]{2,1,0:T(8,128)(2,1)}, bf16[8,128,256]{2,1,0:T(8,128)(2,1)S(1)}, u32[]{:S(2)}, u32[]{:S(2)}) collective-permute-start(bf16[8,128,256]{2,1,0:T(8,128)(2,1)} %forward.1), channel_id=1, source_target_pairs={{0,64},{64,128},{128,192},{192,256},{256,320},{320,384},{384,448},... | collective-permute-start | bytes 1572872 | tf_op jit(solution)/shard_map/ppermute | solution.py:339
  69.8 0.0 copy-done.6
  69.8 3.6 %collective-permute-start.3 = (bf16[8,128,256]{2,1,0:T(8,128)(2,1)S(1)}, bf16[8,128,256]{2,1,0:T(8,128)(2,1)S(1)}, u32[]{:S(2)}, u32[]{:S(2)}) collective-permute-start(bf16[8,128,256]{2,1,0:T(8,128)(2,1)S(1)} %copy-done.6), channel_id=1, source_target_pairs={{64,0},{128,64},{192,128},{256,192},{320,256},{384,320},{448,384},... | collective-permute-start | bytes 1572872 | tf_op jit(solution)/shard_map/ppermute | solution.py:347
  73.5 5.1 %collective-permute-done.2.act_ref = bf16[8,128,256]{2,1,0:T(8,128)(2,1)S(1)} collective-permute-done((bf16[8,128,256]{2,1,0:T(8,128)(2,1)}, bf16[8,128,256]{2,1,0:T(8,128)(2,1)S(1)}, u32[]{:S(2)}, u32[]{:S(2)}) %collective-permute-start.2) | collective-permute-done | bytes 524320 | tf_op jit(solution)/shard_map/ppermute | solution.py:339
  78.6 1.6 %collective-permute-done.3.grad_ref = bf16[8,128,256]{2,1,0:T(8,128)(2,1)S(1)} collective-permute-done((bf16[8,128,256]{2,1,0:T(8,128)(2,1)S(1)}, bf16[8,128,256]{2,1,0:T(8,128)(2,1)S(1)}, u32[]{:S(2)}, u32[]{:S(2)}) %collective-permute-start.3) | collective-permute-done | bytes 524320 | tf_op jit(solution)/shard_map/ppermute | solution.py:347
  80.1 1.1 %turn.1 = (bf16[128,8,256]{2,1,0:T(8,128)(2,1)}, bf16[128,8,256]{2,1,0:T(8,128)(2,1)}) custom-call(bf16[8,128,256]{2,1,0:T(8,128)(2,1)S(1)} %collective-permute-done.2.act_ref, bf16[8,128,256]{2,1,0:T(8,128)(2,1)S(1)} %collective-permute-done.3.grad_ref), custom_call_target="tpu_custom_call" | custom-call | bytes 2097152 | tf_op jit(solution)/shard_map/turn/pallas_call | solution.py:287
  81.2 7.2 %all-to-all-done.1 = bf16[64,40,128]{2,1,0:T(8,128)(2,1)S(1)} async-done(((bf16[64,40,128]{2,1,0:T(8,128)(2,1)}), bf16[64,40,128]{2,1,0:T(8,128)(2,1)S(1)}, u32[]{:S(2)}, u32[]{:S(2)}) %all-to-all-start.1) | async-done | bytes 655392 | tf_op jit(solution)/shard_map/all_to_all | solution.py:356
  88.4 1.1 %spread.1 = (f32[128,1152]{1,0:T(8,128)}, f32[128,1152]{1,0:T(8,128)}) custom-call(bf16[2560,128]{1,0:T(8,128)(2,1)S(1)} %bitcast.15), custom_call_target="tpu_custom_call" | custom-call | bytes 1835008 | tf_op jit(solution)/shard_map/spread/pallas_call | solution.py:287
Async XLA Ops:
  0.6 8.1 %copy-start.9 = (s32[1,2,8,256]{3,2,1,0:T(8,128)S(1)}, s32[1,2,8,256]{3,2,1,0:T(8,128)}, u32[]{:S(2)}) copy-start(s32[1,2,8,256]{3,2,1,0:T(8,128)} %param.10) | copy-start | bytes 49156
  0.6 8.1 %copy-start = (bf16[1,128,8,256]{3,2,1,0:T(8,128)(2,1)S(1)}, bf16[1,128,8,256]{3,2,1,0:T(8,128)(2,1)}, u32[]{:S(2)}) copy-start(bf16[1,128,8,256]{3,2,1,0:T(8,128)(2,1)} %param.9) | copy-start | bytes 1572868
  0.7 8.1 %copy-start.3 = (bf16[1,128,8,256]{3,2,1,0:T(8,128)(2,1)S(1)}, bf16[1,128,8,256]{3,2,1,0:T(8,128)(2,1)}, u32[]{:S(2)}) copy-start(bf16[1,128,8,256]{3,2,1,0:T(8,128)(2,1)} %param.8) | copy-start | bytes 1572868
  0.7 8.1 %copy-start.1 = (bf16[1,128,1152]{2,1,0:T(8,128)(2,1)S(1)}, bf16[1,128,1152]{2,1,0:T(8,128)(2,1)}, u32[]{:S(2)}) copy-start(bf16[1,128,1152]{2,1,0:T(8,128)(2,1)} %param.12) | copy-start | bytes 884740
  0.7 8.1 %copy-start.10 = (f32[1,128,8]{1,2,0:T(8,128)S(1)}, f32[1,128,8]{1,2,0:T(8,128)}, u32[]{:S(2)}) copy-start(f32[1,128,8]{1,2,0:T(8,128)} %param.11) | copy-start | bytes 12292
  3.2 13.1 %collective-permute-start = (bf16[784,256]{1,0:T(8,128)(2,1)}, bf16[784,256]{1,0:T(8,128)(2,1)S(1)}, u32[]{:S(2)}, u32[]{:S(2)}) collective-permute-start(bf16[784,256]{1,0:T(8,128)(2,1)} %get-tuple-element.21), channel_id=1, source_target_pairs={{0,1},{1,2},{2,3},{3,4},{4,5},{5,6},{6,7},{7,8},{8,9},{9,10},{10,1... | collective-permute-start | bytes 1204232 | tf_op jit(solution)/shard_map/ppermute | solution.py:314
  7.5 13.5 %collective-permute-start.1 = (bf16[784,256]{1,0:T(8,128)(2,1)}, bf16[784,256]{1,0:T(8,128)(2,1)S(1)}, u32[]{:S(2)}, u32[]{:S(2)}) collective-permute-start(bf16[784,256]{1,0:T(8,128)(2,1)} %get-tuple-element.22), channel_id=1, source_target_pairs={{1,0},{2,1},{3,2},{4,3},{5,4},{6,5},{7,6},{8,7},{9,8},{10,9},{11,1... | collective-permute-start | bytes 1204232 | tf_op jit(solution)/shard_map/ppermute | solution.py:314
  8.8 1.0 %copy-start.11 = (bf16[1,128,1152]{2,1,0:T(8,128)(2,1)S(1)}, bf16[1,128,1152]{2,1,0:T(8,128)(2,1)}, u32[]{:S(2)}) copy-start(bf16[1,128,1152]{2,1,0:T(8,128)(2,1)} %param.13) | copy-start | bytes 884740
  22.7 0.9 copy-start.2
  23.6 0.7 copy-start.7
  24.2 36.8 %all-to-all-start = ((bf16[64,40,128]{2,1,0:T(8,128)(2,1)}), bf16[64,40,128]{2,1,0:T(8,128)(2,1)S(1)}, u32[]{:S(2)}, u32[]{:S(2)}) async-start(bf16[64,40,128]{2,1,0:T(8,128)(2,1)} %bitcast.23), calls=%async_computation | async-start | bytes 1310720 | tf_op jit(solution)/shard_map/all_to_all | solution.py:329
  40.2 0.9 %copy-start.8 = (bf16[2,128,256]{2,1,0:T(8,128)(2,1)S(1)}, bf16[2,128,256]{2,1,0:T(8,128)(2,1)}, u32[]{:S(2)}) copy-start(bf16[2,128,256]{2,1,0:T(8,128)(2,1)} %copy-done.7) | copy-start | bytes 393220
  41.1 3.6 %copy-start.4 = (bf16[1,128,8,256]{3,2,1,0:T(8,128)(2,1)S(1)}, bf16[1,128,8,256]{3,2,1,0:T(8,128)(2,1)}, u32[]{:S(2)}) copy-start(bf16[1,128,8,256]{3,2,1,0:T(8,128)(2,1)} %param.7) | copy-start | bytes 1572868
  41.1 3.6 %copy-start.12 = (bf16[1,128,1152]{2,1,0:T(8,128)(2,1)S(1)}, bf16[1,128,1152]{2,1,0:T(8,128)(2,1)}, u32[]{:S(2)}) copy-start(bf16[1,128,1152]{2,1,0:T(8,128)(2,1)} %param.13) | copy-start | bytes 884740
  43.9 0.8 copy-start.5
  49.1 20.7 %copy-start.6 = (bf16[8,128,256]{2,1,0:T(8,128)(2,1)S(1)}, bf16[8,128,256]{2,1,0:T(8,128)(2,1)}, u32[]{:S(2)}) copy-start(bf16[8,128,256]{2,1,0:T(8,128)(2,1)} %copy-done.5) | copy-start | bytes 1572868
  62.0 26.4 %all-to-all-start.1 = ((bf16[64,40,128]{2,1,0:T(8,128)(2,1)}), bf16[64,40,128]{2,1,0:T(8,128)(2,1)S(1)}, u32[]{:S(2)}, u32[]{:S(2)}) async-start(bf16[64,40,128]{2,1,0:T(8,128)(2,1)} %sum_shares.1), calls=%async_computation.1 | async-start | bytes 1310720 | tf_op jit(solution)/shard_map/all_to_all | solution.py:356
  67.9 10.7 %collective-permute-start.2 = (bf16[8,128,256]{2,1,0:T(8,128)(2,1)}, bf16[8,128,256]{2,1,0:T(8,128)(2,1)S(1)}, u32[]{:S(2)}, u32[]{:S(2)}) collective-permute-start(bf16[8,128,256]{2,1,0:T(8,128)(2,1)} %forward.1), channel_id=1, source_target_pairs={{0,64},{64,128},{128,192},{192,256},{256,320},{320,384},{384,448},... | collective-permute-start | bytes 1572872 | tf_op jit(solution)/shard_map/ppermute | solution.py:339
  69.8 10.3 %collective-permute-start.3 = (bf16[8,128,256]{2,1,0:T(8,128)(2,1)S(1)}, bf16[8,128,256]{2,1,0:T(8,128)(2,1)S(1)}, u32[]{:S(2)}, u32[]{:S(2)}) collective-permute-start(bf16[8,128,256]{2,1,0:T(8,128)(2,1)S(1)} %copy-done.6), channel_id=1, source_target_pairs={{64,0},{128,64},{192,128},{256,192},{320,256},{384,320},{448,384},... | collective-permute-start | bytes 1572872 | tf_op jit(solution)/shard_map/ppermute | solution.py:347

commit v3 on v2

--- a/solution.py
+++ b/solution.py
@@ -85,41 +85,37 @@
 
 
 def inner_kernel(
-    bwd_hbm, grad_hbm, use_hbm, table_hbm, first_hbm, second_hbm,
+    top_ref, bwd_ref, grad_ref, use_ref, table_ref, first_ref, second_ref,
     gh_out_ref, near_ref, sum_ref, fric_ref, flip_ref,
-    bwd_ref, grad_ref, use_ref, table_ref, first_ref, second_ref,
-    wide_b_ref, wide_g_ref, actb_ref, gh_ref, class_ref, sems,
+    wide_b_ref, wide_g_ref, actb_ref, gh_ref, class_ref,
 ):
-    copies = fetch(
-        sems, (second_hbm, second_ref), (bwd_hbm, bwd_ref), (grad_hbm, grad_ref),
-        (use_hbm, use_ref), (table_hbm, table_ref), (first_hbm, first_ref),
-    )
     for ref in (actb_ref, gh_ref):
-        for r in (0, 1, 8, 9):
+        for r in (0, 8, 9):
             ref[r] = jnp.zeros((CH, COLS), BF16)
-    copies[0].wait()
     put_flipped(flip_ref, second_ref)
     for i, (ref, wide_ref) in enumerate(((bwd_ref, wide_b_ref), (grad_ref, wide_g_ref))):
-        copies[1 + i].wait()
         rows = jnp.swapaxes(ref[...], 0, 1)
+        wide_ref[0] = jnp.zeros((WIDE, COLS), BF16)
         for r in range(LOCAL):
-            put_shifted(wide_ref, r, rows[r])
+            put_shifted(wide_ref, r + 1, rows[r])
         for k, r in enumerate((0, 1, LOCAL - 2, LOCAL - 1)):
             near_ref[i, k] = rows[r]
-    copies[3].wait()
-    copies[4].wait()
     class_ref[...] = use_ref[1].astype(F32) + 1.0
     terms = friction_terms(table_ref[...])
-    for k, r in enumerate((0, LOCAL - 1)):
-        fric_ref[k] = friction_row(terms, class_ref[r : r + 1])
-    copies[5].wait()
+    fric_ref[...] = friction_row(terms, class_ref[LOCAL - 1 : LOCAL])
+    active, gh = backward_row(
+        first_ref[...], flip_ref[...], friction_row(terms, class_ref[0:1] * top_ref[0]),
+        three_rows(wide_b_ref, 0), three_rows(wide_g_ref, 0),
+    )
+    actb_ref[1] = active
+    gh_ref[1] = gh
 
     def step(n, carry):
         for k in range(3):
             r = 3 * n + k + 1
             active, gh = backward_row(
                 first_ref[...], flip_ref[...], friction_row(terms, class_ref[pl.ds(r, 1)]),
-                three_rows(wide_b_ref, r - 1), three_rows(wide_g_ref, r - 1),
+                three_rows(wide_b_ref, r), three_rows(wide_g_ref, r),
             )
             actb_ref[r + 1] = active
             gh_ref[r + 1] = gh
@@ -129,32 +125,30 @@
     lax.fori_loop(0, 2, step, 0)
     total = None
     for r in range(LOCAL):
-        part = dot_cells(three_rows(gh_ref, r), wide_b_ref[r])
+        part = dot_cells(three_rows(gh_ref, r), wide_b_ref[r + 1])
         total = part if total is None else total + part
     sum_ref[0] = total
     total = None
     for r in range(LOCAL):
-        part = dot_cells(wide_g_ref[r], three_rows(actb_ref, r))
+        part = dot_cells(wide_g_ref[r + 1], three_rows(actb_ref, r))
         total = part if total is None else total + part
     sum_ref[1] = total
 
 
 def outer_kernel(
-    first_hbm, near_ref, above_ref, below_ref, fric_ref, flip_ref, sum_ref,
+    table_ref, first_ref, near_ref, below_ref, fric_ref, flip_ref, sum_ref,
     gh_out_ref, gw_ref,
-    first_ref, wide_ref, sems,
+    wide_ref,
 ):
-    (copy,) = fetch(sems, (first_hbm, first_ref))
     for i in range(2):
-        put_shifted(wide_ref.at[i], 0, above_ref[(2 * i + 1) * CH : (2 * i + 2) * CH])
-        for k in range(4):
-            put_shifted(wide_ref.at[i], 1 + k, near_ref[i, k])
-        put_shifted(wide_ref.at[i], 5, below_ref[2 * i * CH : (2 * i + 1) * CH])
-    copy.wait()
+        for k in range(2):
+            put_shifted(wide_ref.at[i], k, near_ref[i, 2 + k])
+            put_shifted(wide_ref.at[i], 2 + k, below_ref[(2 * i + k) * CH : (2 * i + k + 1) * CH])
+    last = friction_row(friction_terms(table_ref[...]), below_ref[6 * CH :].astype(F32)[1:2])
     first_part = second_part = None
-    for k in range(2):
-        stored_rows, grad_rows = three_rows(wide_ref.at[0], 3 * k), three_rows(wide_ref.at[1], 3 * k)
-        active, gh = backward_row(first_ref[...], flip_ref[...], fric_ref[k], stored_rows, grad_rows)
+    for k, fric in enumerate((fric_ref[...], last)):
+        stored_rows, grad_rows = three_rows(wide_ref.at[0], k), three_rows(wide_ref.at[1], k)
+        active, gh = backward_row(first_ref[...], flip_ref[...], fric, stored_rows, grad_rows)
         gh_out_ref[k] = gh
         one, two = dot_cells(gh, stored_rows), dot_cells(grad_rows, active)
         first_part = one if first_part is None else first_part + one
@@ -175,27 +169,19 @@
 
 
 def forward_kernel(
-    fwd_hbm, use_hbm, table_hbm, first_hbm, second_hbm, above_ref, below_ref,
+    fwd_ref, use_ref, table_ref, first_ref, second_ref, above_ref, below_ref,
     out_ref,
-    fwd_ref, use_ref, table_ref, first_ref, second_ref,
-    rows_ref, wide_ref, wide_act_ref, class_ref, sems,
+    rows_ref, wide_ref, wide_act_ref, class_ref,
 ):
-    copies = fetch(
-        sems, (fwd_hbm, fwd_ref), (use_hbm, use_ref), (table_hbm, table_ref),
-        (first_hbm, first_ref), (second_hbm, second_ref),
-    )
     class_ref[0:1] = above_ref[6 * CH :].astype(F32)[0:1]
     class_ref[9:10] = below_ref[6 * CH :].astype(F32)[0:1]
     for k in range(2):
         put_shifted(wide_ref, k, above_ref[(4 + k) * CH : (5 + k) * CH])
         put_shifted(wide_ref, 10 + k, below_ref[(4 + k) * CH : (5 + k) * CH])
-    copies[0].wait()
     rows = jnp.swapaxes(fwd_ref[...], 0, 1)
     rows_ref[...] = rows
     for r in range(LOCAL):
         put_shifted(wide_ref, 2 + r, rows[r])
-    for copy in copies[1:]:
-        copy.wait()
     class_ref[1:9] = use_ref[0].astype(F32) + 1.0
     terms = friction_terms(table_ref[...])
 
@@ -220,32 +206,26 @@
 
 
 def grad_x_kernel(
-    grad_hbm, first_hbm, table_hbm, inner_ref, outer_ref, near_ref, above_ref, below_ref, flip2_ref,
+    use_ref, grad_ref, first_ref, table_ref, inner_ref, outer_ref, near_ref, above_ref, flip2_ref,
     gx_ref,
-    grad_ref, first_ref, table_ref, rows_ref, wide_ref, beside_ref, flip_ref, sems,
+    rows_ref, wide_ref, beside_ref, flip_ref,
 ):
-    copies = fetch(sems, (first_hbm, first_ref), (table_hbm, table_ref), (grad_hbm, grad_ref))
     for i in range(2):
         for k in range(2):
             put_shifted(beside_ref.at[i], k, above_ref[(2 * i + k) * CH : (2 * i + k + 1) * CH])
-            put_shifted(beside_ref.at[i], 4 + k, below_ref[(2 * i + k) * CH : (2 * i + k + 1) * CH])
-        put_shifted(beside_ref.at[i], 2, near_ref[i, 0])
-        put_shifted(beside_ref.at[i], 3, near_ref[i, 3])
-    put_shifted(wide_ref, 1, outer_ref[0])
+            put_shifted(beside_ref.at[i], 2 + k, near_ref[i, k])
     for r in range(LOCAL - 2):
         put_shifted(wide_ref, 2 + r, inner_ref[r])
-    put_shifted(wide_ref, 8, outer_ref[1])
-    for copy in copies[:2]:
-        copy.wait()
+    for k in range(2):
+        put_shifted(wide_ref, 8 + k, outer_ref[k])
     put_flipped(flip_ref, first_ref)
     terms = friction_terms(table_ref[...])
-    for k, ref in enumerate((above_ref, below_ref)):
+    for k, classes in enumerate((above_ref[6 * CH :].astype(F32)[1:2], use_ref[1, 0:1].astype(F32) + 1.0)):
         _, gh = backward_row(
-            first_ref[...], flip2_ref[...], friction_row(terms, ref[6 * CH :].astype(F32)[1:2]),
-            three_rows(beside_ref.at[0], 3 * k), three_rows(beside_ref.at[1], 3 * k),
+            first_ref[...], flip2_ref[...], friction_row(terms, classes),
+            three_rows(beside_ref.at[0], k), three_rows(beside_ref.at[1], k),
         )
-        put_shifted(wide_ref, 9 * k, gh)
-    copies[2].wait()
+        put_shifted(wide_ref, k, gh)
     rows_ref[...] = jnp.swapaxes(grad_ref[...], 0, 1)
 
     def result_rows(step, carry):
@@ -279,20 +259,21 @@
             second_ref[:, to : to + CH] = flat_ref[at : at + CH].astype(F32)
 
 
-def kernel_call(kernel, outs, scratch, name, flops, hbm, vmem, limit=24):
+def kernel_call(kernel, outs, scratch, name, flops, hbm, vmem, limit=24, smem=()):
     outs = [jax.ShapeDtypeStruct(dims, kind) for dims, kind in outs]
     scratch = [(x.shape, x.dtype) for x in hbm] + scratch
     sems = [pltpu.SemaphoreType.DMA((len(hbm),))] if hbm else []
     size = sum(x.size * x.dtype.itemsize for x in [*hbm, *vmem, *outs])
+    spaces = [pltpu.SMEM] * len(smem) + [pltpu.HBM] * len(hbm) + [pltpu.VMEM] * len(vmem)
     return pl.pallas_call(
         kernel,
-        in_specs=[pl.BlockSpec(memory_space=pltpu.HBM)] * len(hbm) + [pl.BlockSpec(memory_space=pltpu.VMEM)] * len(vmem),
+        in_specs=[pl.BlockSpec(memory_space=space) for space in spaces],
         out_shape=outs,
         scratch_shapes=[pltpu.VMEM(dims, kind) for dims, kind in scratch] + sems,
         cost_estimate=pl.CostEstimate(flops=flops, bytes_accessed=size, transcendentals=0),
         compiler_params=pltpu.CompilerParams(vmem_limit_bytes=limit * 1024 * 1024),
         name=name,
-    )(*hbm, *vmem)
+    )(*smem, *hbm, *vmem)
 
 
 def body(fwd_in, bwd_in, grad_in, land_use, friction, weight_in, weight_out):
@@ -311,38 +292,40 @@
     head, tail = kernel_call(
         edges_kernel, [((6 * CH + 16, COLS), BF16)] * 2, [], "edges", 0, [bwd, grad, fwd, use], [], 56
     )
-    above, below = lax.ppermute(tail, "rows", down), lax.ppermute(head, "rows", up)
+    below, above = lax.ppermute(head, "rows", up), lax.ppermute(tail, "rows", down)
+    top = (lax.axis_index("rows") == 0).astype(F32).reshape(1)
     gh_inner, near, sums, fric, flip = kernel_call(
         inner_kernel,
-        [((LOCAL - 2, *row), BF16), ((2, 4, *row), BF16), ((2, WIDE, WIDE), F32), ((2, *row), F32), (weight, BF16)],
-        [((LOCAL, *wide), BF16)] * 2 + [((10, *row), BF16)] * 2 + [((LOCAL, COLS), F32)],
-        "inner", 28 * row_flops,
-        [bwd, grad, use, table, first, second], [],
+        [((LOCAL - 2, *row), BF16), ((2, 4, *row), BF16), ((2, WIDE, WIDE), F32), (row, F32), (weight, BF16)],
+        [((LOCAL + 1, *wide), BF16)] * 2 + [((10, *row), BF16)] * 2 + [((LOCAL, COLS), F32)],
+        "inner", 30 * row_flops,
+        [], [bwd, grad, use, table, first, second], smem=[top],
     )
     gh_outer, partial = kernel_call(
         outer_kernel,
         [((2, *row), BF16), ((row_count * share, CH), BF16)],
-        [((2, 6, *wide), BF16)],
+        [((2, 4, *wide), BF16)],
         "outer", 8 * row_flops,
-        [first], [near, above, below, fric, flip, sums],
-    )
+        [], [table, first, near, below, fric, flip, sums],
+    )
+    partial, above = lax.optimization_barrier((partial, above))
     shares = lax.all_to_all(partial.reshape(row_count, share, CH), "rows", 0, 0)
 
-    above, below, gh_outer = lax.optimization_barrier((above, below, gh_outer))
+    fwd, gh_outer = lax.optimization_barrier((fwd, gh_outer))
     (result,) = kernel_call(
         forward_kernel,
         [((LOCAL, *row), BF16)],
         [((LOCAL, *row), BF16), ((12, *wide), BF16), ((10, *wide), BF16), ((16, COLS), F32)],
         "forward", 18 * row_flops,
-        [fwd, use, table, first, second], [above, below],
+        [], [fwd, use, table, first, second, above, below],
     )
     handed_act = lax.ppermute(result, "pipe", [(i, i + 1) for i in range(sections - 1)])
     (grad_x,) = kernel_call(
         grad_x_kernel,
         [((LOCAL, *row), BF16)],
-        [((LOCAL, *row), BF16), ((10, *wide), BF16), ((2, 6, *wide), BF16), (weight, BF16)],
+        [((LOCAL, *row), BF16), ((10, *wide), BF16), ((2, 4, *wide), BF16), (weight, BF16)],
         "grad_x", 12 * row_flops,
-        [grad, first, table], [gh_inner, gh_outer, near, above, below, flip],
+        [], [use, grad, first, table, gh_inner, gh_outer, near, above, flip],
     )
     handed_grad = lax.ppermute(grad_x, "pipe", [(i + 1, i) for i in range(sections - 1)])
     handed_act, handed_grad = kernel_call(

time: 90.3 us -> 87.9 us (0.973)
  starting transfers between devices: 33 us -> 36.6 us
  waiting for transfers between devices: 32 us -> 29.3 us
  Pallas kernels: 19.4 us -> 17.5 us
  local copies, waits for them, and re-layouts: 4.18 us -> 2.99 us
    all_to_all x1, starting transfers between devices: 16 us -> 19.1 us  [body(): shares = lax.all_to_all(partial.reshape(row_count, share, CH), 'rows', 0, 0)]
    ppermute x1, waiting for transfers between devices: 4.65 us -> 2.13 us  [body(): lax.ppermute(head, 'rows', up)]
    pallas_call x8, Pallas kernels: 19.4 us -> 17.5 us  [kernel_call(): pl.pallas_call(kernel, in_specs=[pl.BlockSpec(memory_space=space) for spa...]
    ppermute x1, waiting for transfers between devices: 1.63 us -> 0.01 us  [body(): lax.ppermute(tail, 'rows', down)]
    all_to_all x1, waiting for transfers between devices: 11.9 us -> 13.3 us  [body(): shares = lax.all_to_all(partial.reshape(row_count, share, CH), 'rows', 0, 0)]
    unnamed x26, local copies, waits for them, and re-layouts: 4.18 us -> 2.99 us
  transfers between devices with their start and end apart: 6 -> 6, of which waited for: 6 -> 5; matrix products, arithmetic and copies ran while one was open for 0% -> 0% of each run, Pallas kernels for 15% -> 15%
where the time goes in v3:
time: 87.9 us; the launch traced here: 87.2 us
  starting transfers between devices  36.6 us (42%)
  waiting for transfers between devices  29.3 us (33%)
  Pallas kernels  17.5 us (20%)
  local copies, waits for them, and re-layouts  2.99 us (3%)
    all_to_all x1, starting transfers between devices, body(): shares = lax.all_to_all(partial.reshape(row_count, share, CH), 'rows', 0, 0)  19.1 us
    pallas_call x8, Pallas kernels, kernel_call(): pl.pallas_call(kernel, in_specs=[pl.BlockSpec(memory_space=space) for spa...  17.5 us
    all_to_all x1, waiting for transfers between devices, body(): shares = lax.all_to_all(partial.reshape(row_count, share, CH), 'rows', 0, 0)  13.3 us
    all_to_all x1, waiting for transfers between devices, body(): lax.all_to_all(summed, 'rows', 0, 0).reshape(row_count * share, CH)  7.16 us
    all_to_all x1, starting transfers between devices, body(): lax.all_to_all(summed, 'rows', 0, 0).reshape(row_count * share, CH)  5.74 us
    ppermute x1, starting transfers between devices, body(): lax.ppermute(tail, 'rows', down)  4.93 us
    ppermute x1, waiting for transfers between devices, body(): lax.ppermute(result, 'pipe', [(i, i + 1) for i in range(sections - 1)])  4.92 us
    ppermute x1, starting transfers between devices, body(): lax.ppermute(grad_x, 'pipe', [(i + 1, i) for i in range(sections - 1)])  3.64 us
  transfers between devices with their start and end apart: 6, of which 5 were waited for; matrix products, arithmetic and copies ran while one was open for 0% of the time, Pallas kernels for 15%

profile of v3, /device:TPU:6, one launch (start us, length us, event | category | flops | bytes accessed | tf_op | source)
XLA Modules:
  0.0 87.2 jit_solution(10955103675511573057)
XLA Ops:
  0.6 0.0 copy-start.4
  0.6 0.0 copy-start.1
  0.7 0.0 copy-start
  0.7 0.0 copy-start.3
  0.7 0.0 copy-start.5
  0.7 2.5 %edges.1 = (bf16[784,256]{1,0:T(8,128)(2,1)}, bf16[784,256]{1,0:T(8,128)(2,1)}) custom-call(bf16[128,8,256]{2,1,0:T(8,128)(2,1)} %bitcast.17, bf16[128,8,256]{2,1,0:T(8,128)(2,1)} %bitcast.19, bf16[128,8,256]{2,1,0:T(8,128)(2,1)} %bitcast.22, s32[2,8,256]{2,1,0:T(8,128)} %bitcast.28), custom_call_target="tpu_custom_call" | custom-call | bytes 2392064 | tf_op jit(solution)/shard_map/edges/pallas_call | solution.py:268
  3.2 1.3 %collective-permute-start = (bf16[784,256]{1,0:T(8,128)(2,1)}, bf16[784,256]{1,0:T(8,128)(2,1)S(1)}, u32[]{:S(2)}, u32[]{:S(2)}) collective-permute-start(bf16[784,256]{1,0:T(8,128)(2,1)} %get-tuple-element.23), channel_id=1, source_target_pairs={{1,0},{2,1},{3,2},{4,3},{5,4},{6,5},{7,6},{8,7},{9,8},{10,9},{11,1... | collective-permute-start | bytes 1204232 | tf_op jit(solution)/shard_map/ppermute | solution.py:295
  4.5 4.9 %collective-permute-start.1 = (bf16[784,256]{1,0:T(8,128)(2,1)}, bf16[784,256]{1,0:T(8,128)(2,1)S(1)}, u32[]{:S(2)}, u32[]{:S(2)}) collective-permute-start(bf16[784,256]{1,0:T(8,128)(2,1)} %get-tuple-element.30), channel_id=1, source_target_pairs={{0,1},{1,2},{2,3},{3,4},{4,5},{5,6},{6,7},{7,8},{8,9},{9,10},{10,1... | collective-permute-start | bytes 1204232 | tf_op jit(solution)/shard_map/ppermute | solution.py:295
  9.4 0.0 copy-done.4
  9.4 0.0 copy-done.1
  9.4 0.0 copy-done
  9.4 0.0 copy-done.3
  9.5 0.0 copy-done.5
  9.5 0.0 copy-start.9
  9.5 1.0 %copy-done.9 = bf16[1,128,1152]{2,1,0:T(8,128)(2,1)S(1)} copy-done((bf16[1,128,1152]{2,1,0:T(8,128)(2,1)S(1)}, bf16[1,128,1152]{2,1,0:T(8,128)(2,1)}, u32[]{:S(2)}) %copy-start.9) | copy-done | bytes 294936
  10.4 4.4 %inner.1 = (bf16[6,128,256]{2,1,0:T(8,128)(2,1)S(1)}, bf16[2,4,128,256]{3,2,1,0:T(8,128)(2,1)S(1)}, f32[2,384,384]{2,1,0:T(8,128)S(1)}, f32[128,256]{1,0:T(8,128)S(1)}, bf16[128,1152]{1,0:T(8,128)(2,1)S(1)}) custom-call(f32[1]{0:T(128)} %bitcast.4.top_ref, bf16[128,8,256]{2,1,0:T(8,128)(2,1)S(1)} %bitcast.18, bf16[128,8,256]{2,1,0:T(8,128)(2,1)S(1)} %bitcast.20, ...), custom_call_target="tpu_custom_call" | custom-call | flops 2264924160 | bytes 4182016 | tf_op jit(solution)/shard_map/inner/pallas_call | solution.py:268
  14.8 0.0 copy-start.11
  14.8 2.1 %collective-permute-done.below_ref = bf16[784,256]{1,0:T(8,128)(2,1)S(1)} collective-permute-done((bf16[784,256]{1,0:T(8,128)(2,1)}, bf16[784,256]{1,0:T(8,128)(2,1)S(1)}, u32[]{:S(2)}, u32[]{:S(2)}) %collective-permute-start) | collective-permute-done | bytes 401440 | tf_op jit(solution)/shard_map/ppermute | solution.py:295
  16.9 2.3 %outer.1 = (bf16[2,128,256]{2,1,0:T(8,128)(2,1)S(1)}, bf16[2560,128]{1,0:T(8,128)(2,1)}) custom-call(f32[8,128]{1,0:T(8,128)S(1)} %bitcast.33, bf16[128,1152]{1,0:T(8,128)(2,1)S(1)} %bitcast.25, bf16[2,4,128,256]{3,2,1,0:T(8,128)(2,1)S(1)} %get-tuple-element.22.near_ref, bf16[784,256]{1,0:T(8,128)(2,1)S(1)} %collective-permute-done.below_ref, ...), custom_call_target="tpu_custom_call" | custom-call | flops 603979776 | bytes 3616768 | tf_op jit(solution)/shard_map/outer/pallas_call | solution.py:268
  19.2 0.0 copy-done.11
  19.2 0.0 collective-permute-done.1.above_ref
  19.2 0.0 copy-start.6
  19.2 19.1 %all-to-all-start = ((bf16[64,40,128]{2,1,0:T(8,128)(2,1)}), bf16[64,40,128]{2,1,0:T(8,128)(2,1)S(1)}, u32[]{:S(2)}, u32[]{:S(2)}) async-start(bf16[64,40,128]{2,1,0:T(8,128)(2,1)} %bitcast.12), calls=%async_computation | async-start | bytes 1310720 | tf_op jit(solution)/shard_map/all_to_all | solution.py:312
  38.3 0.0 copy-done.6
  38.3 0.0 copy-start.7
  38.3 1.0 %copy-done.7 = bf16[784,256]{1,0:T(8,128)(2,1)S(1)} copy-done((bf16[784,256]{1,0:T(8,128)(2,1)S(1)}, bf16[784,256]{1,0:T(8,128)(2,1)}, u32[]{:S(2)}) %copy-start.7) | copy-done | bytes 401432
  39.3 0.0 copy-start.12
  39.3 1.0 %copy-done.12 = bf16[6,128,256]{2,1,0:T(8,128)(2,1)S(1)} copy-done((bf16[6,128,256]{2,1,0:T(8,128)(2,1)S(1)}, bf16[6,128,256]{2,1,0:T(8,128)(2,1)}, u32[]{:S(2)}) %copy-start.12) | copy-done | bytes 393240
  40.3 0.0 copy-start.2
  40.3 0.0 copy-start.8
  40.3 0.0 copy-start.10
  40.3 2.0 %grad_x.1 = bf16[8,128,256]{2,1,0:T(8,128)(2,1)S(1)} custom-call(s32[2,8,256]{2,1,0:T(8,128)S(1)} %bitcast.30, bf16[128,8,256]{2,1,0:T(8,128)(2,1)S(1)} %bitcast.21, bf16[128,1152]{1,0:T(8,128)(2,1)S(1)} %bitcast.26, f32[8,128]{1,0:T(8,128)S(1)} %bitcast.34, bf16[6,128,256]{2,1,0:T(8,128)(2,1)S(1)} %copy-done.12, ...), custom_call_target="tpu_custom_call" | custom-call | flops 905969664 | bytes 3108864 | tf_op jit(solution)/shard_map/grad_x/pallas_call | solution.py:268
  42.4 0.0 copy-done.2
  42.4 0.0 copy-done.8
  42.4 0.0 copy-done.10
  42.4 3.2 %forward.1 = bf16[8,128,256]{2,1,0:T(8,128)(2,1)S(1)} custom-call(bf16[128,8,256]{2,1,0:T(8,128)(2,1)S(1)} %bitcast.23, s32[2,8,256]{2,1,0:T(8,128)S(1)} %bitcast.31, f32[8,128]{1,0:T(8,128)S(1)} %bitcast.35, bf16[128,1152]{1,0:T(8,128)(2,1)S(1)} %bitcast.27, bf16[128,1152]{1,0:T(8,128)(2,1)S(1)} %bitcast.37, bf16[784,256]{1,0:T(8,128)(2,1)S(1)} %copy-done.8, ...), custom_call_target="tpu_custom_call" | custom-call | flops 1358954496 | bytes 2461696 | tf_op jit(solution)/shard_map/forward/pallas_call | solution.py:268
  45.6 13.3 %all-to-all-done.refs_0_ = bf16[64,40,128]{2,1,0:T(8,128)(2,1)S(1)} async-done(((bf16[64,40,128]{2,1,0:T(8,128)(2,1)}), bf16[64,40,128]{2,1,0:T(8,128)(2,1)S(1)}, u32[]{:S(2)}, u32[]{:S(2)}) %all-to-all-start) | async-done | bytes 655392 | tf_op jit(solution)/shard_map/all_to_all | solution.py:312
  58.9 1.0 %sum_shares.1 = bf16[64,40,128]{2,1,0:T(8,128)(2,1)} custom-call(bf16[64,40,128]{2,1,0:T(8,128)(2,1)S(1)} %all-to-all-done.refs_0_), custom_call_target="tpu_custom_call" | custom-call | bytes 1310720 | tf_op jit(solution)/shard_map/sum_shares/pallas_call | solution.py:268
  59.9 5.7 %all-to-all-start.1 = ((bf16[64,40,128]{2,1,0:T(8,128)(2,1)}), bf16[64,40,128]{2,1,0:T(8,128)(2,1)S(1)}, u32[]{:S(2)}, u32[]{:S(2)}) async-start(bf16[64,40,128]{2,1,0:T(8,128)(2,1)} %sum_shares.1), calls=%async_computation.1 | async-start | bytes 1310720 | tf_op jit(solution)/shard_map/all_to_all | solution.py:339
  65.6 1.9 %collective-permute-start.2 = (bf16[8,128,256]{2,1,0:T(8,128)(2,1)S(1)}, bf16[8,128,256]{2,1,0:T(8,128)(2,1)S(1)}, u32[]{:S(2)}, u32[]{:S(2)}) collective-permute-start(bf16[8,128,256]{2,1,0:T(8,128)(2,1)S(1)} %forward.1), channel_id=1, source_target_pairs={{0,64},{64,128},{128,192},{192,256},{256,320},{320,384},{384,448},... | collective-permute-start | bytes 1572872 | tf_op jit(solution)/shard_map/ppermute | solution.py:322
  67.6 3.6 %collective-permute-start.3 = (bf16[8,128,256]{2,1,0:T(8,128)(2,1)S(1)}, bf16[8,128,256]{2,1,0:T(8,128)(2,1)S(1)}, u32[]{:S(2)}, u32[]{:S(2)}) collective-permute-start(bf16[8,128,256]{2,1,0:T(8,128)(2,1)S(1)} %grad_x.1), channel_id=1, source_target_pairs={{64,0},{128,64},{192,128},{256,192},{320,256},{384,320},{448,384},... | collective-permute-start | bytes 1572872 | tf_op jit(solution)/shard_map/ppermute | solution.py:330
  71.2 4.9 %collective-permute-done.2.act_ref = bf16[8,128,256]{2,1,0:T(8,128)(2,1)S(1)} collective-permute-done((bf16[8,128,256]{2,1,0:T(8,128)(2,1)S(1)}, bf16[8,128,256]{2,1,0:T(8,128)(2,1)S(1)}, u32[]{:S(2)}, u32[]{:S(2)}) %collective-permute-start.2) | collective-permute-done | bytes 524320 | tf_op jit(solution)/shard_map/ppermute | solution.py:322
  76.1 1.8 %collective-permute-done.3.grad_ref = bf16[8,128,256]{2,1,0:T(8,128)(2,1)S(1)} collective-permute-done((bf16[8,128,256]{2,1,0:T(8,128)(2,1)S(1)}, bf16[8,128,256]{2,1,0:T(8,128)(2,1)S(1)}, u32[]{:S(2)}, u32[]{:S(2)}) %collective-permute-start.3) | collective-permute-done | bytes 524320 | tf_op jit(solution)/shard_map/ppermute | solution.py:330
  77.9 1.1 %turn.1 = (bf16[128,8,256]{2,1,0:T(8,128)(2,1)}, bf16[128,8,256]{2,1,0:T(8,128)(2,1)}) custom-call(bf16[8,128,256]{2,1,0:T(8,128)(2,1)S(1)} %collective-permute-done.2.act_ref, bf16[8,128,256]{2,1,0:T(8,128)(2,1)S(1)} %collective-permute-done.3.grad_ref), custom_call_target="tpu_custom_call" | custom-call | bytes 2097152 | tf_op jit(solution)/shard_map/turn/pallas_call | solution.py:268
  79.0 7.2 %all-to-all-done.1 = bf16[64,40,128]{2,1,0:T(8,128)(2,1)S(1)} async-done(((bf16[64,40,128]{2,1,0:T(8,128)(2,1)}), bf16[64,40,128]{2,1,0:T(8,128)(2,1)S(1)}, u32[]{:S(2)}, u32[]{:S(2)}) %all-to-all-start.1) | async-done | bytes 655392 | tf_op jit(solution)/shard_map/all_to_all | solution.py:339
  86.1 1.1 %spread.1 = (f32[128,1152]{1,0:T(8,128)}, f32[128,1152]{1,0:T(8,128)}) custom-call(bf16[2560,128]{1,0:T(8,128)(2,1)S(1)} %bitcast.16), custom_call_target="tpu_custom_call" | custom-call | bytes 1835008 | tf_op jit(solution)/shard_map/spread/pallas_call | solution.py:268
Async XLA Ops:
  0.6 8.8 %copy-start.4 = (s32[1,2,8,256]{3,2,1,0:T(8,128)S(1)}, s32[1,2,8,256]{3,2,1,0:T(8,128)}, u32[]{:S(2)}) copy-start(s32[1,2,8,256]{3,2,1,0:T(8,128)} %param.10) | copy-start | bytes 49156
  0.6 8.8 %copy-start.1 = (bf16[1,128,8,256]{3,2,1,0:T(8,128)(2,1)S(1)}, bf16[1,128,8,256]{3,2,1,0:T(8,128)(2,1)}, u32[]{:S(2)}) copy-start(bf16[1,128,8,256]{3,2,1,0:T(8,128)(2,1)} %param.9) | copy-start | bytes 1572868
  0.7 8.8 %copy-start = (bf16[1,128,8,256]{3,2,1,0:T(8,128)(2,1)S(1)}, bf16[1,128,8,256]{3,2,1,0:T(8,128)(2,1)}, u32[]{:S(2)}) copy-start(bf16[1,128,8,256]{3,2,1,0:T(8,128)(2,1)} %param.8) | copy-start | bytes 1572868
  0.7 8.8 %copy-start.3 = (bf16[1,128,1152]{2,1,0:T(8,128)(2,1)S(1)}, bf16[1,128,1152]{2,1,0:T(8,128)(2,1)}, u32[]{:S(2)}) copy-start(bf16[1,128,1152]{2,1,0:T(8,128)(2,1)} %param.12) | copy-start | bytes 884740
  0.7 8.8 %copy-start.5 = (f32[1,128,8]{1,2,0:T(8,128)S(1)}, f32[1,128,8]{1,2,0:T(8,128)}, u32[]{:S(2)}) copy-start(f32[1,128,8]{1,2,0:T(8,128)} %param.11) | copy-start | bytes 12292
  3.2 13.8 %collective-permute-start = (bf16[784,256]{1,0:T(8,128)(2,1)}, bf16[784,256]{1,0:T(8,128)(2,1)S(1)}, u32[]{:S(2)}, u32[]{:S(2)}) collective-permute-start(bf16[784,256]{1,0:T(8,128)(2,1)} %get-tuple-element.23), channel_id=1, source_target_pairs={{1,0},{2,1},{3,2},{4,3},{5,4},{6,5},{7,6},{8,7},{9,8},{10,9},{11,1... | collective-permute-start | bytes 1204232 | tf_op jit(solution)/shard_map/ppermute | solution.py:295
  4.5 14.7 %collective-permute-start.1 = (bf16[784,256]{1,0:T(8,128)(2,1)}, bf16[784,256]{1,0:T(8,128)(2,1)S(1)}, u32[]{:S(2)}, u32[]{:S(2)}) collective-permute-start(bf16[784,256]{1,0:T(8,128)(2,1)} %get-tuple-element.30), channel_id=1, source_target_pairs={{0,1},{1,2},{2,3},{3,4},{4,5},{5,6},{6,7},{7,8},{8,9},{9,10},{10,1... | collective-permute-start | bytes 1204232 | tf_op jit(solution)/shard_map/ppermute | solution.py:295
  9.5 1.0 %copy-start.9 = (bf16[1,128,1152]{2,1,0:T(8,128)(2,1)S(1)}, bf16[1,128,1152]{2,1,0:T(8,128)(2,1)}, u32[]{:S(2)}) copy-start(bf16[1,128,1152]{2,1,0:T(8,128)(2,1)} %param.13) | copy-start | bytes 884740
  14.8 4.4 %copy-start.11 = (bf16[6,128,256]{2,1,0:T(8,128)(2,1)}, bf16[6,128,256]{2,1,0:T(8,128)(2,1)S(1)}, u32[]{:S(2)}) copy-start(bf16[6,128,256]{2,1,0:T(8,128)(2,1)S(1)} %get-tuple-element.32.inner_ref) | copy-start | bytes 1179652
  19.2 19.1 %copy-start.6 = (bf16[784,256]{1,0:T(8,128)(2,1)}, bf16[784,256]{1,0:T(8,128)(2,1)S(1)}, u32[]{:S(2)}) copy-start(bf16[784,256]{1,0:T(8,128)(2,1)S(1)} %collective-permute-done.1.above_ref) | copy-start | bytes 1204228
  19.2 39.7 %all-to-all-start = ((bf16[64,40,128]{2,1,0:T(8,128)(2,1)}), bf16[64,40,128]{2,1,0:T(8,128)(2,1)S(1)}, u32[]{:S(2)}, u32[]{:S(2)}) async-start(bf16[64,40,128]{2,1,0:T(8,128)(2,1)} %bitcast.12), calls=%async_computation | async-start | bytes 1310720 | tf_op jit(solution)/shard_map/all_to_all | solution.py:312
  38.3 1.0 %copy-start.7 = (bf16[784,256]{1,0:T(8,128)(2,1)S(1)}, bf16[784,256]{1,0:T(8,128)(2,1)}, u32[]{:S(2)}) copy-start(bf16[784,256]{1,0:T(8,128)(2,1)} %copy-done.6) | copy-start | bytes 1204228
  39.3 1.0 %copy-start.12 = (bf16[6,128,256]{2,1,0:T(8,128)(2,1)S(1)}, bf16[6,128,256]{2,1,0:T(8,128)(2,1)}, u32[]{:S(2)}) copy-start(bf16[6,128,256]{2,1,0:T(8,128)(2,1)} %copy-done.11) | copy-start | bytes 1179652
  40.3 2.1 %copy-start.2 = (bf16[1,128,8,256]{3,2,1,0:T(8,128)(2,1)S(1)}, bf16[1,128,8,256]{3,2,1,0:T(8,128)(2,1)}, u32[]{:S(2)}) copy-start(bf16[1,128,8,256]{3,2,1,0:T(8,128)(2,1)} %param.7) | copy-start | bytes 1572868
  40.3 2.1 %copy-start.8 = (bf16[784,256]{1,0:T(8,128)(2,1)S(1)}, bf16[784,256]{1,0:T(8,128)(2,1)}, u32[]{:S(2)}) copy-start(bf16[784,256]{1,0:T(8,128)(2,1)} %copy-done.6) | copy-start | bytes 1204228
  40.3 2.1 %copy-start.10 = (bf16[1,128,1152]{2,1,0:T(8,128)(2,1)S(1)}, bf16[1,128,1152]{2,1,0:T(8,128)(2,1)}, u32[]{:S(2)}) copy-start(bf16[1,128,1152]{2,1,0:T(8,128)(2,1)} %param.13) | copy-start | bytes 884740
  59.9 26.3 %all-to-all-start.1 = ((bf16[64,40,128]{2,1,0:T(8,128)(2,1)}), bf16[64,40,128]{2,1,0:T(8,128)(2,1)S(1)}, u32[]{:S(2)}, u32[]{:S(2)}) async-start(bf16[64,40,128]{2,1,0:T(8,128)(2,1)} %sum_shares.1), calls=%async_computation.1 | async-start | bytes 1310720 | tf_op jit(solution)/shard_map/all_to_all | solution.py:339
  65.6 10.5 %collective-permute-start.2 = (bf16[8,128,256]{2,1,0:T(8,128)(2,1)S(1)}, bf16[8,128,256]{2,1,0:T(8,128)(2,1)S(1)}, u32[]{:S(2)}, u32[]{:S(2)}) collective-permute-start(bf16[8,128,256]{2,1,0:T(8,128)(2,1)S(1)} %forward.1), channel_id=1, source_target_pairs={{0,64},{64,128},{128,192},{192,256},{256,320},{320,384},{384,448},... | collective-permute-start | bytes 1572872 | tf_op jit(solution)/shard_map/ppermute | solution.py:322
  67.6 10.3 %collective-permute-start.3 = (bf16[8,128,256]{2,1,0:T(8,128)(2,1)S(1)}, bf16[8,128,256]{2,1,0:T(8,128)(2,1)S(1)}, u32[]{:S(2)}, u32[]{:S(2)}) collective-permute-start(bf16[8,128,256]{2,1,0:T(8,128)(2,1)S(1)} %grad_x.1), channel_id=1, source_target_pairs={{64,0},{128,64},{192,128},{256,192},{320,256},{384,320},{448,384},... | collective-permute-start | bytes 1572872 | tf_op jit(solution)/shard_map/ppermute | solution.py:330

commit v4 on v3

--- a/solution.py
+++ b/solution.py
@@ -163,9 +163,6 @@
             whole = sum_ref[1, a * CH : (a + 1) * CH, b * CH : (b + 1) * CH]
             whole = whole + second_part[(2 - b) * WIDE + a * CH : (2 - b) * WIDE + (a + 1) * CH]
             gw_ref[at : at + CH] = whole.astype(BF16)
-    spare = gw_ref.shape[0] - 2 * TAPS * CH
-    if spare:
-        gw_ref[2 * TAPS * CH :] = jnp.zeros((spare, CH), BF16)
 
 
 def forward_kernel(
@@ -244,8 +241,11 @@
 
 
 def sum_kernel(scale, parts_ref, out_ref):
+    share = out_ref.shape[1] // 2
     total = jnp.sum(parts_ref[...].astype(F32), axis=0) * scale
-    out_ref[...] = jnp.broadcast_to(total.astype(BF16)[None], out_ref.shape)
+    total = total[:share] + total[share:]
+    both = jnp.concatenate([total, total], axis=0).astype(BF16)
+    out_ref[...] = jnp.broadcast_to(both[None], out_ref.shape)
 
 
 def spread_kernel(flat_ref, first_ref, second_ref):
@@ -257,6 +257,11 @@
             at = (TAPS + a * 3 + b) * CH
             to = (b * 3 + 2 - a) * CH
             second_ref[:, to : to + CH] = flat_ref[at : at + CH].astype(F32)
+
+
+def spread_out(values):
+    count = lax.axis_size("rows")
+    return lax.all_to_all(values.reshape(count, -1, 2, CH), "rows", 0, 0).reshape(values.shape)
 
 
 def kernel_call(kernel, outs, scratch, name, flops, hbm, vmem, limit=24, smem=()):
@@ -282,7 +287,7 @@
     fwd, bwd, grad = fwd_in[0], bwd_in[0], grad_in[0]
     use, table, first, second = land_use[0], friction[0].T, weight_in[0], weight_out[0]
     scale = 1.0 / (LOCAL * row_count * COLS) ** 0.5
-    share = -(-2 * TAPS * CH // (8 * row_count)) * 8
+    share = 2 * TAPS * CH // row_count
     cells, weight = (CH, LOCAL, COLS), (CH, TAPS * CH)
     row, wide = (CH, COLS), (WIDE, COLS)
     row_flops = 2 * CH * TAPS * CH * COLS
@@ -309,7 +314,7 @@
         [], [table, first, near, below, fric, flip, sums],
     )
     partial, above = lax.optimization_barrier((partial, above))
-    shares = lax.all_to_all(partial.reshape(row_count, share, CH), "rows", 0, 0)
+    shares = spread_out(partial)
 
     fwd, gh_outer = lax.optimization_barrier((fwd, gh_outer))
     (result,) = kernel_call(
@@ -333,10 +338,11 @@
     )
     shares, result, grad_x = lax.optimization_barrier((shares, result, grad_x))
 
+    pairs = (row_count // 2, 2 * share, CH)
     (summed,) = kernel_call(
-        lambda *refs: sum_kernel(scale, *refs), [((row_count, share, CH), BF16)], [], "sum_shares", 0, [], [shares]
-    )
-    gathered = lax.all_to_all(summed, "rows", 0, 0).reshape(row_count * share, CH)
+        lambda *refs: sum_kernel(scale, *refs), [(pairs, BF16)], [], "sum_shares", 0, [], [shares.reshape(pairs)]
+    )
+    gathered = spread_out(summed.reshape(partial.shape))
     grad_first, grad_second = kernel_call(spread_kernel, [(weight, F32)] * 2, [], "spread", 0, [], [gathered])
     return (handed_act[None], handed_grad[None], grad_first[None], grad_second[None])
 

time: 87.9 us -> 84.9 us (0.966)
  waiting for transfers between devices: 29.3 us -> 26.7 us
    all_to_all x2, waiting for transfers between devices: 20.5 us -> 17.9 us  [spread_out(): lax.all_to_all(values.reshape(count, -1, 2, CH), 'rows', 0, 0)]
where the time goes in v4:
time: 84.9 us; the launch traced here: 84.3 us
  starting transfers between devices  36.3 us (43%)
  waiting for transfers between devices  26.7 us (31%)
  Pallas kernels  17.4 us (20%)
  local copies, waits for them, and re-layouts  2.99 us (4%)
  between operations  0.86 us (1%)
    all_to_all x2, starting transfers between devices, spread_out(): lax.all_to_all(values.reshape(count, -1, 2, CH), 'rows', 0, 0)  24.5 us
    all_to_all x2, waiting for transfers between devices, spread_out(): lax.all_to_all(values.reshape(count, -1, 2, CH), 'rows', 0, 0)  17.9 us
    pallas_call x8, Pallas kernels, kernel_call(): pl.pallas_call(kernel, in_specs=[pl.BlockSpec(memory_space=space) for spa...  17.4 us
    ppermute x1, starting transfers between devices, body(): lax.ppermute(tail, 'rows', down)  4.93 us
    ppermute x1, waiting for transfers between devices, body(): lax.ppermute(result, 'pipe', [(i, i + 1) for i in range(sections - 1)])  4.92 us
    ppermute x1, starting transfers between devices, body(): lax.ppermute(grad_x, 'pipe', [(i + 1, i) for i in range(sections - 1)])  3.64 us
    unnamed x26, local copies, waits for them, and re-layouts  2.99 us
    ppermute x1, waiting for transfers between devices, body(): lax.ppermute(head, 'rows', up)  2.12 us
  transfers between devices with their start and end apart: 6, of which 5 were waited for; matrix products, arithmetic and copies ran while one was open for 0% of the time, Pallas kernels for 15%

profile of v4, /device:TPU:6, one launch (start us, length us, event | category | flops | bytes accessed | tf_op | source)
XLA Modules:
  0.0 84.3 jit_solution(7638214621343553267)
XLA Ops:
  0.6 0.0 copy-start.4
  0.6 0.0 copy-start.1
  0.7 0.0 copy-start
  0.7 0.0 copy-start.3
  0.7 0.0 copy-start.5
  0.7 2.5 %edges.1 = (bf16[784,256]{1,0:T(8,128)(2,1)}, bf16[784,256]{1,0:T(8,128)(2,1)}) custom-call(bf16[128,8,256]{2,1,0:T(8,128)(2,1)} %bitcast.21, bf16[128,8,256]{2,1,0:T(8,128)(2,1)} %bitcast.23, bf16[128,8,256]{2,1,0:T(8,128)(2,1)} %bitcast.26, s32[2,8,256]{2,1,0:T(8,128)} %bitcast.32), custom_call_target="tpu_custom_call" | custom-call | bytes 2392064 | tf_op jit(solution)/shard_map/edges/pallas_call | solution.py:273
  3.2 1.3 %collective-permute-start = (bf16[784,256]{1,0:T(8,128)(2,1)}, bf16[784,256]{1,0:T(8,128)(2,1)S(1)}, u32[]{:S(2)}, u32[]{:S(2)}) collective-permute-start(bf16[784,256]{1,0:T(8,128)(2,1)} %get-tuple-element.23), channel_id=1, source_target_pairs={{1,0},{2,1},{3,2},{4,3},{5,4},{6,5},{7,6},{8,7},{9,8},{10,9},{11,1... | collective-permute-start | bytes 1204232 | tf_op jit(solution)/shard_map/ppermute | solution.py:300
  4.5 4.9 %collective-permute-start.1 = (bf16[784,256]{1,0:T(8,128)(2,1)}, bf16[784,256]{1,0:T(8,128)(2,1)S(1)}, u32[]{:S(2)}, u32[]{:S(2)}) collective-permute-start(bf16[784,256]{1,0:T(8,128)(2,1)} %get-tuple-element.30), channel_id=1, source_target_pairs={{0,1},{1,2},{2,3},{3,4},{4,5},{5,6},{6,7},{7,8},{8,9},{9,10},{10,1... | collective-permute-start | bytes 1204232 | tf_op jit(solution)/shard_map/ppermute | solution.py:300
  9.4 0.0 copy-done.4
  9.4 0.0 copy-done.1
  9.4 0.0 copy-done
  9.4 0.0 copy-done.3
  9.5 0.0 copy-done.5
  9.5 0.0 copy-start.9
  9.5 1.0 %copy-done.9 = bf16[1,128,1152]{2,1,0:T(8,128)(2,1)S(1)} copy-done((bf16[1,128,1152]{2,1,0:T(8,128)(2,1)S(1)}, bf16[1,128,1152]{2,1,0:T(8,128)(2,1)}, u32[]{:S(2)}) %copy-start.9) | copy-done | bytes 294936
  10.4 4.4 %inner.1 = (bf16[6,128,256]{2,1,0:T(8,128)(2,1)S(1)}, bf16[2,4,128,256]{3,2,1,0:T(8,128)(2,1)S(1)}, f32[2,384,384]{2,1,0:T(8,128)S(1)}, f32[128,256]{1,0:T(8,128)S(1)}, bf16[128,1152]{1,0:T(8,128)(2,1)S(1)}) custom-call(f32[1]{0:T(128)} %bitcast.4.top_ref, bf16[128,8,256]{2,1,0:T(8,128)(2,1)S(1)} %bitcast.22, bf16[128,8,256]{2,1,0:T(8,128)(2,1)S(1)} %bitcast.24, ...), custom_call_target="tpu_custom_call" | custom-call | flops 2264924160 | bytes 4182016 | tf_op jit(solution)/shard_map/inner/pallas_call | solution.py:273
  14.8 0.0 copy-start.11
  14.8 2.1 %collective-permute-done.below_ref = bf16[784,256]{1,0:T(8,128)(2,1)S(1)} collective-permute-done((bf16[784,256]{1,0:T(8,128)(2,1)}, bf16[784,256]{1,0:T(8,128)(2,1)S(1)}, u32[]{:S(2)}, u32[]{:S(2)}) %collective-permute-start) | collective-permute-done | bytes 401440 | tf_op jit(solution)/shard_map/ppermute | solution.py:300
  16.9 2.2 %outer.1 = (bf16[2,128,256]{2,1,0:T(8,128)(2,1)S(1)}, bf16[2304,128]{1,0:T(8,128)(2,1)}) custom-call(f32[8,128]{1,0:T(8,128)S(1)} %bitcast.37, bf16[128,1152]{1,0:T(8,128)(2,1)S(1)} %bitcast.29, bf16[2,4,128,256]{3,2,1,0:T(8,128)(2,1)S(1)} %get-tuple-element.22.near_ref, bf16[784,256]{1,0:T(8,128)(2,1)S(1)} %collective-permute-done.below_ref, ...), custom_call_target="tpu_custom_call" | custom-call | flops 603979776 | bytes 3551232 | tf_op jit(solution)/shard_map/outer/pallas_call | solution.py:273
  19.2 0.0 copy-done.11
  19.2 0.0 collective-permute-done.1.above_ref
  19.2 0.0 copy-start.6
  19.2 19.1 %all-to-all-start = ((bf16[64,18,2,128]{3,2,1,0:T(2,128)(2,1)}), bf16[64,18,2,128]{3,2,1,0:T(2,128)(2,1)S(1)}, u32[]{:S(2)}, u32[]{:S(2)}) async-start(bf16[64,18,2,128]{3,2,1,0:T(2,128)(2,1)} %bitcast.12), calls=%async_computation | async-start | bytes 1179648 | tf_op jit(solution)/shard_map/all_to_all | solution.py:264
  38.3 0.0 copy-done.6
  38.3 0.0 copy-start.7
  38.3 1.0 %copy-done.7 = bf16[784,256]{1,0:T(8,128)(2,1)S(1)} copy-done((bf16[784,256]{1,0:T(8,128)(2,1)S(1)}, bf16[784,256]{1,0:T(8,128)(2,1)}, u32[]{:S(2)}) %copy-start.7) | copy-done | bytes 401432
  39.3 0.0 copy-start.12
  39.3 1.0 %copy-done.12 = bf16[6,128,256]{2,1,0:T(8,128)(2,1)S(1)} copy-done((bf16[6,128,256]{2,1,0:T(8,128)(2,1)S(1)}, bf16[6,128,256]{2,1,0:T(8,128)(2,1)}, u32[]{:S(2)}) %copy-start.12) | copy-done | bytes 393240
  40.3 0.0 copy-start.2
  40.3 0.0 copy-start.8
  40.3 0.0 copy-start.10
  40.3 2.0 %grad_x.1 = bf16[8,128,256]{2,1,0:T(8,128)(2,1)S(1)} custom-call(s32[2,8,256]{2,1,0:T(8,128)S(1)} %bitcast.34, bf16[128,8,256]{2,1,0:T(8,128)(2,1)S(1)} %bitcast.25, bf16[128,1152]{1,0:T(8,128)(2,1)S(1)} %bitcast.30, f32[8,128]{1,0:T(8,128)S(1)} %bitcast.38, bf16[6,128,256]{2,1,0:T(8,128)(2,1)S(1)} %copy-done.12, ...), custom_call_target="tpu_custom_call" | custom-call | flops 905969664 | bytes 3108864 | tf_op jit(solution)/shard_map/grad_x/pallas_call | solution.py:273
  42.4 0.0 copy-done.2
  42.4 0.0 copy-done.8
  42.4 0.0 copy-done.10
  42.4 3.2 %forward.1 = bf16[8,128,256]{2,1,0:T(8,128)(2,1)S(1)} custom-call(bf16[128,8,256]{2,1,0:T(8,128)(2,1)S(1)} %bitcast.27, s32[2,8,256]{2,1,0:T(8,128)S(1)} %bitcast.35, f32[8,128]{1,0:T(8,128)S(1)} %bitcast.39, bf16[128,1152]{1,0:T(8,128)(2,1)S(1)} %bitcast.31, bf16[128,1152]{1,0:T(8,128)(2,1)S(1)} %bitcast.41, bf16[784,256]{1,0:T(8,128)(2,1)S(1)} %copy-done.8, ...), custom_call_target="tpu_custom_call" | custom-call | flops 1358954496 | bytes 2461696 | tf_op jit(solution)/shard_map/forward/pallas_call | solution.py:273
  45.6 12.2 %all-to-all-done = bf16[64,18,2,128]{3,2,1,0:T(2,128)(2,1)S(1)} async-done(((bf16[64,18,2,128]{3,2,1,0:T(2,128)(2,1)}), bf16[64,18,2,128]{3,2,1,0:T(2,128)(2,1)S(1)}, u32[]{:S(2)}, u32[]{:S(2)}) %all-to-all-start) | async-done | bytes 589856 | tf_op jit(solution)/shard_map/all_to_all | solution.py:264
  57.7 0.9 %sum_shares.1 = bf16[32,72,128]{2,1,0:T(8,128)(2,1)} custom-call(bf16[32,72,128]{2,1,0:T(8,128)(2,1)S(1)} %bitcast.20), custom_call_target="tpu_custom_call" | custom-call | bytes 1179648 | tf_op jit(solution)/shard_map/sum_shares/pallas_call | solution.py:273
  58.7 5.4 %all-to-all-start.1 = ((bf16[64,18,2,128]{3,2,1,0:T(2,128)(2,1)}), bf16[64,18,2,128]{3,2,1,0:T(2,128)(2,1)S(1)}, u32[]{:S(2)}, u32[]{:S(2)}) async-start(bf16[64,18,2,128]{3,2,1,0:T(2,128)(2,1)} %bitcast.15), calls=%async_computation.1 | async-start | bytes 1179648 | tf_op jit(solution)/shard_map/all_to_all | solution.py:264
  64.1 1.9 %collective-permute-start.2 = (bf16[8,128,256]{2,1,0:T(8,128)(2,1)S(1)}, bf16[8,128,256]{2,1,0:T(8,128)(2,1)S(1)}, u32[]{:S(2)}, u32[]{:S(2)}) collective-permute-start(bf16[8,128,256]{2,1,0:T(8,128)(2,1)S(1)} %forward.1), channel_id=1, source_target_pairs={{0,64},{64,128},{128,192},{192,256},{256,320},{320,384},{384,448},... | collective-permute-start | bytes 1572872 | tf_op jit(solution)/shard_map/ppermute | solution.py:327
  66.0 3.6 %collective-permute-start.3 = (bf16[8,128,256]{2,1,0:T(8,128)(2,1)S(1)}, bf16[8,128,256]{2,1,0:T(8,128)(2,1)S(1)}, u32[]{:S(2)}, u32[]{:S(2)}) collective-permute-start(bf16[8,128,256]{2,1,0:T(8,128)(2,1)S(1)} %grad_x.1), channel_id=1, source_target_pairs={{64,0},{128,64},{192,128},{256,192},{320,256},{384,320},{448,384},... | collective-permute-start | bytes 1572872 | tf_op jit(solution)/shard_map/ppermute | solution.py:335
  69.7 4.9 %collective-permute-done.2.act_ref = bf16[8,128,256]{2,1,0:T(8,128)(2,1)S(1)} collective-permute-done((bf16[8,128,256]{2,1,0:T(8,128)(2,1)S(1)}, bf16[8,128,256]{2,1,0:T(8,128)(2,1)S(1)}, u32[]{:S(2)}, u32[]{:S(2)}) %collective-permute-start.2) | collective-permute-done | bytes 524320 | tf_op jit(solution)/shard_map/ppermute | solution.py:327
  74.6 1.8 %collective-permute-done.3.grad_ref = bf16[8,128,256]{2,1,0:T(8,128)(2,1)S(1)} collective-permute-done((bf16[8,128,256]{2,1,0:T(8,128)(2,1)S(1)}, bf16[8,128,256]{2,1,0:T(8,128)(2,1)S(1)}, u32[]{:S(2)}, u32[]{:S(2)}) %collective-permute-start.3) | collective-permute-done | bytes 524320 | tf_op jit(solution)/shard_map/ppermute | solution.py:335
  76.4 1.1 %turn.1 = (bf16[128,8,256]{2,1,0:T(8,128)(2,1)}, bf16[128,8,256]{2,1,0:T(8,128)(2,1)}) custom-call(bf16[8,128,256]{2,1,0:T(8,128)(2,1)S(1)} %collective-permute-done.2.act_ref, bf16[8,128,256]{2,1,0:T(8,128)(2,1)S(1)} %collective-permute-done.3.grad_ref), custom_call_target="tpu_custom_call" | custom-call | bytes 2097152 | tf_op jit(solution)/shard_map/turn/pallas_call | solution.py:273
  77.5 5.7 %all-to-all-done.1 = bf16[64,18,2,128]{3,2,1,0:T(2,128)(2,1)S(1)} async-done(((bf16[64,18,2,128]{3,2,1,0:T(2,128)(2,1)}), bf16[64,18,2,128]{3,2,1,0:T(2,128)(2,1)S(1)}, u32[]{:S(2)}, u32[]{:S(2)}) %all-to-all-start.1) | async-done | bytes 589856 | tf_op jit(solution)/shard_map/all_to_all | solution.py:264
  83.2 1.1 %spread.1 = (f32[128,1152]{1,0:T(8,128)}, f32[128,1152]{1,0:T(8,128)}) custom-call(bf16[2304,128]{1,0:T(8,128)(2,1)S(1)} %bitcast.19), custom_call_target="tpu_custom_call" | custom-call | bytes 1769472 | tf_op jit(solution)/shard_map/spread/pallas_call | solution.py:273
Async XLA Ops:
  0.6 8.8 %copy-start.4 = (s32[1,2,8,256]{3,2,1,0:T(8,128)S(1)}, s32[1,2,8,256]{3,2,1,0:T(8,128)}, u32[]{:S(2)}) copy-start(s32[1,2,8,256]{3,2,1,0:T(8,128)} %param.10) | copy-start | bytes 49156
  0.6 8.8 %copy-start.1 = (bf16[1,128,8,256]{3,2,1,0:T(8,128)(2,1)S(1)}, bf16[1,128,8,256]{3,2,1,0:T(8,128)(2,1)}, u32[]{:S(2)}) copy-start(bf16[1,128,8,256]{3,2,1,0:T(8,128)(2,1)} %param.9) | copy-start | bytes 1572868
  0.7 8.8 %copy-start = (bf16[1,128,8,256]{3,2,1,0:T(8,128)(2,1)S(1)}, bf16[1,128,8,256]{3,2,1,0:T(8,128)(2,1)}, u32[]{:S(2)}) copy-start(bf16[1,128,8,256]{3,2,1,0:T(8,128)(2,1)} %param.8) | copy-start | bytes 1572868
  0.7 8.8 %copy-start.3 = (bf16[1,128,1152]{2,1,0:T(8,128)(2,1)S(1)}, bf16[1,128,1152]{2,1,0:T(8,128)(2,1)}, u32[]{:S(2)}) copy-start(bf16[1,128,1152]{2,1,0:T(8,128)(2,1)} %param.12) | copy-start | bytes 884740
  0.7 8.8 %copy-start.5 = (f32[1,128,8]{1,2,0:T(8,128)S(1)}, f32[1,128,8]{1,2,0:T(8,128)}, u32[]{:S(2)}) copy-start(f32[1,128,8]{1,2,0:T(8,128)} %param.11) | copy-start | bytes 12292
  3.2 13.8 %collective-permute-start = (bf16[784,256]{1,0:T(8,128)(2,1)}, bf16[784,256]{1,0:T(8,128)(2,1)S(1)}, u32[]{:S(2)}, u32[]{:S(2)}) collective-permute-start(bf16[784,256]{1,0:T(8,128)(2,1)} %get-tuple-element.23), channel_id=1, source_target_pairs={{1,0},{2,1},{3,2},{4,3},{5,4},{6,5},{7,6},{8,7},{9,8},{10,9},{11,1... | collective-permute-start | bytes 1204232 | tf_op jit(solution)/shard_map/ppermute | solution.py:300
  4.5 14.7 %collective-permute-start.1 = (bf16[784,256]{1,0:T(8,128)(2,1)}, bf16[784,256]{1,0:T(8,128)(2,1)S(1)}, u32[]{:S(2)}, u32[]{:S(2)}) collective-permute-start(bf16[784,256]{1,0:T(8,128)(2,1)} %get-tuple-element.30), channel_id=1, source_target_pairs={{0,1},{1,2},{2,3},{3,4},{4,5},{5,6},{6,7},{7,8},{8,9},{9,10},{10,1... | collective-permute-start | bytes 1204232 | tf_op jit(solution)/shard_map/ppermute | solution.py:300
  9.5 1.0 %copy-start.9 = (bf16[1,128,1152]{2,1,0:T(8,128)(2,1)S(1)}, bf16[1,128,1152]{2,1,0:T(8,128)(2,1)}, u32[]{:S(2)}) copy-start(bf16[1,128,1152]{2,1,0:T(8,128)(2,1)} %param.13) | copy-start | bytes 884740
  14.8 4.4 %copy-start.11 = (bf16[6,128,256]{2,1,0:T(8,128)(2,1)}, bf16[6,128,256]{2,1,0:T(8,128)(2,1)S(1)}, u32[]{:S(2)}) copy-start(bf16[6,128,256]{2,1,0:T(8,128)(2,1)S(1)} %get-tuple-element.32.inner_ref) | copy-start | bytes 1179652
  19.2 19.1 %copy-start.6 = (bf16[784,256]{1,0:T(8,128)(2,1)}, bf16[784,256]{1,0:T(8,128)(2,1)S(1)}, u32[]{:S(2)}) copy-start(bf16[784,256]{1,0:T(8,128)(2,1)S(1)} %collective-permute-done.1.above_ref) | copy-start | bytes 1204228
  19.2 38.6 %all-to-all-start = ((bf16[64,18,2,128]{3,2,1,0:T(2,128)(2,1)}), bf16[64,18,2,128]{3,2,1,0:T(2,128)(2,1)S(1)}, u32[]{:S(2)}, u32[]{:S(2)}) async-start(bf16[64,18,2,128]{3,2,1,0:T(2,128)(2,1)} %bitcast.12), calls=%async_computation | async-start | bytes 1179648 | tf_op jit(solution)/shard_map/all_to_all | solution.py:264
  38.3 1.0 %copy-start.7 = (bf16[784,256]{1,0:T(8,128)(2,1)S(1)}, bf16[784,256]{1,0:T(8,128)(2,1)}, u32[]{:S(2)}) copy-start(bf16[784,256]{1,0:T(8,128)(2,1)} %copy-done.6) | copy-start | bytes 1204228
  39.3 1.0 %copy-start.12 = (bf16[6,128,256]{2,1,0:T(8,128)(2,1)S(1)}, bf16[6,128,256]{2,1,0:T(8,128)(2,1)}, u32[]{:S(2)}) copy-start(bf16[6,128,256]{2,1,0:T(8,128)(2,1)} %copy-done.11) | copy-start | bytes 1179652
  40.3 2.1 %copy-start.2 = (bf16[1,128,8,256]{3,2,1,0:T(8,128)(2,1)S(1)}, bf16[1,128,8,256]{3,2,1,0:T(8,128)(2,1)}, u32[]{:S(2)}) copy-start(bf16[1,128,8,256]{3,2,1,0:T(8,128)(2,1)} %param.7) | copy-start | bytes 1572868
  40.3 2.1 %copy-start.8 = (bf16[784,256]{1,0:T(8,128)(2,1)S(1)}, bf16[784,256]{1,0:T(8,128)(2,1)}, u32[]{:S(2)}) copy-start(bf16[784,256]{1,0:T(8,128)(2,1)} %copy-done.6) | copy-start | bytes 1204228
  40.3 2.1 %copy-start.10 = (bf16[1,128,1152]{2,1,0:T(8,128)(2,1)S(1)}, bf16[1,128,1152]{2,1,0:T(8,128)(2,1)}, u32[]{:S(2)}) copy-start(bf16[1,128,1152]{2,1,0:T(8,128)(2,1)} %param.13) | copy-start | bytes 884740
  58.7 24.5 %all-to-all-start.1 = ((bf16[64,18,2,128]{3,2,1,0:T(2,128)(2,1)}), bf16[64,18,2,128]{3,2,1,0:T(2,128)(2,1)S(1)}, u32[]{:S(2)}, u32[]{:S(2)}) async-start(bf16[64,18,2,128]{3,2,1,0:T(2,128)(2,1)} %bitcast.15), calls=%async_computation.1 | async-start | bytes 1179648 | tf_op jit(solution)/shard_map/all_to_all | solution.py:264
  64.1 10.5 %collective-permute-start.2 = (bf16[8,128,256]{2,1,0:T(8,128)(2,1)S(1)}, bf16[8,128,256]{2,1,0:T(8,128)(2,1)S(1)}, u32[]{:S(2)}, u32[]{:S(2)}) collective-permute-start(bf16[8,128,256]{2,1,0:T(8,128)(2,1)S(1)} %forward.1), channel_id=1, source_target_pairs={{0,64},{64,128},{128,192},{192,256},{256,320},{320,384},{384,448},... | collective-permute-start | bytes 1572872 | tf_op jit(solution)/shard_map/ppermute | solution.py:327
  66.0 10.3 %collective-permute-start.3 = (bf16[8,128,256]{2,1,0:T(8,128)(2,1)S(1)}, bf16[8,128,256]{2,1,0:T(8,128)(2,1)S(1)}, u32[]{:S(2)}, u32[]{:S(2)}) collective-permute-start(bf16[8,128,256]{2,1,0:T(8,128)(2,1)S(1)} %grad_x.1), channel_id=1, source_target_pairs={{64,0},{128,64},{192,128},{256,192},{320,256},{384,320},{448,384},... | collective-permute-start | bytes 1572872 | tf_op jit(solution)/shard_map/ppermute | solution.py:335

commit v5 on v4

--- a/solution.py
+++ b/solution.py
@@ -137,32 +137,46 @@
 
 def outer_kernel(
     table_ref, first_ref, near_ref, below_ref, fric_ref, flip_ref, sum_ref,
-    gh_out_ref, gw_ref,
-    wide_ref,
+    gh_out_ref, gw_hbm,
+    wide_ref, gw_ref, sems,
 ):
     for i in range(2):
         for k in range(2):
             put_shifted(wide_ref.at[i], k, near_ref[i, 2 + k])
             put_shifted(wide_ref.at[i], 2 + k, below_ref[(2 * i + k) * CH : (2 * i + k + 1) * CH])
     last = friction_row(friction_terms(table_ref[...]), below_ref[6 * CH :].astype(F32)[1:2])
-    first_part = second_part = None
+    rows = []
     for k, fric in enumerate((fric_ref[...], last)):
         stored_rows, grad_rows = three_rows(wide_ref.at[0], k), three_rows(wide_ref.at[1], k)
         active, gh = backward_row(first_ref[...], flip_ref[...], fric, stored_rows, grad_rows)
         gh_out_ref[k] = gh
-        one, two = dot_cells(gh, stored_rows), dot_cells(grad_rows, active)
-        first_part = one if first_part is None else first_part + one
-        second_part = two if second_part is None else second_part + two
+        rows.append((stored_rows, grad_rows, active, gh))
+    half = TAPS * CH
+
+    def send(n):
+        part = pl.ds(n * half, half)
+        copy = pltpu.make_async_copy(gw_ref.at[part], gw_hbm.at[part], sems.at[n])
+        copy.start()
+        return copy
+
+    part = sum(dot_cells(gh, stored_rows) for stored_rows, _, _, gh in rows)
     for a in range(3):
         for b in range(3):
             at = (a * 3 + b) * CH
             whole = sum_ref[0, a * CH : (a + 1) * CH, b * CH : (b + 1) * CH]
-            whole = whole + first_part[:, (2 - a) * WIDE + b * CH : (2 - a) * WIDE + (b + 1) * CH]
+            whole = whole + part[:, (2 - a) * WIDE + b * CH : (2 - a) * WIDE + (b + 1) * CH]
             gw_ref[at : at + CH] = whole.astype(BF16)
+    sent_first = send(0)
+    part = sum(dot_cells(grad_rows, active) for _, grad_rows, active, _ in rows)
+    for a in range(3):
+        for b in range(3):
             at = (TAPS + a * 3 + b) * CH
             whole = sum_ref[1, a * CH : (a + 1) * CH, b * CH : (b + 1) * CH]
-            whole = whole + second_part[(2 - b) * WIDE + a * CH : (2 - b) * WIDE + (a + 1) * CH]
+            whole = whole + part[(2 - b) * WIDE + a * CH : (2 - b) * WIDE + (a + 1) * CH]
             gw_ref[at : at + CH] = whole.astype(BF16)
+    sent_second = send(1)
+    sent_first.wait()
+    sent_second.wait()
 
 
 def forward_kernel(
@@ -264,15 +278,17 @@
     return lax.all_to_all(values.reshape(count, -1, 2, CH), "rows", 0, 0).reshape(values.shape)
 
 
-def kernel_call(kernel, outs, scratch, name, flops, hbm, vmem, limit=24, smem=()):
-    outs = [jax.ShapeDtypeStruct(dims, kind) for dims, kind in outs]
+def kernel_call(kernel, outs, scratch, name, flops, hbm, vmem, limit=24, smem=(), out_sems=0):
+    out_places = [pltpu.HBM if isinstance(kind, list) else pltpu.VMEM for _, kind in outs]
+    outs = [jax.ShapeDtypeStruct(dims, kind[0] if isinstance(kind, list) else kind) for dims, kind in outs]
     scratch = [(x.shape, x.dtype) for x in hbm] + scratch
-    sems = [pltpu.SemaphoreType.DMA((len(hbm),))] if hbm else []
+    sems = [pltpu.SemaphoreType.DMA((count,)) for count in (out_sems, len(hbm)) if count]
     size = sum(x.size * x.dtype.itemsize for x in [*hbm, *vmem, *outs])
     spaces = [pltpu.SMEM] * len(smem) + [pltpu.HBM] * len(hbm) + [pltpu.VMEM] * len(vmem)
     return pl.pallas_call(
         kernel,
         in_specs=[pl.BlockSpec(memory_space=space) for space in spaces],
+        out_specs=[pl.BlockSpec(memory_space=place) for place in out_places],
         out_shape=outs,
         scratch_shapes=[pltpu.VMEM(dims, kind) for dims, kind in scratch] + sems,
         cost_estimate=pl.CostEstimate(flops=flops, bytes_accessed=size, transcendentals=0),
@@ -308,10 +324,10 @@
     )
     gh_outer, partial = kernel_call(
         outer_kernel,
-        [((2, *row), BF16), ((row_count * share, CH), BF16)],
-        [((2, 4, *wide), BF16)],
+        [((2, *row), BF16), ((2 * TAPS * CH, CH), [BF16])],
+        [((2, 4, *wide), BF16), ((2 * TAPS * CH, CH), BF16)],
         "outer", 8 * row_flops,
-        [], [table, first, near, below, fric, flip, sums],
+        [], [table, first, near, below, fric, flip, sums], out_sems=2,
     )
     partial, above = lax.optimization_barrier((partial, above))
     shares = spread_out(partial)

time: 84.9 us -> 84.9 us (level)
  no operation moved by 1% of the time
where the time goes in v5:
time: 84.9 us; the launch traced here: 84.3 us
  starting transfers between devices  36.4 us (43%)
  waiting for transfers between devices  26.7 us (31%)
  Pallas kernels  17.3 us (20%)
  local copies, waits for them, and re-layouts  2.99 us (4%)
  between operations  0.89 us (1%)
    all_to_all x2, starting transfers between devices, spread_out(): lax.all_to_all(values.reshape(count, -1, 2, CH), 'rows', 0, 0)  24.6 us
    all_to_all x2, waiting for transfers between devices, spread_out(): lax.all_to_all(values.reshape(count, -1, 2, CH), 'rows', 0, 0)  17.9 us
    pallas_call x8, Pallas kernels, kernel_call(): pl.pallas_call(kernel, in_specs=[pl.BlockSpec(memory_space=space) for spa...  17.3 us
    ppermute x1, starting transfers between devices, body(): lax.ppermute(tail, 'rows', down)  4.93 us
    ppermute x1, waiting for transfers between devices, body(): lax.ppermute(result, 'pipe', [(i, i + 1) for i in range(sections - 1)])  4.92 us
    ppermute x1, starting transfers between devices, body(): lax.ppermute(grad_x, 'pipe', [(i + 1, i) for i in range(sections - 1)])  3.64 us
    unnamed x26, local copies, waits for them, and re-layouts  2.99 us
    ppermute x1, waiting for transfers between devices, body(): lax.ppermute(head, 'rows', up)  2.12 us
  transfers between devices with their start and end apart: 6, of which 5 were waited for; matrix products, arithmetic and copies ran while one was open for 0% of the time, Pallas kernels for 15%

profile of v5, /device:TPU:6, one launch (start us, length us, event | category | flops | bytes accessed | tf_op | source)
XLA Modules:
  0.0 84.3 jit_solution(6296674092557525850)
XLA Ops:
  0.6 0.0 copy-start.4
  0.6 0.0 copy-start.1
  0.7 0.0 copy-start
  0.7 0.0 copy-start.3
  0.7 0.0 copy-start.5
  0.7 2.5 %edges.1 = (bf16[784,256]{1,0:T(8,128)(2,1)}, bf16[784,256]{1,0:T(8,128)(2,1)}) custom-call(bf16[128,8,256]{2,1,0:T(8,128)(2,1)} %bitcast.21, bf16[128,8,256]{2,1,0:T(8,128)(2,1)} %bitcast.23, bf16[128,8,256]{2,1,0:T(8,128)(2,1)} %bitcast.26, s32[2,8,256]{2,1,0:T(8,128)} %bitcast.32), custom_call_target="tpu_custom_call" | custom-call | bytes 2392064 | tf_op jit(solution)/shard_map/edges/pallas_call | solution.py:288
  3.2 1.3 %collective-permute-start = (bf16[784,256]{1,0:T(8,128)(2,1)}, bf16[784,256]{1,0:T(8,128)(2,1)S(1)}, u32[]{:S(2)}, u32[]{:S(2)}) collective-permute-start(bf16[784,256]{1,0:T(8,128)(2,1)} %get-tuple-element.23), channel_id=1, source_target_pairs={{1,0},{2,1},{3,2},{4,3},{5,4},{6,5},{7,6},{8,7},{9,8},{10,9},{11,1... | collective-permute-start | bytes 1204232 | tf_op jit(solution)/shard_map/ppermute | solution.py:316
  4.5 4.9 %collective-permute-start.1 = (bf16[784,256]{1,0:T(8,128)(2,1)}, bf16[784,256]{1,0:T(8,128)(2,1)S(1)}, u32[]{:S(2)}, u32[]{:S(2)}) collective-permute-start(bf16[784,256]{1,0:T(8,128)(2,1)} %get-tuple-element.30), channel_id=1, source_target_pairs={{0,1},{1,2},{2,3},{3,4},{4,5},{5,6},{6,7},{7,8},{8,9},{9,10},{10,1... | collective-permute-start | bytes 1204232 | tf_op jit(solution)/shard_map/ppermute | solution.py:316
  9.4 0.0 copy-done.4
  9.4 0.0 copy-done.1
  9.4 0.0 copy-done
  9.4 0.0 copy-done.3
  9.5 0.0 copy-done.5
  9.5 0.0 copy-start.9
  9.5 1.0 %copy-done.9 = bf16[1,128,1152]{2,1,0:T(8,128)(2,1)S(1)} copy-done((bf16[1,128,1152]{2,1,0:T(8,128)(2,1)S(1)}, bf16[1,128,1152]{2,1,0:T(8,128)(2,1)}, u32[]{:S(2)}) %copy-start.9) | copy-done | bytes 294936
  10.4 4.4 %inner.1 = (bf16[6,128,256]{2,1,0:T(8,128)(2,1)S(1)}, bf16[2,4,128,256]{3,2,1,0:T(8,128)(2,1)S(1)}, f32[2,384,384]{2,1,0:T(8,128)S(1)}, f32[128,256]{1,0:T(8,128)S(1)}, bf16[128,1152]{1,0:T(8,128)(2,1)S(1)}) custom-call(f32[1]{0:T(128)} %bitcast.4.top_ref, bf16[128,8,256]{2,1,0:T(8,128)(2,1)S(1)} %bitcast.22, bf16[128,8,256]{2,1,0:T(8,128)(2,1)S(1)} %bitcast.24, ...), custom_call_target="tpu_custom_call" | custom-call | flops 2264924160 | bytes 4182016 | tf_op jit(solution)/shard_map/inner/pallas_call | solution.py:288
  14.8 0.0 copy-start.11
  14.8 2.1 %collective-permute-done.below_ref = bf16[784,256]{1,0:T(8,128)(2,1)S(1)} collective-permute-done((bf16[784,256]{1,0:T(8,128)(2,1)}, bf16[784,256]{1,0:T(8,128)(2,1)S(1)}, u32[]{:S(2)}, u32[]{:S(2)}) %collective-permute-start) | collective-permute-done | bytes 401440 | tf_op jit(solution)/shard_map/ppermute | solution.py:316
  16.9 2.1 %outer.1 = (bf16[2,128,256]{2,1,0:T(8,128)(2,1)S(1)}, bf16[2304,128]{1,0:T(8,128)(2,1)}) custom-call(f32[8,128]{1,0:T(8,128)S(1)} %bitcast.37, bf16[128,1152]{1,0:T(8,128)(2,1)S(1)} %bitcast.29, bf16[2,4,128,256]{3,2,1,0:T(8,128)(2,1)S(1)} %get-tuple-element.22.near_ref, bf16[784,256]{1,0:T(8,128)(2,1)S(1)} %collective-permute-done.below_ref, ...), custom_call_target="tpu_custom_call" | custom-call | flops 603979776 | bytes 3551232 | tf_op jit(solution)/shard_map/outer/pallas_call | solution.py:288
  19.1 0.0 copy-done.11
  19.1 0.0 collective-permute-done.1.above_ref
  19.1 0.0 copy-start.6
  19.1 19.2 %all-to-all-start = ((bf16[64,18,2,128]{3,2,1,0:T(2,128)(2,1)}), bf16[64,18,2,128]{3,2,1,0:T(2,128)(2,1)S(1)}, u32[]{:S(2)}, u32[]{:S(2)}) async-start(bf16[64,18,2,128]{3,2,1,0:T(2,128)(2,1)} %bitcast.12), calls=%async_computation | async-start | bytes 1179648 | tf_op jit(solution)/shard_map/all_to_all | solution.py:278
  38.3 0.0 copy-done.6
  38.3 0.0 copy-start.7
  38.3 1.0 %copy-done.7 = bf16[784,256]{1,0:T(8,128)(2,1)S(1)} copy-done((bf16[784,256]{1,0:T(8,128)(2,1)S(1)}, bf16[784,256]{1,0:T(8,128)(2,1)}, u32[]{:S(2)}) %copy-start.7) | copy-done | bytes 401432
  39.3 0.0 copy-start.12
  39.3 1.0 %copy-done.12 = bf16[6,128,256]{2,1,0:T(8,128)(2,1)S(1)} copy-done((bf16[6,128,256]{2,1,0:T(8,128)(2,1)S(1)}, bf16[6,128,256]{2,1,0:T(8,128)(2,1)}, u32[]{:S(2)}) %copy-start.12) | copy-done | bytes 393240
  40.3 0.0 copy-start.2
  40.3 0.0 copy-start.8
  40.3 0.0 copy-start.10
  40.3 2.0 %grad_x.1 = bf16[8,128,256]{2,1,0:T(8,128)(2,1)S(1)} custom-call(s32[2,8,256]{2,1,0:T(8,128)S(1)} %bitcast.34, bf16[128,8,256]{2,1,0:T(8,128)(2,1)S(1)} %bitcast.25, bf16[128,1152]{1,0:T(8,128)(2,1)S(1)} %bitcast.30, f32[8,128]{1,0:T(8,128)S(1)} %bitcast.38, bf16[6,128,256]{2,1,0:T(8,128)(2,1)S(1)} %copy-done.12, ...), custom_call_target="tpu_custom_call" | custom-call | flops 905969664 | bytes 3108864 | tf_op jit(solution)/shard_map/grad_x/pallas_call | solution.py:288
  42.4 0.0 copy-done.2
  42.4 0.0 copy-done.8
  42.4 0.0 copy-done.10
  42.4 3.2 %forward.1 = bf16[8,128,256]{2,1,0:T(8,128)(2,1)S(1)} custom-call(bf16[128,8,256]{2,1,0:T(8,128)(2,1)S(1)} %bitcast.27, s32[2,8,256]{2,1,0:T(8,128)S(1)} %bitcast.35, f32[8,128]{1,0:T(8,128)S(1)} %bitcast.39, bf16[128,1152]{1,0:T(8,128)(2,1)S(1)} %bitcast.31, bf16[128,1152]{1,0:T(8,128)(2,1)S(1)} %bitcast.41, bf16[784,256]{1,0:T(8,128)(2,1)S(1)} %copy-done.8, ...), custom_call_target="tpu_custom_call" | custom-call | flops 1358954496 | bytes 2461696 | tf_op jit(solution)/shard_map/forward/pallas_call | solution.py:288
  45.6 12.2 %all-to-all-done = bf16[64,18,2,128]{3,2,1,0:T(2,128)(2,1)S(1)} async-done(((bf16[64,18,2,128]{3,2,1,0:T(2,128)(2,1)}), bf16[64,18,2,128]{3,2,1,0:T(2,128)(2,1)S(1)}, u32[]{:S(2)}, u32[]{:S(2)}) %all-to-all-start) | async-done | bytes 589856 | tf_op jit(solution)/shard_map/all_to_all | solution.py:278
  57.7 0.9 %sum_shares.1 = bf16[32,72,128]{2,1,0:T(8,128)(2,1)} custom-call(bf16[32,72,128]{2,1,0:T(8,128)(2,1)S(1)} %bitcast.20), custom_call_target="tpu_custom_call" | custom-call | bytes 1179648 | tf_op jit(solution)/shard_map/sum_shares/pallas_call | solution.py:288
  58.7 5.4 %all-to-all-start.1 = ((bf16[64,18,2,128]{3,2,1,0:T(2,128)(2,1)}), bf16[64,18,2,128]{3,2,1,0:T(2,128)(2,1)S(1)}, u32[]{:S(2)}, u32[]{:S(2)}) async-start(bf16[64,18,2,128]{3,2,1,0:T(2,128)(2,1)} %bitcast.15), calls=%async_computation.1 | async-start | bytes 1179648 | tf_op jit(solution)/shard_map/all_to_all | solution.py:278
  64.1 1.9 %collective-permute-start.2 = (bf16[8,128,256]{2,1,0:T(8,128)(2,1)S(1)}, bf16[8,128,256]{2,1,0:T(8,128)(2,1)S(1)}, u32[]{:S(2)}, u32[]{:S(2)}) collective-permute-start(bf16[8,128,256]{2,1,0:T(8,128)(2,1)S(1)} %forward.1), channel_id=1, source_target_pairs={{0,64},{64,128},{128,192},{192,256},{256,320},{320,384},{384,448},... | collective-permute-start | bytes 1572872 | tf_op jit(solution)/shard_map/ppermute | solution.py:343
  66.0 3.6 %collective-permute-start.3 = (bf16[8,128,256]{2,1,0:T(8,128)(2,1)S(1)}, bf16[8,128,256]{2,1,0:T(8,128)(2,1)S(1)}, u32[]{:S(2)}, u32[]{:S(2)}) collective-permute-start(bf16[8,128,256]{2,1,0:T(8,128)(2,1)S(1)} %grad_x.1), channel_id=1, source_target_pairs={{64,0},{128,64},{192,128},{256,192},{320,256},{384,320},{448,384},... | collective-permute-start | bytes 1572872 | tf_op jit(solution)/shard_map/ppermute | solution.py:351
  69.7 4.9 %collective-permute-done.2.act_ref = bf16[8,128,256]{2,1,0:T(8,128)(2,1)S(1)} collective-permute-done((bf16[8,128,256]{2,1,0:T(8,128)(2,1)S(1)}, bf16[8,128,256]{2,1,0:T(8,128)(2,1)S(1)}, u32[]{:S(2)}, u32[]{:S(2)}) %collective-permute-start.2) | collective-permute-done | bytes 524320 | tf_op jit(solution)/shard_map/ppermute | solution.py:343
  74.6 1.8 %collective-permute-done.3.grad_ref = bf16[8,128,256]{2,1,0:T(8,128)(2,1)S(1)} collective-permute-done((bf16[8,128,256]{2,1,0:T(8,128)(2,1)S(1)}, bf16[8,128,256]{2,1,0:T(8,128)(2,1)S(1)}, u32[]{:S(2)}, u32[]{:S(2)}) %collective-permute-start.3) | collective-permute-done | bytes 524320 | tf_op jit(solution)/shard_map/ppermute | solution.py:351
  76.4 1.1 %turn.1 = (bf16[128,8,256]{2,1,0:T(8,128)(2,1)}, bf16[128,8,256]{2,1,0:T(8,128)(2,1)}) custom-call(bf16[8,128,256]{2,1,0:T(8,128)(2,1)S(1)} %collective-permute-done.2.act_ref, bf16[8,128,256]{2,1,0:T(8,128)(2,1)S(1)} %collective-permute-done.3.grad_ref), custom_call_target="tpu_custom_call" | custom-call | bytes 2097152 | tf_op jit(solution)/shard_map/turn/pallas_call | solution.py:288
  77.5 5.7 %all-to-all-done.1 = bf16[64,18,2,128]{3,2,1,0:T(2,128)(2,1)S(1)} async-done(((bf16[64,18,2,128]{3,2,1,0:T(2,128)(2,1)}), bf16[64,18,2,128]{3,2,1,0:T(2,128)(2,1)S(1)}, u32[]{:S(2)}, u32[]{:S(2)}) %all-to-all-start.1) | async-done | bytes 589856 | tf_op jit(solution)/shard_map/all_to_all | solution.py:278
  83.2 1.1 %spread.1 = (f32[128,1152]{1,0:T(8,128)}, f32[128,1152]{1,0:T(8,128)}) custom-call(bf16[2304,128]{1,0:T(8,128)(2,1)S(1)} %bitcast.19), custom_call_target="tpu_custom_call" | custom-call | bytes 1769472 | tf_op jit(solution)/shard_map/spread/pallas_call | solution.py:288
Async XLA Ops:
  0.6 8.8 %copy-start.4 = (s32[1,2,8,256]{3,2,1,0:T(8,128)S(1)}, s32[1,2,8,256]{3,2,1,0:T(8,128)}, u32[]{:S(2)}) copy-start(s32[1,2,8,256]{3,2,1,0:T(8,128)} %param.10) | copy-start | bytes 49156
  0.6 8.8 %copy-start.1 = (bf16[1,128,8,256]{3,2,1,0:T(8,128)(2,1)S(1)}, bf16[1,128,8,256]{3,2,1,0:T(8,128)(2,1)}, u32[]{:S(2)}) copy-start(bf16[1,128,8,256]{3,2,1,0:T(8,128)(2,1)} %param.9) | copy-start | bytes 1572868
  0.7 8.8 %copy-start = (bf16[1,128,8,256]{3,2,1,0:T(8,128)(2,1)S(1)}, bf16[1,128,8,256]{3,2,1,0:T(8,128)(2,1)}, u32[]{:S(2)}) copy-start(bf16[1,128,8,256]{3,2,1,0:T(8,128)(2,1)} %param.8) | copy-start | bytes 1572868
  0.7 8.8 %copy-start.3 = (bf16[1,128,1152]{2,1,0:T(8,128)(2,1)S(1)}, bf16[1,128,1152]{2,1,0:T(8,128)(2,1)}, u32[]{:S(2)}) copy-start(bf16[1,128,1152]{2,1,0:T(8,128)(2,1)} %param.12) | copy-start | bytes 884740
  0.7 8.8 %copy-start.5 = (f32[1,128,8]{1,2,0:T(8,128)S(1)}, f32[1,128,8]{1,2,0:T(8,128)}, u32[]{:S(2)}) copy-start(f32[1,128,8]{1,2,0:T(8,128)} %param.11) | copy-start | bytes 12292
  3.2 13.8 %collective-permute-start = (bf16[784,256]{1,0:T(8,128)(2,1)}, bf16[784,256]{1,0:T(8,128)(2,1)S(1)}, u32[]{:S(2)}, u32[]{:S(2)}) collective-permute-start(bf16[784,256]{1,0:T(8,128)(2,1)} %get-tuple-element.23), channel_id=1, source_target_pairs={{1,0},{2,1},{3,2},{4,3},{5,4},{6,5},{7,6},{8,7},{9,8},{10,9},{11,1... | collective-permute-start | bytes 1204232 | tf_op jit(solution)/shard_map/ppermute | solution.py:316
  4.5 14.6 %collective-permute-start.1 = (bf16[784,256]{1,0:T(8,128)(2,1)}, bf16[784,256]{1,0:T(8,128)(2,1)S(1)}, u32[]{:S(2)}, u32[]{:S(2)}) collective-permute-start(bf16[784,256]{1,0:T(8,128)(2,1)} %get-tuple-element.30), channel_id=1, source_target_pairs={{0,1},{1,2},{2,3},{3,4},{4,5},{5,6},{6,7},{7,8},{8,9},{9,10},{10,1... | collective-permute-start | bytes 1204232 | tf_op jit(solution)/shard_map/ppermute | solution.py:316
  9.5 1.0 %copy-start.9 = (bf16[1,128,1152]{2,1,0:T(8,128)(2,1)S(1)}, bf16[1,128,1152]{2,1,0:T(8,128)(2,1)}, u32[]{:S(2)}) copy-start(bf16[1,128,1152]{2,1,0:T(8,128)(2,1)} %param.13) | copy-start | bytes 884740
  14.8 4.3 %copy-start.11 = (bf16[6,128,256]{2,1,0:T(8,128)(2,1)}, bf16[6,128,256]{2,1,0:T(8,128)(2,1)S(1)}, u32[]{:S(2)}) copy-start(bf16[6,128,256]{2,1,0:T(8,128)(2,1)S(1)} %get-tuple-element.32.inner_ref) | copy-start | bytes 1179652
  19.1 19.2 %copy-start.6 = (bf16[784,256]{1,0:T(8,128)(2,1)}, bf16[784,256]{1,0:T(8,128)(2,1)S(1)}, u32[]{:S(2)}) copy-start(bf16[784,256]{1,0:T(8,128)(2,1)S(1)} %collective-permute-done.1.above_ref) | copy-start | bytes 1204228
  19.1 38.6 %all-to-all-start = ((bf16[64,18,2,128]{3,2,1,0:T(2,128)(2,1)}), bf16[64,18,2,128]{3,2,1,0:T(2,128)(2,1)S(1)}, u32[]{:S(2)}, u32[]{:S(2)}) async-start(bf16[64,18,2,128]{3,2,1,0:T(2,128)(2,1)} %bitcast.12), calls=%async_computation | async-start | bytes 1179648 | tf_op jit(solution)/shard_map/all_to_all | solution.py:278
  38.3 1.0 %copy-start.7 = (bf16[784,256]{1,0:T(8,128)(2,1)S(1)}, bf16[784,256]{1,0:T(8,128)(2,1)}, u32[]{:S(2)}) copy-start(bf16[784,256]{1,0:T(8,128)(2,1)} %copy-done.6) | copy-start | bytes 1204228
  39.3 1.0 %copy-start.12 = (bf16[6,128,256]{2,1,0:T(8,128)(2,1)S(1)}, bf16[6,128,256]{2,1,0:T(8,128)(2,1)}, u32[]{:S(2)}) copy-start(bf16[6,128,256]{2,1,0:T(8,128)(2,1)} %copy-done.11) | copy-start | bytes 1179652
  40.3 2.1 %copy-start.2 = (bf16[1,128,8,256]{3,2,1,0:T(8,128)(2,1)S(1)}, bf16[1,128,8,256]{3,2,1,0:T(8,128)(2,1)}, u32[]{:S(2)}) copy-start(bf16[1,128,8,256]{3,2,1,0:T(8,128)(2,1)} %param.7) | copy-start | bytes 1572868
  40.3 2.1 %copy-start.8 = (bf16[784,256]{1,0:T(8,128)(2,1)S(1)}, bf16[784,256]{1,0:T(8,128)(2,1)}, u32[]{:S(2)}) copy-start(bf16[784,256]{1,0:T(8,128)(2,1)} %copy-done.6) | copy-start | bytes 1204228
  40.3 2.1 %copy-start.10 = (bf16[1,128,1152]{2,1,0:T(8,128)(2,1)S(1)}, bf16[1,128,1152]{2,1,0:T(8,128)(2,1)}, u32[]{:S(2)}) copy-start(bf16[1,128,1152]{2,1,0:T(8,128)(2,1)} %param.13) | copy-start | bytes 884740
  58.7 24.5 %all-to-all-start.1 = ((bf16[64,18,2,128]{3,2,1,0:T(2,128)(2,1)}), bf16[64,18,2,128]{3,2,1,0:T(2,128)(2,1)S(1)}, u32[]{:S(2)}, u32[]{:S(2)}) async-start(bf16[64,18,2,128]{3,2,1,0:T(2,128)(2,1)} %bitcast.15), calls=%async_computation.1 | async-start | bytes 1179648 | tf_op jit(solution)/shard_map/all_to_all | solution.py:278
  64.1 10.5 %collective-permute-start.2 = (bf16[8,128,256]{2,1,0:T(8,128)(2,1)S(1)}, bf16[8,128,256]{2,1,0:T(8,128)(2,1)S(1)}, u32[]{:S(2)}, u32[]{:S(2)}) collective-permute-start(bf16[8,128,256]{2,1,0:T(8,128)(2,1)S(1)} %forward.1), channel_id=1, source_target_pairs={{0,64},{64,128},{128,192},{192,256},{256,320},{320,384},{384,448},... | collective-permute-start | bytes 1572872 | tf_op jit(solution)/shard_map/ppermute | solution.py:343
  66.0 10.3 %collective-permute-start.3 = (bf16[8,128,256]{2,1,0:T(8,128)(2,1)S(1)}, bf16[8,128,256]{2,1,0:T(8,128)(2,1)S(1)}, u32[]{:S(2)}, u32[]{:S(2)}) collective-permute-start(bf16[8,128,256]{2,1,0:T(8,128)(2,1)S(1)} %grad_x.1), channel_id=1, source_target_pairs={{64,0},{128,64},{192,128},{256,192},{320,256},{384,320},{448,384},... | collective-permute-start | bytes 1572872 | tf_op jit(solution)/shard_map/ppermute | solution.py:351

commit v6 on v4

--- a/solution.py
+++ b/solution.py
@@ -259,9 +259,19 @@
             second_ref[:, to : to + CH] = flat_ref[at : at + CH].astype(F32)
 
 
+def section_rows(sections, row_count):
+    groups = []
+    for section in range(sections):
+        line = [(k * 27 if section % 2 else k * 37) % row_count for k in range(row_count)]
+        groups.append([section * row_count + k for k in line])
+    return groups
+
+
 def spread_out(values):
     count = lax.axis_size("rows")
-    return lax.all_to_all(values.reshape(count, -1, 2, CH), "rows", 0, 0).reshape(values.shape)
+    groups = section_rows(lax.axis_size("pipe"), count)
+    parts = lax.all_to_all(values.reshape(count, -1, 2, CH), ("pipe", "rows"), 0, 0, axis_index_groups=groups)
+    return parts.reshape(values.shape)
 
 
 def kernel_call(kernel, outs, scratch, name, flops, hbm, vmem, limit=24, smem=()):

time: 84.9 us -> 87.6 us (1.032)
  waiting for transfers between devices: 26.7 us -> 30.2 us
    all_to_all x2, waiting for transfers between devices: 17.9 us -> 21.5 us  [spread_out(): lax.all_to_all(values.reshape(count, -1, 2, CH), ('pipe', 'rows'), 0, 0,...]
where the time goes in v6:
time: 87.6 us; the launch traced here: 87.1 us
  starting transfers between devices  35.5 us (41%)
  waiting for transfers between devices  30.2 us (34%)
  Pallas kernels  17.4 us (20%)
  local copies, waits for them, and re-layouts  2.99 us (3%)
    all_to_all x2, starting transfers between devices, spread_out(): lax.all_to_all(values.reshape(count, -1, 2, CH), ('pipe', 'rows'), 0, 0,...  23.8 us
    all_to_all x2, waiting for transfers between devices, spread_out(): lax.all_to_all(values.reshape(count, -1, 2, CH), ('pipe', 'rows'), 0, 0,...  21.5 us
    pallas_call x8, Pallas kernels, kernel_call(): pl.pallas_call(kernel, in_specs=[pl.BlockSpec(memory_space=space) for spa...  17.4 us
    ppermute x1, starting transfers between devices, body(): lax.ppermute(tail, 'rows', down)  4.93 us
    ppermute x1, waiting for transfers between devices, body(): lax.ppermute(result, 'pipe', [(i, i + 1) for i in range(sections - 1)])  4.92 us
    ppermute x1, starting transfers between devices, body(): lax.ppermute(grad_x, 'pipe', [(i + 1, i) for i in range(sections - 1)])  3.64 us
    unnamed x26, local copies, waits for them, and re-layouts  2.99 us
    ppermute x1, waiting for transfers between devices, body(): lax.ppermute(head, 'rows', up)  2.12 us
  transfers between devices with their start and end apart: 6, of which 5 were waited for; matrix products, arithmetic and copies ran while one was open for 0% of the time, Pallas kernels for 15%

profile of v6, /device:TPU:6, one launch (start us, length us, event | category | flops | bytes accessed | tf_op | source)
XLA Modules:
  0.0 87.1 jit_solution(11883117182340703344)
XLA Ops:
  0.6 0.0 copy-start.4
  0.6 0.0 copy-start.1
  0.7 0.0 copy-start
  0.7 0.0 copy-start.3
  0.7 0.0 copy-start.5
  0.7 2.5 %edges.1 = (bf16[784,256]{1,0:T(8,128)(2,1)}, bf16[784,256]{1,0:T(8,128)(2,1)}) custom-call(bf16[128,8,256]{2,1,0:T(8,128)(2,1)} %bitcast.21, bf16[128,8,256]{2,1,0:T(8,128)(2,1)} %bitcast.23, bf16[128,8,256]{2,1,0:T(8,128)(2,1)} %bitcast.26, s32[2,8,256]{2,1,0:T(8,128)} %bitcast.32), custom_call_target="tpu_custom_call" | custom-call | bytes 2392064 | tf_op jit(solution)/shard_map/edges/pallas_call | solution.py:283
  3.2 1.3 %collective-permute-start = (bf16[784,256]{1,0:T(8,128)(2,1)}, bf16[784,256]{1,0:T(8,128)(2,1)S(1)}, u32[]{:S(2)}, u32[]{:S(2)}) collective-permute-start(bf16[784,256]{1,0:T(8,128)(2,1)} %get-tuple-element.23), channel_id=1, source_target_pairs={{1,0},{2,1},{3,2},{4,3},{5,4},{6,5},{7,6},{8,7},{9,8},{10,9},{11,1... | collective-permute-start | bytes 1204232 | tf_op jit(solution)/shard_map/ppermute | solution.py:310
  4.5 4.9 %collective-permute-start.1 = (bf16[784,256]{1,0:T(8,128)(2,1)}, bf16[784,256]{1,0:T(8,128)(2,1)S(1)}, u32[]{:S(2)}, u32[]{:S(2)}) collective-permute-start(bf16[784,256]{1,0:T(8,128)(2,1)} %get-tuple-element.30), channel_id=1, source_target_pairs={{0,1},{1,2},{2,3},{3,4},{4,5},{5,6},{6,7},{7,8},{8,9},{9,10},{10,1... | collective-permute-start | bytes 1204232 | tf_op jit(solution)/shard_map/ppermute | solution.py:310
  9.4 0.0 copy-done.4
  9.4 0.0 copy-done.1
  9.4 0.0 copy-done
  9.4 0.0 copy-done.3
  9.5 0.0 copy-done.5
  9.5 0.0 copy-start.9
  9.5 1.0 %copy-done.9 = bf16[1,128,1152]{2,1,0:T(8,128)(2,1)S(1)} copy-done((bf16[1,128,1152]{2,1,0:T(8,128)(2,1)S(1)}, bf16[1,128,1152]{2,1,0:T(8,128)(2,1)}, u32[]{:S(2)}) %copy-start.9) | copy-done | bytes 294936
  10.4 4.4 %inner.1 = (bf16[6,128,256]{2,1,0:T(8,128)(2,1)S(1)}, bf16[2,4,128,256]{3,2,1,0:T(8,128)(2,1)S(1)}, f32[2,384,384]{2,1,0:T(8,128)S(1)}, f32[128,256]{1,0:T(8,128)S(1)}, bf16[128,1152]{1,0:T(8,128)(2,1)S(1)}) custom-call(f32[1]{0:T(128)} %bitcast.4.top_ref, bf16[128,8,256]{2,1,0:T(8,128)(2,1)S(1)} %bitcast.22, bf16[128,8,256]{2,1,0:T(8,128)(2,1)S(1)} %bitcast.24, ...), custom_call_target="tpu_custom_call" | custom-call | flops 2264924160 | bytes 4182016 | tf_op jit(solution)/shard_map/inner/pallas_call | solution.py:283
  14.8 0.0 copy-start.11
  14.8 2.1 %collective-permute-done.below_ref = bf16[784,256]{1,0:T(8,128)(2,1)S(1)} collective-permute-done((bf16[784,256]{1,0:T(8,128)(2,1)}, bf16[784,256]{1,0:T(8,128)(2,1)S(1)}, u32[]{:S(2)}, u32[]{:S(2)}) %collective-permute-start) | collective-permute-done | bytes 401440 | tf_op jit(solution)/shard_map/ppermute | solution.py:310
  16.9 2.2 %outer.1 = (bf16[2,128,256]{2,1,0:T(8,128)(2,1)S(1)}, bf16[2304,128]{1,0:T(8,128)(2,1)}) custom-call(f32[8,128]{1,0:T(8,128)S(1)} %bitcast.37, bf16[128,1152]{1,0:T(8,128)(2,1)S(1)} %bitcast.29, bf16[2,4,128,256]{3,2,1,0:T(8,128)(2,1)S(1)} %get-tuple-element.22.near_ref, bf16[784,256]{1,0:T(8,128)(2,1)S(1)} %collective-permute-done.below_ref, ...), custom_call_target="tpu_custom_call" | custom-call | flops 603979776 | bytes 3551232 | tf_op jit(solution)/shard_map/outer/pallas_call | solution.py:283
  19.2 0.0 copy-done.11
  19.2 0.0 collective-permute-done.1.above_ref
  19.2 0.0 copy-start.6
  19.2 19.1 %all-to-all-start = ((bf16[64,18,2,128]{3,2,1,0:T(2,128)(2,1)}), bf16[64,18,2,128]{3,2,1,0:T(2,128)(2,1)S(1)}, u32[]{:S(2)}, u32[]{:S(2)}) async-start(bf16[64,18,2,128]{3,2,1,0:T(2,128)(2,1)} %bitcast.12), calls=%async_computation | async-start | bytes 1179648 | tf_op jit(solution)/shard_map/all_to_all | solution.py:273
  38.3 0.0 copy-done.6
  38.3 0.0 copy-start.7
  38.3 1.0 %copy-done.7 = bf16[784,256]{1,0:T(8,128)(2,1)S(1)} copy-done((bf16[784,256]{1,0:T(8,128)(2,1)S(1)}, bf16[784,256]{1,0:T(8,128)(2,1)}, u32[]{:S(2)}) %copy-start.7) | copy-done | bytes 401432
  39.3 0.0 copy-start.12
  39.3 1.0 %copy-done.12 = bf16[6,128,256]{2,1,0:T(8,128)(2,1)S(1)} copy-done((bf16[6,128,256]{2,1,0:T(8,128)(2,1)S(1)}, bf16[6,128,256]{2,1,0:T(8,128)(2,1)}, u32[]{:S(2)}) %copy-start.12) | copy-done | bytes 393240
  40.3 0.0 copy-start.2
  40.3 0.0 copy-start.8
  40.3 0.0 copy-start.10
  40.3 2.0 %grad_x.1 = bf16[8,128,256]{2,1,0:T(8,128)(2,1)S(1)} custom-call(s32[2,8,256]{2,1,0:T(8,128)S(1)} %bitcast.34, bf16[128,8,256]{2,1,0:T(8,128)(2,1)S(1)} %bitcast.25, bf16[128,1152]{1,0:T(8,128)(2,1)S(1)} %bitcast.30, f32[8,128]{1,0:T(8,128)S(1)} %bitcast.38, bf16[6,128,256]{2,1,0:T(8,128)(2,1)S(1)} %copy-done.12, ...), custom_call_target="tpu_custom_call" | custom-call | flops 905969664 | bytes 3108864 | tf_op jit(solution)/shard_map/grad_x/pallas_call | solution.py:283
  42.4 0.0 copy-done.2
  42.4 0.0 copy-done.8
  42.4 0.0 copy-done.10
  42.4 3.2 %forward.1 = bf16[8,128,256]{2,1,0:T(8,128)(2,1)S(1)} custom-call(bf16[128,8,256]{2,1,0:T(8,128)(2,1)S(1)} %bitcast.27, s32[2,8,256]{2,1,0:T(8,128)S(1)} %bitcast.35, f32[8,128]{1,0:T(8,128)S(1)} %bitcast.39, bf16[128,1152]{1,0:T(8,128)(2,1)S(1)} %bitcast.31, bf16[128,1152]{1,0:T(8,128)(2,1)S(1)} %bitcast.41, bf16[784,256]{1,0:T(8,128)(2,1)S(1)} %copy-done.8, ...), custom_call_target="tpu_custom_call" | custom-call | flops 1358954496 | bytes 2461696 | tf_op jit(solution)/shard_map/forward/pallas_call | solution.py:283
  45.6 14.5 %all-to-all-done = bf16[64,18,2,128]{3,2,1,0:T(2,128)(2,1)S(1)} async-done(((bf16[64,18,2,128]{3,2,1,0:T(2,128)(2,1)}), bf16[64,18,2,128]{3,2,1,0:T(2,128)(2,1)S(1)}, u32[]{:S(2)}, u32[]{:S(2)}) %all-to-all-start) | async-done | bytes 589856 | tf_op jit(solution)/shard_map/all_to_all | solution.py:273
  60.1 0.9 %sum_shares.1 = bf16[32,72,128]{2,1,0:T(8,128)(2,1)} custom-call(bf16[32,72,128]{2,1,0:T(8,128)(2,1)S(1)} %bitcast.20), custom_call_target="tpu_custom_call" | custom-call | bytes 1179648 | tf_op jit(solution)/shard_map/sum_shares/pallas_call | solution.py:283
  61.0 4.6 %all-to-all-start.1 = ((bf16[64,18,2,128]{3,2,1,0:T(2,128)(2,1)}), bf16[64,18,2,128]{3,2,1,0:T(2,128)(2,1)S(1)}, u32[]{:S(2)}, u32[]{:S(2)}) async-start(bf16[64,18,2,128]{3,2,1,0:T(2,128)(2,1)} %bitcast.15), calls=%async_computation.1 | async-start | bytes 1179648 | tf_op jit(solution)/shard_map/all_to_all | solution.py:273
  65.7 1.9 %collective-permute-start.2 = (bf16[8,128,256]{2,1,0:T(8,128)(2,1)S(1)}, bf16[8,128,256]{2,1,0:T(8,128)(2,1)S(1)}, u32[]{:S(2)}, u32[]{:S(2)}) collective-permute-start(bf16[8,128,256]{2,1,0:T(8,128)(2,1)S(1)} %forward.1), channel_id=1, source_target_pairs={{0,64},{64,128},{128,192},{192,256},{256,320},{320,384},{384,448},... | collective-permute-start | bytes 1572872 | tf_op jit(solution)/shard_map/ppermute | solution.py:337
  67.6 3.6 %collective-permute-start.3 = (bf16[8,128,256]{2,1,0:T(8,128)(2,1)S(1)}, bf16[8,128,256]{2,1,0:T(8,128)(2,1)S(1)}, u32[]{:S(2)}, u32[]{:S(2)}) collective-permute-start(bf16[8,128,256]{2,1,0:T(8,128)(2,1)S(1)} %grad_x.1), channel_id=1, source_target_pairs={{64,0},{128,64},{192,128},{256,192},{320,256},{384,320},{448,384},... | collective-permute-start | bytes 1572872 | tf_op jit(solution)/shard_map/ppermute | solution.py:345
  71.2 4.9 %collective-permute-done.2.act_ref = bf16[8,128,256]{2,1,0:T(8,128)(2,1)S(1)} collective-permute-done((bf16[8,128,256]{2,1,0:T(8,128)(2,1)S(1)}, bf16[8,128,256]{2,1,0:T(8,128)(2,1)S(1)}, u32[]{:S(2)}, u32[]{:S(2)}) %collective-permute-start.2) | collective-permute-done | bytes 524320 | tf_op jit(solution)/shard_map/ppermute | solution.py:337
  76.2 1.8 %collective-permute-done.3.grad_ref = bf16[8,128,256]{2,1,0:T(8,128)(2,1)S(1)} collective-permute-done((bf16[8,128,256]{2,1,0:T(8,128)(2,1)S(1)}, bf16[8,128,256]{2,1,0:T(8,128)(2,1)S(1)}, u32[]{:S(2)}, u32[]{:S(2)}) %collective-permute-start.3) | collective-permute-done | bytes 524320 | tf_op jit(solution)/shard_map/ppermute | solution.py:345
  77.9 1.1 %turn.1 = (bf16[128,8,256]{2,1,0:T(8,128)(2,1)}, bf16[128,8,256]{2,1,0:T(8,128)(2,1)}) custom-call(bf16[8,128,256]{2,1,0:T(8,128)(2,1)S(1)} %collective-permute-done.2.act_ref, bf16[8,128,256]{2,1,0:T(8,128)(2,1)S(1)} %collective-permute-done.3.grad_ref), custom_call_target="tpu_custom_call" | custom-call | bytes 2097152 | tf_op jit(solution)/shard_map/turn/pallas_call | solution.py:283
  79.0 7.0 %all-to-all-done.1 = bf16[64,18,2,128]{3,2,1,0:T(2,128)(2,1)S(1)} async-done(((bf16[64,18,2,128]{3,2,1,0:T(2,128)(2,1)}), bf16[64,18,2,128]{3,2,1,0:T(2,128)(2,1)S(1)}, u32[]{:S(2)}, u32[]{:S(2)}) %all-to-all-start.1) | async-done | bytes 589856 | tf_op jit(solution)/shard_map/all_to_all | solution.py:273
  86.0 1.1 %spread.1 = (f32[128,1152]{1,0:T(8,128)}, f32[128,1152]{1,0:T(8,128)}) custom-call(bf16[2304,128]{1,0:T(8,128)(2,1)S(1)} %bitcast.19), custom_call_target="tpu_custom_call" | custom-call | bytes 1769472 | tf_op jit(solution)/shard_map/spread/pallas_call | solution.py:283
Async XLA Ops:
  0.6 8.8 %copy-start.4 = (s32[1,2,8,256]{3,2,1,0:T(8,128)S(1)}, s32[1,2,8,256]{3,2,1,0:T(8,128)}, u32[]{:S(2)}) copy-start(s32[1,2,8,256]{3,2,1,0:T(8,128)} %param.10) | copy-start | bytes 49156
  0.6 8.8 %copy-start.1 = (bf16[1,128,8,256]{3,2,1,0:T(8,128)(2,1)S(1)}, bf16[1,128,8,256]{3,2,1,0:T(8,128)(2,1)}, u32[]{:S(2)}) copy-start(bf16[1,128,8,256]{3,2,1,0:T(8,128)(2,1)} %param.9) | copy-start | bytes 1572868
  0.7 8.8 %copy-start = (bf16[1,128,8,256]{3,2,1,0:T(8,128)(2,1)S(1)}, bf16[1,128,8,256]{3,2,1,0:T(8,128)(2,1)}, u32[]{:S(2)}) copy-start(bf16[1,128,8,256]{3,2,1,0:T(8,128)(2,1)} %param.8) | copy-start | bytes 1572868
  0.7 8.8 %copy-start.3 = (bf16[1,128,1152]{2,1,0:T(8,128)(2,1)S(1)}, bf16[1,128,1152]{2,1,0:T(8,128)(2,1)}, u32[]{:S(2)}) copy-start(bf16[1,128,1152]{2,1,0:T(8,128)(2,1)} %param.12) | copy-start | bytes 884740
  0.7 8.8 %copy-start.5 = (f32[1,128,8]{1,2,0:T(8,128)S(1)}, f32[1,128,8]{1,2,0:T(8,128)}, u32[]{:S(2)}) copy-start(f32[1,128,8]{1,2,0:T(8,128)} %param.11) | copy-start | bytes 12292
  3.2 13.8 %collective-permute-start = (bf16[784,256]{1,0:T(8,128)(2,1)}, bf16[784,256]{1,0:T(8,128)(2,1)S(1)}, u32[]{:S(2)}, u32[]{:S(2)}) collective-permute-start(bf16[784,256]{1,0:T(8,128)(2,1)} %get-tuple-element.23), channel_id=1, source_target_pairs={{1,0},{2,1},{3,2},{4,3},{5,4},{6,5},{7,6},{8,7},{9,8},{10,9},{11,1... | collective-permute-start | bytes 1204232 | tf_op jit(solution)/shard_map/ppermute | solution.py:310
  4.5 14.7 %collective-permute-start.1 = (bf16[784,256]{1,0:T(8,128)(2,1)}, bf16[784,256]{1,0:T(8,128)(2,1)S(1)}, u32[]{:S(2)}, u32[]{:S(2)}) collective-permute-start(bf16[784,256]{1,0:T(8,128)(2,1)} %get-tuple-element.30), channel_id=1, source_target_pairs={{0,1},{1,2},{2,3},{3,4},{4,5},{5,6},{6,7},{7,8},{8,9},{9,10},{10,1... | collective-permute-start | bytes 1204232 | tf_op jit(solution)/shard_map/ppermute | solution.py:310
  9.5 1.0 %copy-start.9 = (bf16[1,128,1152]{2,1,0:T(8,128)(2,1)S(1)}, bf16[1,128,1152]{2,1,0:T(8,128)(2,1)}, u32[]{:S(2)}) copy-start(bf16[1,128,1152]{2,1,0:T(8,128)(2,1)} %param.13) | copy-start | bytes 884740
  14.8 4.4 %copy-start.11 = (bf16[6,128,256]{2,1,0:T(8,128)(2,1)}, bf16[6,128,256]{2,1,0:T(8,128)(2,1)S(1)}, u32[]{:S(2)}) copy-start(bf16[6,128,256]{2,1,0:T(8,128)(2,1)S(1)} %get-tuple-element.32.inner_ref) | copy-start | bytes 1179652
  19.2 19.1 %copy-start.6 = (bf16[784,256]{1,0:T(8,128)(2,1)}, bf16[784,256]{1,0:T(8,128)(2,1)S(1)}, u32[]{:S(2)}) copy-start(bf16[784,256]{1,0:T(8,128)(2,1)S(1)} %collective-permute-done.1.above_ref) | copy-start | bytes 1204228
  19.2 40.9 %all-to-all-start = ((bf16[64,18,2,128]{3,2,1,0:T(2,128)(2,1)}), bf16[64,18,2,128]{3,2,1,0:T(2,128)(2,1)S(1)}, u32[]{:S(2)}, u32[]{:S(2)}) async-start(bf16[64,18,2,128]{3,2,1,0:T(2,128)(2,1)} %bitcast.12), calls=%async_computation | async-start | bytes 1179648 | tf_op jit(solution)/shard_map/all_to_all | solution.py:273
  38.3 1.0 %copy-start.7 = (bf16[784,256]{1,0:T(8,128)(2,1)S(1)}, bf16[784,256]{1,0:T(8,128)(2,1)}, u32[]{:S(2)}) copy-start(bf16[784,256]{1,0:T(8,128)(2,1)} %copy-done.6) | copy-start | bytes 1204228
  39.3 1.0 %copy-start.12 = (bf16[6,128,256]{2,1,0:T(8,128)(2,1)S(1)}, bf16[6,128,256]{2,1,0:T(8,128)(2,1)}, u32[]{:S(2)}) copy-start(bf16[6,128,256]{2,1,0:T(8,128)(2,1)} %copy-done.11) | copy-start | bytes 1179652
  40.3 2.1 %copy-start.2 = (bf16[1,128,8,256]{3,2,1,0:T(8,128)(2,1)S(1)}, bf16[1,128,8,256]{3,2,1,0:T(8,128)(2,1)}, u32[]{:S(2)}) copy-start(bf16[1,128,8,256]{3,2,1,0:T(8,128)(2,1)} %param.7) | copy-start | bytes 1572868
  40.3 2.1 %copy-start.8 = (bf16[784,256]{1,0:T(8,128)(2,1)S(1)}, bf16[784,256]{1,0:T(8,128)(2,1)}, u32[]{:S(2)}) copy-start(bf16[784,256]{1,0:T(8,128)(2,1)} %copy-done.6) | copy-start | bytes 1204228
  40.3 2.1 %copy-start.10 = (bf16[1,128,1152]{2,1,0:T(8,128)(2,1)S(1)}, bf16[1,128,1152]{2,1,0:T(8,128)(2,1)}, u32[]{:S(2)}) copy-start(bf16[1,128,1152]{2,1,0:T(8,128)(2,1)} %param.13) | copy-start | bytes 884740
  61.0 25.0 %all-to-all-start.1 = ((bf16[64,18,2,128]{3,2,1,0:T(2,128)(2,1)}), bf16[64,18,2,128]{3,2,1,0:T(2,128)(2,1)S(1)}, u32[]{:S(2)}, u32[]{:S(2)}) async-start(bf16[64,18,2,128]{3,2,1,0:T(2,128)(2,1)} %bitcast.15), calls=%async_computation.1 | async-start | bytes 1179648 | tf_op jit(solution)/shard_map/all_to_all | solution.py:273
  65.7 10.5 %collective-permute-start.2 = (bf16[8,128,256]{2,1,0:T(8,128)(2,1)S(1)}, bf16[8,128,256]{2,1,0:T(8,128)(2,1)S(1)}, u32[]{:S(2)}, u32[]{:S(2)}) collective-permute-start(bf16[8,128,256]{2,1,0:T(8,128)(2,1)S(1)} %forward.1), channel_id=1, source_target_pairs={{0,64},{64,128},{128,192},{192,256},{256,320},{320,384},{384,448},... | collective-permute-start | bytes 1572872 | tf_op jit(solution)/shard_map/ppermute | solution.py:337
  67.6 10.3 %collective-permute-start.3 = (bf16[8,128,256]{2,1,0:T(8,128)(2,1)S(1)}, bf16[8,128,256]{2,1,0:T(8,128)(2,1)S(1)}, u32[]{:S(2)}, u32[]{:S(2)}) collective-permute-start(bf16[8,128,256]{2,1,0:T(8,128)(2,1)S(1)} %grad_x.1), channel_id=1, source_target_pairs={{64,0},{128,64},{192,128},{256,192},{320,256},{384,320},{448,384},... | collective-permute-start | bytes 1572872 | tf_op jit(solution)/shard_map/ppermute | solution.py:345
